TPU v7x, 32 devices: a whole 2x2x4 slice. The times are simulated.
32 devices in a mesh: dp: 16 (over z, y, x), tensor: 2 (over core).
Axes of the slice: x: 2, y: 2, z: 4, core: 2. Of those that a mesh axis runs over, the one named last changes fastest.
Arguments:
- tokens: bfloat16 [12288, 2048], P('dp'), may hold values from -6 to 6
- segment_ids: int32 [12288], P('dp'), may hold values from 0 to 12287, as said below
- cotangent: bfloat16 [12288, 2048], P('dp'), may hold values from -6 to 6
- mixer_gain: bfloat16 [2048], replicated, may hold values from 0.5 to 1.5
- w_query: bfloat16 [2048, 1024], P('dp', 'tensor'), as said below
- w_key: bfloat16 [2048, 1024], P('dp', 'tensor'), as said below
- w_value: bfloat16 [2048, 2048], P('dp', 'tensor'), may hold values from -0.125 to 0.125
- w_swish: bfloat16 [2048, 2048], P('dp', 'tensor'), may hold values from -0.125 to 0.125
- decay_down: bfloat16 [2048, 16], replicated, may hold values from -0.125 to 0.125
- decay_up: bfloat16 [16, 1024], replicated, may hold values from -1.5 to 1.5
- decay_bias: bfloat16 [1024], replicated, may hold values from -3 to 6
- head_gain: bfloat16 [512], replicated, may hold values from 0.5 to 1.5
- w_output: bfloat16 [2048, 2048], P('tensor', 'dp'), may hold values from -0.125 to 0.125
- dense_gain: bfloat16 [2048], replicated, may hold values from 0.5 to 1.5
- w_gate: bfloat16 [2048, 5632], P('dp', 'tensor'), may hold values from -0.125 to 0.125
- w_up: bfloat16 [2048, 5632], P('dp', 'tensor'), may hold values from -0.125 to 0.125
- w_down: bfloat16 [5632, 2048], P('tensor', 'dp'), may hold values from -0.078125 to 0.078125
Outputs:
- output: bfloat16 [12288, 2048], P('dp')
- grad_tokens: float32 [12288, 2048], P('dp')
- grad_mixer_gain: float32 [2048], replicated
- grad_w_query: float32 [2048, 1024], P('dp', 'tensor')
- grad_w_key: float32 [2048, 1024], P('dp', 'tensor')
- grad_w_value: float32 [2048, 2048], P('dp', 'tensor')
- grad_w_swish: float32 [2048, 2048], P('dp', 'tensor')
- grad_decay_down: float32 [2048, 16], replicated
- grad_decay_up: float32 [16, 1024], replicated
- grad_decay_bias: float32 [1024], replicated
- grad_head_gain: float32 [512], replicated
- grad_w_output: float32 [2048, 2048], P('tensor', 'dp')
- grad_dense_gain: float32 [2048], replicated
- grad_w_gate: float32 [2048, 5632], P('dp', 'tensor')
- grad_w_up: float32 [2048, 5632], P('dp', 'tensor')
- grad_w_down: float32 [5632, 2048], P('tensor', 'dp')
Inputs may be any that keep to these rules, and one draw needn't show every extreme that they name: `segment_ids`: A token's segment id is the position of its document's first token. Ids never fall along the tokens, a new document starts at every multiple of 256, so no document crosses such a boundary, and the last token starts a document of its own. `w_query`: entries of order 2048^-0.5. `w_key`: entries of order 2048^-0.5.
All inputs are finite; a program needn't handle non-finite values.
Results may differ from a plain program's by a relative error of at most 0.014.
Values may be sent and summed in bfloat16 or wider, within the bound.
A program may use at most 1.1875 GiB of HBM per device.

v0:
```python
from functools import partial

import jax
import jax.numpy as jnp
from jax import lax
from jax.sharding import PartitionSpec as P

DK = 256
DV = 512
SPAN = 64
MB = 3


norm_eps = 1e-06
head_eps = 1e-05


def root_norm(values, eps):
    return values * lax.rsqrt(jnp.mean(values * values, axis=-1, keepdims=True) + eps)


def scaled_norm(values, gain):
    return root_norm(values, norm_eps) * gain


def span_step(state, inputs):
    query, keyset, valueset, decay, segment, previous = inputs
    length = query.shape[0]
    running = jnp.cumsum(decay, axis=0)
    places = jnp.arange(length)
    allowed = (places[:, None] >= places[None, :]) & (segment[:, None] == segment[None, :])
    allowed = allowed[:, :, None, None]
    spread = running[:, None] - running[None, :]
    factor = jnp.where(allowed, jnp.exp(jnp.where(allowed, spread, 0.0)), 0.0)
    scores = jnp.sum(query[:, None] * keyset[None, :] * factor, axis=-1)
    inner = jnp.einsum("tsh,she->the", scores, valueset, precision=lax.Precision.HIGHEST)
    carried = (segment == previous).astype(jnp.float32)
    outer = carried[:, None, None] * jnp.einsum(
        "thd,hde->the", query * jnp.exp(running), state, precision=lax.Precision.HIGHEST
    )
    final = running[-1]
    same_last = (segment == segment[-1]).astype(jnp.float32)
    moved = keyset * jnp.exp(final[None] - running) * same_last[:, None, None]
    keep_state = (segment[-1] == previous).astype(jnp.float32)
    fresh = jnp.einsum("shd,she->hde", moved, valueset, precision=lax.Precision.HIGHEST)
    new_state = keep_state * jnp.exp(final)[:, :, None] * state + fresh
    return (new_state, inner + outer)


def to_blocks(values, count):
    return values.reshape((count, SPAN) + values.shape[1:])


def gla_core(query, keyset, valueset, decay, segments):
    length, heads, width = query.shape
    count = length // SPAN
    query = query * width ** (-0.5)
    seg_blocks = segments.reshape(count, SPAN)
    previous = jnp.concatenate([jnp.full((1,), -1, jnp.int32), seg_blocks[:-1, -1]])
    state = jnp.zeros((heads, width, valueset.shape[-1]), jnp.float32)
    _, mixed = lax.scan(
        span_step,
        state,
        (
            to_blocks(query, count),
            to_blocks(keyset, count),
            to_blocks(valueset, count),
            to_blocks(decay, count),
            seg_blocks,
            previous,
        ),
    )
    return mixed.reshape(length, heads, valueset.shape[-1])


def mixer_core(query, keyset, valueset, decay, swish_in, gain, segments):
    length = query.shape[0]
    heads = query.shape[1] // DK
    mixed = gla_core(
        query.reshape(length, heads, DK),
        keyset.reshape(length, heads, DK),
        valueset.reshape(length, heads, DV),
        decay.reshape(length, heads, DK),
        segments,
    )
    normed = root_norm(mixed, head_eps) * gain
    return (normed * jax.nn.silu(swish_in.reshape(length, heads, DV))).reshape(length, heads * DV)


def decay_gate(lowrank, up_factor, bias):
    return (
        jax.nn.log_sigmoid(jnp.dot(lowrank, up_factor, precision=lax.Precision.HIGHEST) + bias)
        / 16.0
    )


def matmul(left, right):
    return jnp.dot(left, right, preferred_element_type=jnp.float32)


def on_device(
    tokens,
    segment_ids,
    cotangent,
    mixer_gain,
    w_query,
    w_key,
    w_value,
    w_swish,
    decay_down,
    decay_up,
    decay_bias,
    head_gain,
    w_output,
    dense_gain,
    w_gate,
    w_up,
    w_down,
):
    shards = (w_query, w_key, w_value, w_swish, w_output, w_gate, w_up, w_down)
    gathered = (
        lax.all_gather(shards[0], "dp", axis=0, tiled=True),
        lax.all_gather(shards[1], "dp", axis=0, tiled=True),
        lax.all_gather(shards[2], "dp", axis=0, tiled=True),
        lax.all_gather(shards[3], "dp", axis=0, tiled=True),
        lax.all_gather(shards[4], "dp", axis=1, tiled=True),
        lax.all_gather(shards[5], "dp", axis=0, tiled=True),
        lax.all_gather(shards[6], "dp", axis=0, tiled=True),
        lax.all_gather(shards[7], "dp", axis=1, tiled=True),
    )
    rank = lax.axis_index("tensor")
    groups = lax.axis_size("tensor")
    key_cols = w_query.shape[1]
    rows = tokens.shape[0] // MB
    half_rows = rows // groups
    up_own = lax.dynamic_slice_in_dim(decay_up, rank * key_cols, key_cols, 1).astype(jnp.float32)
    bias_own = lax.dynamic_slice_in_dim(decay_bias, rank * key_cols, key_cols, 0).astype(
        jnp.float32
    )
    down_full = decay_down.astype(jnp.float32)
    gain_first = mixer_gain.astype(jnp.float32)
    gain_second = dense_gain.astype(jnp.float32)
    gain_heads = head_gain.astype(jnp.float32)
    totals = tuple((jnp.zeros(matrix.shape, jnp.float32) for matrix in gathered))
    small = (
        jnp.zeros(mixer_gain.shape, jnp.float32),
        jnp.zeros(dense_gain.shape, jnp.float32),
        jnp.zeros(head_gain.shape, jnp.float32),
        jnp.zeros(decay_down.shape, jnp.float32),
        jnp.zeros(decay_up.shape, jnp.float32),
        jnp.zeros(decay_bias.shape, jnp.float32),
    )
    outputs = []
    input_grads = []
    for batch_index in range(MB):
        begin = batch_index * rows
        wq_all, wk_all, wv_all, ws_all, wo_all, wg_all, wu_all, wd_all = gathered
        x_part = tokens[begin : begin + rows].astype(jnp.float32)
        seg_part = segment_ids[begin : begin + rows]
        first_f, first_pull = jax.vjp(partial(scaled_norm, gain=gain_first), x_part)
        first_normed = root_norm(x_part, norm_eps)
        first = first_f.astype(jnp.bfloat16)
        query = matmul(first, wq_all).astype(jnp.bfloat16)
        keyset = matmul(first, wk_all).astype(jnp.bfloat16)
        valueset = matmul(first, wv_all).astype(jnp.bfloat16)
        swish_in = matmul(first, ws_all)
        lowrank = matmul(first, decay_down)
        decay, gate_pull = jax.vjp(decay_gate, lowrank, up_own, bias_own)
        gated_f, core_pull = jax.vjp(
            partial(mixer_core, segments=seg_part),
            query.astype(jnp.float32),
            keyset.astype(jnp.float32),
            valueset.astype(jnp.float32),
            decay,
            swish_in,
            gain_heads,
        )
        gated = gated_f.astype(jnp.bfloat16)
        branch = lax.psum(matmul(gated, wo_all), "tensor")
        hidden = x_part + branch
        second_f, second_pull = jax.vjp(partial(scaled_norm, gain=gain_second), hidden)
        second_normed = root_norm(hidden, norm_eps)
        second = second_f.astype(jnp.bfloat16)
        gate = matmul(second, wg_all)
        upper = matmul(second, wu_all)
        sigma = jax.nn.sigmoid(gate)
        swished = gate * sigma
        product = (swished * upper).astype(jnp.bfloat16)
        dense_out = lax.psum(matmul(product, wd_all), "tensor")
        outputs.append((hidden + dense_out).astype(jnp.bfloat16))
        wq_all, wk_all, wv_all, ws_all, wo_all, wg_all, wu_all, wd_all = (
            lax.all_gather(shards[0], "dp", axis=0, tiled=True),
            lax.all_gather(shards[1], "dp", axis=0, tiled=True),
            lax.all_gather(shards[2], "dp", axis=0, tiled=True),
            lax.all_gather(shards[3], "dp", axis=0, tiled=True),
            lax.all_gather(shards[4], "dp", axis=1, tiled=True),
            lax.all_gather(shards[5], "dp", axis=0, tiled=True),
            lax.all_gather(shards[6], "dp", axis=0, tiled=True),
            lax.all_gather(shards[7], "dp", axis=1, tiled=True),
        )
        cot_part = cotangent[begin : begin + rows]
        cot_float = cot_part.astype(jnp.float32)
        d_product = matmul(cot_part, wd_all.T)
        grad_down = matmul(product.T, cot_part)
        d_gate = (d_product * upper * (sigma + gate * sigma * (1.0 - sigma))).astype(jnp.bfloat16)
        d_up = (d_product * swished).astype(jnp.bfloat16)
        grad_gate = matmul(second.T, d_gate)
        grad_up = matmul(second.T, d_up)
        d_second = lax.psum(matmul(d_gate, wg_all.T) + matmul(d_up, wu_all.T), "tensor")
        d_hidden = cot_float + second_pull(d_second)[0]
        second_gain_part = jnp.sum(
            lax.dynamic_slice_in_dim(d_second * second_normed, rank * half_rows, half_rows, 0),
            axis=0,
        )
        d_branch = d_hidden.astype(jnp.bfloat16)
        grad_output = matmul(gated.T, d_branch)
        d_gated = matmul(d_branch, wo_all.T)
        d_query, d_keyset, d_valueset, d_decay, d_swish, head_part = core_pull(d_gated)
        d_query = d_query.astype(jnp.bfloat16)
        d_keyset = d_keyset.astype(jnp.bfloat16)
        d_valueset = d_valueset.astype(jnp.bfloat16)
        d_swish = d_swish.astype(jnp.bfloat16)
        d_lowrank, up_part, bias_part = gate_pull(d_decay)
        d_first_part = (
            matmul(d_query, wq_all.T)
            + matmul(d_keyset, wk_all.T)
            + matmul(d_valueset, wv_all.T)
            + matmul(d_swish, ws_all.T)
            + jnp.dot(d_lowrank, down_full.T, precision=lax.Precision.HIGHEST)
        )
        d_first = lax.psum(d_first_part, "tensor")
        input_grads.append(d_hidden + first_pull(d_first)[0])
        first_gain_part = jnp.sum(
            lax.dynamic_slice_in_dim(d_first * first_normed, rank * half_rows, half_rows, 0), axis=0
        )
        first_float = first.astype(jnp.float32)
        down_part = jnp.dot(first_float.T, d_lowrank, precision=lax.Precision.HIGHEST)
        up_whole = lax.dynamic_update_slice_in_dim(
            jnp.zeros(decay_up.shape, jnp.float32), up_part, rank * key_cols, 1
        )
        bias_whole = lax.dynamic_update_slice_in_dim(
            jnp.zeros(decay_bias.shape, jnp.float32), bias_part, rank * key_cols, 0
        )
        terms = (
            matmul(first.T, d_query),
            matmul(first.T, d_keyset),
            matmul(first.T, d_valueset),
            matmul(first.T, d_swish),
            grad_output,
            grad_gate,
            grad_up,
            grad_down,
        )
        totals = tuple((current + added for current, added in zip(totals, terms)))
        small = (
            small[0] + first_gain_part,
            small[1] + second_gain_part,
            small[2] + head_part,
            small[3] + down_part,
            small[4] + up_whole,
            small[5] + bias_whole,
        )
    totals = (
        lax.psum_scatter(totals[0], "dp", scatter_dimension=0, tiled=True),
        lax.psum_scatter(totals[1], "dp", scatter_dimension=0, tiled=True),
        lax.psum_scatter(totals[2], "dp", scatter_dimension=0, tiled=True),
        lax.psum_scatter(totals[3], "dp", scatter_dimension=0, tiled=True),
        lax.psum_scatter(totals[4], "dp", scatter_dimension=1, tiled=True),
        lax.psum_scatter(totals[5], "dp", scatter_dimension=0, tiled=True),
        lax.psum_scatter(totals[6], "dp", scatter_dimension=0, tiled=True),
        lax.psum_scatter(totals[7], "dp", scatter_dimension=1, tiled=True),
    )
    small = lax.psum((small[0], small[1], small[2], small[3], small[4], small[5]), ("dp", "tensor"))
    output = jnp.concatenate(outputs, axis=0)
    grad_tokens = jnp.concatenate(input_grads, axis=0)
    return (
        output,
        grad_tokens,
        small[0],
        totals[0],
        totals[1],
        totals[2],
        totals[3],
        small[3],
        small[4],
        small[5],
        small[2],
        totals[4],
        small[1],
        totals[5],
        totals[6],
        totals[7],
    )


def solution(mesh):
    in_specs = (
        P("dp", None),
        P("dp"),
        P("dp", None),
        P(),
        P("dp", "tensor"),
        P("dp", "tensor"),
        P("dp", "tensor"),
        P("dp", "tensor"),
        P(),
        P(),
        P(),
        P(),
        P("tensor", "dp"),
        P(),
        P("dp", "tensor"),
        P("dp", "tensor"),
        P("tensor", "dp"),
    )
    out_specs = (
        P("dp", None),
        P("dp", None),
        P(),
        P("dp", "tensor"),
        P("dp", "tensor"),
        P("dp", "tensor"),
        P("dp", "tensor"),
        P(),
        P(),
        P(),
        P(),
        P("tensor", "dp"),
        P(),
        P("dp", "tensor"),
        P("dp", "tensor"),
        P("tensor", "dp"),
    )
    return jax.shard_map(
        on_device, mesh=mesh, in_specs=in_specs, out_specs=out_specs, check_vma=False
    )
```

profile of v0, /device:TPU:10, one launch (start us, length us, event | category | flops | bytes accessed | tf_op | source)
XLA Modules:
  0.0 4866.0 jit_solution(2740324352787111061)
XLA Ops:
  33.1 39.5 all-gather.13.cloned.1.call-done
  78.0 56.8 %all-gather.9.cloned.1.call-done = bf16[2048,512]{1,0:T(8,128)(2,1)} async-done(((bf16[128,512]{1,0:T(8,128)(2,1)}), bf16[2048,512]{1,0:T(8,128)(2,1)}) %all-gather.9.cloned.1.call-update) | async-done | bytes 2097168 | tf_op jit(solution)/shard_map/all_gather | solution.py:123
  162.0 50.5 %all-gather.11.cloned.1.call-done = bf16[2048,1024]{1,0:T(8,128)(2,1)} async-done(((bf16[128,1024]{1,0:T(8,128)(2,1)}), bf16[2048,1024]{1,0:T(8,128)(2,1)}) %all-gather.11.cloned.1.call-update) | async-done | bytes 4194320 | tf_op jit(solution)/shard_map/all_gather | solution.py:124
  277.5 217.6 %while.226 = (s32[]{:T(128)}, f32[2,256,512]{2,1,0:T(8,128)}, f32[4,64,2,512]{3,1,2,0:T(8,128)}, pred[4,64,64,2,256]{4,3,2,1,0:T(4,128)(4,1)}, f32[4,64,64,2,256...) while((s32[]{:T(128)}, f32[2,256,512]{2,1,0:T(8,128)}, ...), condition=%wide.region_13.15_spmd.clone, body=%wide.region_10.14_spmd.clone.sunk | while | flops 477730304 | bytes 41205016 | solution.py:61
  557.2 208.2 %while.227 = (s32[]{:T(128)}, f32[2,256,512]{2,1,0:T(8,128)S(1)}, f32[4,64,2,512]{3,1,2,0:T(8,128)S(1)}, pred[4,64,64,2,256]{4,3,2,1,0:T(4,128)(4,1)}, f32[4,64,...) while((s32[]{:T(128)}, f32[2,256,512]{2,1,0:T(8,128)S(1)}, ...), condition=%wide.region_22.24_spmd.clone, body=%wide.region_19.23_spmd.clone.sunk | while | flops 477730304 | bytes 41219568 | solution.py:61
  828.6 210.9 %while.225 = (s32[]{:T(128)}, f32[2,256,512]{2,1,0:T(8,128)S(1)}, f32[4,64,2,512]{3,1,2,0:T(8,128)}, pred[4,64,64,2,256]{4,3,2,1,0:T(4,128)(4,1)}, f32[4,64,64,2...) while((s32[]{:T(128)}, f32[2,256,512]{2,1,0:T(8,128)S(1)}, ...), condition=%wide.region_4.6_spmd.clone, body=%wide.region_1.5_spmd.clone.sunk | while | flops 477730304 | bytes 41186800 | solution.py:61
  1077.1 29.0 all-reduce.19.cloned.1.call-done
  1114.9 135.4 %all-gather.19.cloned.1.call-done = bf16[2048,2816]{1,0:T(8,128)(2,1)} async-done(((bf16[128,2816]{1,0:T(8,128)(2,1)}), bf16[2048,2816]{1,0:T(8,128)(2,1)}) %all-gather.19.cloned.1.call-update) | async-done | bytes 11534352 | tf_op jit(solution)/shard_map/all_gather | solution.py:127
  1259.8 134.0 %all-gather.21.cloned.1.call-done = bf16[2048,2816]{1,0:T(8,128)(2,1)} async-done(((bf16[128,2816]{1,0:T(8,128)(2,1)}), bf16[2048,2816]{1,0:T(8,128)(2,1)}) %all-gather.21.cloned.1.call-update) | async-done | bytes 11534352 | tf_op jit(solution)/shard_map/all_gather | solution.py:128
  1422.1 154.8 %all-gather.23.cloned.1.call-done = bf16[2816,2048]{1,0:T(8,128)(2,1)} async-done(((bf16[2816,128]{1,0:T(8,128)(2,1)}), bf16[2816,2048]{1,0:T(8,128)(2,1)}) %all-gather.23.cloned.1.call-update) | async-done | bytes 11534352 | tf_op jit(solution)/shard_map/all_gather | solution.py:129
  1760.7 223.2 %while.229 = (s32[]{:T(128)}, f32[2,256,512]{2,1,0:T(8,128)S(1)}, f32[4,64,2,256]{3,2,1,0:T(2,128)}, bf16[4,64,2,256]{3,1,2,0:T(8,128)(2,1)}, bf16[4,64,2,512]{3...) while((s32[]{:T(128)}, f32[2,256,512]{2,1,0:T(8,128)S(1)}, ...), condition=%wide.region_52.54_spmd.clone, body=%wide.region_44.53_spmd.clone.sunk | while | flops 933855744 | bytes 66290916 | solution.py:61
  1991.5 223.9 %while.228 = (s32[]{:T(128)}, f32[2,256,512]{2,1,0:T(8,128)S(1)}, f32[4,64,2,256]{3,2,1,0:T(2,128)}, bf16[4,64,2,256]{3,1,2,0:T(8,128)(2,1)}, bf16[4,64,2,512]{3...) while((s32[]{:T(128)}, f32[2,256,512]{2,1,0:T(8,128)S(1)}, ...), condition=%wide.region_38.40_spmd.clone, body=%wide.region_30.39_spmd.clone.sunk | while | flops 933855744 | bytes 66290916 | solution.py:61
  2220.3 224.3 %while.230 = (s32[]{:T(128)}, f32[2,256,512]{2,1,0:T(8,128)S(1)}, f32[4,64,2,256]{3,2,1,0:T(2,128)}, bf16[4,64,2,256]{3,1,2,0:T(8,128)(2,1)}, bf16[4,64,2,512]{3...) while((s32[]{:T(128)}, f32[2,256,512]{2,1,0:T(8,128)S(1)}, ...), condition=%wide.region_66.68_spmd.clone, body=%wide.region_58.67_spmd.clone.sunk | while | flops 933855744 | bytes 66290916 | solution.py:61
  2562.4 24.7 add_add_fusion
  2608.6 24.5 add_add_fusion.1
  2653.6 24.5 add_add_fusion.2
  2701.3 45.8 all-reduce.3
  2762.3 96.8 %reduce-scatter.9.cloned.1.call-done = f32[128,512]{1,0:T(8,128)} async-done(((f32[2048,512]{1,0:T(8,128)}), f32[128,512]{1,0:T(8,128)}) %reduce-scatter.9.cloned.1.call-update) | async-done | bytes 262160 | tf_op jit(solution)/shard_map/reduce_scatter | solution.py:264
  2859.1 183.7 %reduce-scatter.17.cloned.1.call-done = f32[1024,128]{1,0:T(8,128)} async-done(((f32[1024,2048]{1,0:T(8,128)}), f32[1024,128]{1,0:T(8,128)}) %reduce-scatter.17.cloned.1.call-update) | async-done | bytes 524304 | tf_op jit(solution)/shard_map/reduce_scatter | solution.py:268
  3042.8 183.0 %reduce-scatter.15.cloned.1.call-done = f32[128,1024]{1,0:T(8,128)} async-done(((f32[2048,1024]{1,0:T(8,128)}), f32[128,1024]{1,0:T(8,128)}) %reduce-scatter.15.cloned.1.call-update) | async-done | bytes 524304 | tf_op jit(solution)/shard_map/reduce_scatter | solution.py:267
  3225.8 183.0 %reduce-scatter.13.cloned.1.call-done = f32[128,1024]{1,0:T(8,128)} async-done(((f32[2048,1024]{1,0:T(8,128)}), f32[128,1024]{1,0:T(8,128)}) %reduce-scatter.13.cloned.1.call-update) | async-done | bytes 524304 | tf_op jit(solution)/shard_map/reduce_scatter | solution.py:266
  3408.7 481.9 %reduce-scatter.23.cloned.1.call-done = f32[2816,128]{1,0:T(8,128)} async-done(((f32[2816,2048]{1,0:T(8,128)}), f32[2816,128]{1,0:T(8,128)}) %reduce-scatter.23.cloned.1.call-update) | async-done | bytes 1441808 | tf_op jit(solution)/shard_map/reduce_scatter | solution.py:271
  3890.6 482.7 %reduce-scatter.21.cloned.1.call-done = f32[128,2816]{1,0:T(8,128)} async-done(((f32[2048,2816]{1,0:T(8,128)}), f32[128,2816]{1,0:T(8,128)}) %reduce-scatter.21.cloned.1.call-update) | async-done | bytes 1441808 | tf_op jit(solution)/shard_map/reduce_scatter | solution.py:270
  4373.3 482.6 %reduce-scatter.19.cloned.1.call-done = f32[128,2816]{1,0:T(8,128)} async-done(((f32[2048,2816]{1,0:T(8,128)}), f32[128,2816]{1,0:T(8,128)}) %reduce-scatter.19.cloned.1.call-update) | async-done | bytes 1441808 | tf_op jit(solution)/shard_map/reduce_scatter | solution.py:269
  (1672 shorter events, 2015.5 us)
Async XLA Ops:
  7.2 65.4 %all-gather.13.cloned.1.call-start = ((), (), s32[]{:S(2)}) async-start(), calls=%async_computation.10 | async-start | bytes 2228224 | tf_op jit(solution)/shard_map/all_gather | solution.py:122
  8.0 126.8 %all-gather.9.cloned.1.call-start = ((), (), s32[]{:S(2)}) async-start(), calls=%async_computation.8 | async-start | bytes 2228224 | tf_op jit(solution)/shard_map/all_gather | solution.py:123
  8.7 203.8 %all-gather.11.cloned.1.call-start = ((), (), s32[]{:S(2)}) async-start(), calls=%async_computation.9 | async-start | bytes 4456448 | tf_op jit(solution)/shard_map/all_gather | solution.py:124
  9.4 1043.3 %all-gather.15.cloned.1.call-start = ((), (), s32[]{:S(2)}) async-start(), calls=%async_computation.11 | async-start | bytes 4456448 | tf_op jit(solution)/shard_map/all_gather | solution.py:125
  10.0 1054.0 %all-gather.17.cloned.1.call-start = ((), (), s32[]{:S(2)}) async-start(), calls=%async_computation.12 | async-start | bytes 4456448 | tf_op jit(solution)/shard_map/all_gather | solution.py:126
  10.6 1095.5 %all-reduce.19.cloned.1.call-start = ((), (), s32[]{:S(2)}) async-start(), calls=%async_computation.27 | async-start | bytes 12582912 | tf_op jit(solution)/shard_map/psum | solution.py:179
  11.4 483.7 %copy-start.67 = (f32[2048]{0:T(1024)}, f32[2048]{0:T(1024)S(1)}, u32[]{:S(2)}) copy-start(f32[2048]{0:T(1024)S(1)} %convert_element_type.390) | copy-start | bytes 24580
  765.4 278.1 %copy-start.20 = (f32[4,64,2,512]{3,1,2,0:T(8,128)}, f32[4,64,2,512]{3,1,2,0:T(8,128)S(1)}, u32[]{:S(2)}) copy-start(f32[4,64,2,512]{3,1,2,0:T(8,128)S(1)} %get-tuple-element.2901) | copy-start | bytes 3145732
  828.6 210.9 %copy-start.18 = (f32[4,64,2,512]{3,1,2,0:T(8,128)S(1)}, f32[4,64,2,512]{3,1,2,0:T(8,128)}, u32[]{:S(2)}) copy-start(f32[4,64,2,512]{3,1,2,0:T(8,128)} %get-tuple-element.2899) | copy-start | bytes 3145732
  1074.8 175.5 %all-gather.19.cloned.1.call-start = ((), (), s32[]{:S(2)}) async-start(), calls=%async_computation.13 | async-start | bytes 12255232 | tf_op jit(solution)/shard_map/all_gather | solution.py:127
  1075.6 318.2 %all-gather.21.cloned.1.call-start = ((), (), s32[]{:S(2)}) async-start(), calls=%async_computation.14 | async-start | bytes 12255232 | tf_op jit(solution)/shard_map/all_gather | solution.py:128
  1076.3 500.5 %all-gather.23.cloned.1.call-start = ((), (), s32[]{:S(2)}) async-start(), calls=%async_computation.15 | async-start | bytes 12255232 | tf_op jit(solution)/shard_map/all_gather | solution.py:129
  1077.0 632.5 %all-reduce.17.cloned.1.call-start = ((), (), s32[]{:S(2)}) async-start(), calls=%async_computation.26 | async-start | bytes 12582912 | tf_op jit(solution)/shard_map/psum | solution.py:209
  1673.3 1010.9 %all-reduce.15.cloned.1.call-start = ((), (), s32[]{:S(2)}) async-start(), calls=%async_computation.25 | async-start | bytes 25165824 | tf_op jit(solution)/shard_map/psum | solution.py:189
  1760.7 225.3 %copy-start.172 = (f32[4,64,2]{1,2,0:T(2,128)S(1)}, f32[4,64,2]{1,2,0:T(2,128)}, u32[]{:S(2)}) copy-start(f32[4,64,2]{1,2,0:T(2,128)} %copy-done.171) | copy-start | bytes 6148
  2479.2 275.1 %all-reduce.13.cloned.1.call-start = ((), (), s32[]{:S(2)}) async-start(), calls=%async_computation.24 | async-start | bytes 393216 | tf_op jit(solution)/shard_map/psum | solution.py:273
  2495.7 266.6 %reduce-scatter.11.cloned.1.call-start = ((), (), s32[]{:S(2)}) async-start(), calls=%async_computation.17 | async-start | bytes 4456448 | tf_op jit(solution)/shard_map/reduce_scatter | solution.py:265
  2503.8 355.3 %reduce-scatter.9.cloned.1.call-start = ((), (), s32[]{:S(2)}) async-start(), calls=%async_computation.16 | async-start | bytes 4456448 | tf_op jit(solution)/shard_map/reduce_scatter | solution.py:264
  2510.3 532.5 %reduce-scatter.17.cloned.1.call-start = ((), (), s32[]{:S(2)}) async-start(), calls=%async_computation.20 | async-start | bytes 8912896 | tf_op jit(solution)/shard_map/reduce_scatter | solution.py:268
  2521.2 704.6 %reduce-scatter.15.cloned.1.call-start = ((), (), s32[]{:S(2)}) async-start(), calls=%async_computation.19 | async-start | bytes 8912896 | tf_op jit(solution)/shard_map/reduce_scatter | solution.py:267
  2530.7 878.0 %reduce-scatter.13.cloned.1.call-start = ((), (), s32[]{:S(2)}) async-start(), calls=%async_computation.18 | async-start | bytes 8912896 | tf_op jit(solution)/shard_map/reduce_scatter | solution.py:266
  2540.0 1350.6 %reduce-scatter.23.cloned.1.call-start = ((), (), s32[]{:S(2)}) async-start(), calls=%async_computation.23 | async-start | bytes 24510464 | tf_op jit(solution)/shard_map/reduce_scatter | solution.py:271
  2587.1 1786.2 %reduce-scatter.21.cloned.1.call-start = ((), (), s32[]{:S(2)}) async-start(), calls=%async_computation.22 | async-start | bytes 24510464 | tf_op jit(solution)/shard_map/reduce_scatter | solution.py:270
  2633.2 2222.7 %reduce-scatter.19.cloned.1.call-start = ((), (), s32[]{:S(2)}) async-start(), calls=%async_computation.21 | async-start | bytes 24510464 | tf_op jit(solution)/shard_map/reduce_scatter | solution.py:269
  (335 other events, 3719.1 us)
Sparse Core Ops, SparseCore 0:
  10.8 61.7 all-gather.12
  75.4 59.3 all-gather.8
  137.6 74.8 all-gather.10
  215.1 74.6 all-gather.14
  292.4 85.0 all-gather.16
  1074.9 31.1 all-reduce.18
  1109.2 141.0 all-gather.18
  1253.4 140.3 all-gather.20
  1396.9 179.9 all-gather.22
  1673.5 33.4 all-reduce.16
  2479.3 51.4 all-reduce.14
  2537.5 126.0 all-reduce.12
  2666.5 95.7 reduce-scatter.10
  2765.0 94.0 reduce-scatter.8
  2861.8 180.8 reduce-scatter.16
  3045.5 180.2 reduce-scatter.14
  3228.5 180.2 reduce-scatter.12
  3411.5 479.1 reduce-scatter.22
  3893.5 479.7 reduce-scatter.20
  4376.0 479.7 reduce-scatter.18
where the time goes:
time: 4890 us; the launch traced here: 4870 us
  waiting for transfers between devices  2710 us (55%)
  other arithmetic  848 us (17%)
  matrix products  641 us (13%)
  local copies, waits for them, and re-layouts  585 us (12%)
    reduce_scatter x1, waiting for transfers between devices, on_device(): lax.psum_scatter(totals[6], 'dp', scatter_dimension=0, tiled=True)  483 us
    reduce_scatter x1, waiting for transfers between devices, on_device(): lax.psum_scatter(totals[5], 'dp', scatter_dimension=0, tiled=True)  483 us
    reduce_scatter x1, waiting for transfers between devices, on_device(): lax.psum_scatter(totals[7], 'dp', scatter_dimension=1, tiled=True)  482 us
    dot_general x75, matrix products, matmul(): return jnp.dot(left, right, preferred_element_type=jnp.float32)  425 us
    dynamic_update_slice x96, other arithmetic, gla_core(): lax.scan(span_step, state, (to_blocks(query, count), to_blocks(keyset, co...  291 us
    reduce_sum x24, other arithmetic, span_step(): scores = jnp.sum(query[:, None] * keyset[None, :] * factor, axis=-1)  289 us
    reduce_scatter x1, waiting for transfers between devices, on_device(): lax.psum_scatter(totals[4], 'dp', scatter_dimension=1, tiled=True)  184 us
    reduce_scatter x1, waiting for transfers between devices, on_device(): lax.psum_scatter(totals[3], 'dp', scatter_dimension=0, tiled=True)  183 us
  transfers between devices with their start and end apart: 20, of which 15 were waited for; matrix products, arithmetic and copies ran while one was open for 24% of the time, Pallas kernels for 0%

commit v1 on v0

v1 whole, which is shorter than its diff:
```python
from functools import partial

import jax
import jax.numpy as jnp
import numpy as np
from jax import lax
from jax.experimental import pallas as pl
from jax.experimental.pallas import tpu as pltpu
from jax.sharding import PartitionSpec as P

DK = 256
DV = 512
PIECE = 256
norm_eps = 1e-06
head_eps = 1e-05
LEVELS = (1, 2, 4, 8, 16, 32, 64, 128)
f32 = jnp.float32
bf16 = jnp.bfloat16
HIGH = lax.Precision.HIGHEST


def layout(chips):
    return {16: (4, 2, 1, 2), 64: (4, 4, 2, 2)}.get(chips, (1, 1, chips // 2, 2))


def shift_pairs(sizes, axis, step):
    pairs = []
    for place in range(int(np.prod(sizes))):
        at = list(np.unravel_index(place, sizes))
        at[axis] = (at[axis] + step) % sizes[axis]
        pairs.append((place, int(np.ravel_multi_index(at, sizes))))
    return pairs


def shift(values, sizes, axis, step):
    return lax.ppermute(values, "dp", shift_pairs(sizes, axis, step))


def core_swap(values):
    return lax.ppermute(values, "tensor", [(0, 1), (1, 0)])


def in_order(index, own, other):
    return jnp.where(
        index == 0, jnp.concatenate([own, other], 0), jnp.concatenate([other, own], 0)
    )


def half(values, index, axis=0):
    size = values.shape[axis] // 2
    return lax.dynamic_slice_in_dim(values, index * size, size, axis)


def mm(left, right):
    return lax.dot_general(left, right, (((1,), (0,)), ((), ())), preferred_element_type=f32)


def mm_nt(left, right):
    return lax.dot_general(left, right, (((1,), (1,)), ((), ())), preferred_element_type=f32)


def mm_tn(left, right):
    return lax.dot_general(left, right, (((0,), (0,)), ((), ())), preferred_element_type=f32)


def reorder_kernel(places, source, target):
    count = places.shape[0]
    width = source.shape[1] // count
    for block in range(count):
        start = pl.multiple_of(places[block] * width, width)
        target[:, block * width : (block + 1) * width] = source[:, pl.ds(start, width)]


def reorder(values, places):
    rows, columns = values.shape
    count = places.shape[0]
    width = columns // count
    if width % 128 != 0:
        return jnp.concatenate(
            [lax.dynamic_slice_in_dim(values, places[i] * width, width, 1) for i in range(count)], 1
        )
    tile = 192 if rows % 192 == 0 else rows
    return pl.pallas_call(
        reorder_kernel,
        out_shape=jax.ShapeDtypeStruct(values.shape, values.dtype),
        grid_spec=pltpu.PrefetchScalarGridSpec(
            num_scalar_prefetch=1,
            grid=(rows // tile,),
            in_specs=[pl.BlockSpec((tile, columns), lambda i, p: (i, 0))],
            out_specs=pl.BlockSpec((tile, columns), lambda i, p: (i, 0)),
        ),
        cost_estimate=pl.CostEstimate(
            flops=0, bytes_accessed=2 * values.size * values.dtype.itemsize, transcendentals=0
        ),
        name="reorder",
    )(places, values)


def bit_of(shape, level):
    return (lax.broadcasted_iota(jnp.int32, shape, 0) & level) != 0


def partner(values, level, upper):
    size = values.shape[0]
    return jnp.where(
        upper, pltpu.roll(values, level, 0), pltpu.roll(values, size - level, 0)
    )


def log_decay(low, up, bias):
    pre = jnp.dot(low, up, precision=HIGH, preferred_element_type=f32) + bias
    return pre, (jnp.minimum(pre, 0.0) - jnp.log1p(jnp.exp(-jnp.abs(pre)))) * (1.0 / 16.0)


def level_exponents(decay):
    prefix, suffix, total = decay, jnp.zeros_like(decay), decay
    found = []
    for level in LEVELS:
        upper = bit_of(decay.shape, level)
        found.append(jnp.where(upper, prefix, suffix))
        if level != LEVELS[-1]:
            beside = partner(total, level, upper)
            prefix = prefix + jnp.where(upper, beside, 0.0)
            suffix = suffix + jnp.where(upper, 0.0, beside)
            total = total + beside
    return found


def pair_distance():
    rows = lax.broadcasted_iota(jnp.int32, (PIECE, PIECE), 0)
    columns = lax.broadcasted_iota(jnp.int32, (PIECE, PIECE), 1)
    return rows ^ columns, rows >= columns


def core_forward_kernel(qkv, swish, low, seg_col, seg_row, up, bias, gain, gated, scores_out, mixed_out):
    query = qkv[:, :DK].astype(f32)
    keyset = qkv[:, DK : 2 * DK].astype(f32)
    values = qkv[:, 2 * DK :]
    _, decay = log_decay(low[...], up[...], bias[...])
    apart, causal = pair_distance()
    scores = mm_nt(qkv[:, :DK], qkv[:, DK : 2 * DK])
    for level, exponent in zip(LEVELS, level_exponents(decay)):
        upper = bit_of(decay.shape, level)
        scaled = (jnp.where(upper, query, keyset) * jnp.exp(exponent)).astype(bf16)
        scores = jnp.where(apart >= level, mm_nt(scaled, scaled), scores)
    allowed = causal & (seg_col[...] == seg_row[0])
    scores = jnp.where(allowed, scores * (DK**-0.5), 0.0).astype(bf16)
    mixed = mm(scores, values)
    scores_out[...] = scores
    mixed_out[...] = mixed
    root = lax.rsqrt(jnp.mean(mixed * mixed, axis=-1, keepdims=True) + head_eps)
    opened = swish[...]
    gated[...] = (mixed * root * gain[...] * (opened * jax.nn.sigmoid(opened))).astype(bf16)


def core_backward_kernel(
    qkv, swish, low, seg_col, seg_row, up, bias, gain, scores_in, mixed_in, d_gated,
    d_qkvs, d_low, d_up, d_bias, d_gain,
):
    query = qkv[:, :DK].astype(f32)
    keyset = qkv[:, DK : 2 * DK].astype(f32)
    values = qkv[:, 2 * DK :]
    pre, decay = log_decay(low[...], up[...], bias[...])
    apart, causal = pair_distance()
    mixed = mixed_in[...]
    root = lax.rsqrt(jnp.mean(mixed * mixed, axis=-1, keepdims=True) + head_eps)
    normed = mixed * root
    opened = swish[...]
    sigma = jax.nn.sigmoid(opened)
    wanted = d_gated[...]
    d_swish = wanted * normed * gain[...] * (sigma + opened * sigma * (1.0 - sigma))
    d_scaled = wanted * (opened * sigma)
    gain_part = jnp.sum(d_scaled * normed, axis=0, keepdims=True)
    d_normed = d_scaled * gain[...]
    d_mixed = root * (d_normed - normed * jnp.mean(d_normed * normed, axis=-1, keepdims=True))
    d_mixed = d_mixed.astype(bf16)
    d_values = mm_tn(scores_in[...], d_mixed)
    allowed = causal & (seg_col[...] == seg_row[0])
    d_scores = jnp.where(allowed, mm_nt(d_mixed, values) * (DK**-0.5), 0.0)
    on_diagonal = jnp.sum(jnp.where(apart == 0, d_scores, 0.0), axis=1, keepdims=True)
    d_query = on_diagonal * keyset
    d_keyset = on_diagonal * query
    both = d_scores + d_scores.T
    exponents = level_exponents(decay)
    d_prefix = d_suffix = d_total = jnp.zeros_like(decay)
    for level, exponent in reversed(list(zip(LEVELS, exponents))):
        upper = bit_of(decay.shape, level)
        if level != LEVELS[-1]:
            d_beside = jnp.where(upper, d_prefix, d_suffix) + d_total
            d_total = d_total + partner(d_beside, level, upper)
        base = jnp.where(upper, query, keyset)
        factor = jnp.exp(exponent)
        scaled = (base * factor).astype(bf16)
        here = jnp.where((apart >= level) & (apart < 2 * level), both, 0.0).astype(bf16)
        d_base = mm(here, scaled) * factor
        d_exponent = d_base * base
        d_query = d_query + jnp.where(upper, d_base, 0.0)
        d_keyset = d_keyset + jnp.where(upper, 0.0, d_base)
        d_prefix = d_prefix + jnp.where(upper, d_exponent, 0.0)
        d_suffix = d_suffix + jnp.where(upper, 0.0, d_exponent)
    d_pre = (d_prefix + d_total) * jax.nn.sigmoid(-pre) * (1.0 / 16.0)
    d_qkvs[:, :DK] = d_query.astype(bf16)
    d_qkvs[:, DK : 2 * DK] = d_keyset.astype(bf16)
    d_qkvs[:, 2 * DK : 2 * DK + DV] = d_values.astype(bf16)
    d_qkvs[:, 2 * DK + DV :] = d_swish.astype(bf16)
    d_low[...] = lax.dot_general(
        d_pre, up[...], (((1,), (1,)), ((), ())), precision=HIGH, preferred_element_type=f32
    )

    @pl.when(pl.program_id(0) == 0)
    def _():
        d_up[...] = jnp.zeros_like(d_up)
        d_bias[...] = jnp.zeros_like(d_bias)
        d_gain[...] = jnp.zeros_like(d_gain)

    d_up[...] += lax.dot_general(
        low[...], d_pre, (((0,), (0,)), ((), ())), precision=HIGH, preferred_element_type=f32
    )
    d_bias[...] += jnp.sum(d_pre, axis=0, keepdims=True)
    d_gain[...] += gain_part


def by_piece(width):
    return pl.BlockSpec((PIECE, width), lambda i: (i, 0))


def at_once(shape):
    return pl.BlockSpec(shape, lambda i: (0,) * len(shape))


def core_specs(rank):
    return [
        by_piece(2 * DK + DV),
        by_piece(DV),
        by_piece(rank),
        by_piece(1),
        pl.BlockSpec((1, 1, PIECE), lambda i: (i, 0, 0)),
        at_once((rank, DK)),
        at_once((1, DK)),
        at_once((1, DV)),
    ]


vmem_limit = 60 * 1024 * 1024


def core_forward(qkv, swish, low, segments, up, bias, gain):
    rows, rank = low.shape
    pieces = rows // PIECE
    return pl.pallas_call(
        core_forward_kernel,
        grid=(pieces,),
        in_specs=core_specs(rank),
        out_specs=[by_piece(DV), by_piece(PIECE), by_piece(DV)],
        out_shape=[
            jax.ShapeDtypeStruct((rows, DV), bf16),
            jax.ShapeDtypeStruct((rows, PIECE), bf16),
            jax.ShapeDtypeStruct((rows, DV), f32),
        ],
        compiler_params=pltpu.CompilerParams(vmem_limit_bytes=vmem_limit),
        cost_estimate=pl.CostEstimate(
            flops=pieces * 11 * 2 * PIECE**3 * 4, bytes_accessed=rows * 9216, transcendentals=pieces * 10 * PIECE**2
        ),
        name="core_forward",
    )(qkv, swish, low, segments[:, None], segments.reshape(pieces, 1, PIECE), up, bias, gain)


def core_backward(qkv, swish, low, segments, up, bias, gain, scores, mixed, d_gated):
    rows, rank = low.shape
    pieces = rows // PIECE
    return pl.pallas_call(
        core_backward_kernel,
        grid=(pieces,),
        in_specs=core_specs(rank) + [by_piece(PIECE), by_piece(DV), by_piece(DV)],
        out_specs=[
            by_piece(2 * DK + 2 * DV),
            by_piece(rank),
            at_once((rank, DK)),
            at_once((1, DK)),
            at_once((1, DV)),
        ],
        out_shape=[
            jax.ShapeDtypeStruct((rows, 2 * DK + 2 * DV), bf16),
            jax.ShapeDtypeStruct((rows, rank), f32),
            jax.ShapeDtypeStruct((rank, DK), f32),
            jax.ShapeDtypeStruct((1, DK), f32),
            jax.ShapeDtypeStruct((1, DV), f32),
        ],
        compiler_params=pltpu.CompilerParams(vmem_limit_bytes=vmem_limit),
        cost_estimate=pl.CostEstimate(
            flops=pieces * 30 * 2 * PIECE**3 * 4, bytes_accessed=rows * 12288, transcendentals=pieces * 12 * PIECE**2
        ),
        name="core_backward",
    )(
        qkv, swish, low, segments[:, None], segments.reshape(pieces, 1, PIECE), up, bias, gain,
        scores, mixed, d_gated,
    )


def on_device(
    tokens, segment_ids, cotangent, mixer_gain, w_query, w_key, w_value, w_swish, decay_down, decay_up,
    decay_bias, head_gain, w_output, dense_gain, w_gate, w_up, w_down,
):
    sizes = layout(lax.axis_size("dp"))
    tall, deep, far, _ = sizes
    core = lax.axis_index("tensor")
    place = lax.axis_index("dp")
    near = place % 2
    far_at = (place // 2) % far
    y_at = (place // (2 * far)) % deep
    z_at = place // (2 * far * deep)
    own_rows = tokens.shape[0]
    half_rows = own_rows // 2
    width = tokens.shape[1]
    block = width // lax.axis_size("dp")

    count = tall * deep * far
    slot = jnp.arange(count, dtype=jnp.int32)
    slot_z, slot_y, slot_far = slot % tall, (slot // tall) % deep, slot // (tall * deep)
    places = (((z_at - slot_z) % tall) * deep + (y_at - slot_y) % deep) * far + (far_at - slot_far) % far
    places = places.astype(jnp.int32)
    from_z, from_y, from_far = slot // (deep * far), (slot // far) % deep, slot % far
    back = (((far_at - from_far) % far) * deep + (y_at - from_y) % deep) * tall + (z_at - from_z) % tall
    back = back.astype(jnp.int32)

    def blocks_of(values, order):
        size = values.shape[0] // count
        return jnp.concatenate(
            [lax.dynamic_slice_in_dim(values, order[i] * size, size, 0) for i in range(count)], 0
        )

    def gathered(shards):
        own = jnp.concatenate([half(shard, near, 1) for shard in shards], 1)
        other = jnp.concatenate([half(shard, 1 - near, 1) for shard in shards], 1)
        pair = in_order(near, own, shift(other, sizes, 3, 1))
        parts = [pair]
        for axis in (0, 1, 2):
            parts = parts + [
                shift(part, sizes, axis, step) for step in range(1, sizes[axis]) for part in parts
            ]
        return jnp.concatenate(parts, 0)

    w_first = gathered((w_query, w_key, w_value, w_swish))
    w_out = gathered((w_output.T,))
    w_g = gathered((w_gate,))
    w_u = gathered((w_up,))
    w_d = gathered((w_down.T,))

    def scattered(left, right):
        return finish(start(left, right))

    def start(left, right):
        slab = tall * 2 * block
        outer = deep * far
        total = None
        got = []
        for number in reversed(range(1, outer)):
            back_far, back_y = number // deep, number % deep
            sent = mm_tn(left[:, number * slab : (number + 1) * slab], right).astype(bf16)
            if back_y:
                sent = shift(sent, sizes, 1, -back_y)
            if back_far:
                sent = shift(sent, sizes, 2, -back_far)
            got.append(sent)
        total = mm_tn(left[:, :slab], right)
        for one in got:
            total = total + one.astype(f32)
        return total.astype(bf16)

    def finish(total):
        rows = 2 * block
        kept = total[:rows].astype(f32)
        for step in range(1, tall):
            kept = kept + shift(total[step * rows : (step + 1) * rows], sizes, 0, -step).astype(f32)
        received = shift(half(kept, 1 - near).astype(bf16), sizes, 3, 1).astype(f32)
        return half(kept, near), received

    def columns(parts, begin, end):
        own, received = (part[:, begin:end] for part in parts)
        return jnp.where(
            near == 0, jnp.concatenate([own, received], 1), jnp.concatenate([received, own], 1)
        )

    def whole_chip(rows):
        return in_order(core, rows, core_swap(rows))

    def from_neighbour(rows):
        return whole_chip(shift(rows, sizes, 3, 1))

    def summed_rows(partial_next, partial_own):
        handed = core_swap(half(partial_next, 1 - core))
        ahead = (half(partial_next, core).astype(f32) + handed.astype(f32)).astype(bf16)
        ahead = shift(ahead, sizes, 3, 1)
        handed_own = core_swap(half(partial_own, 1 - core))
        return half(partial_own, core).astype(f32) + handed_own.astype(f32) + ahead.astype(f32)

    seg = jnp.concatenate([segment_ids, shift(segment_ids, sizes, 3, 1)], 0)
    tok_half = half(tokens, core)
    tok_own = reorder(tokens, places)
    tok_next = reorder(from_neighbour(tok_half), places)
    cot_own = reorder(cotangent, places)
    cot_next = reorder(from_neighbour(half(cotangent, core)), places)
    tok = jnp.concatenate([tok_own, tok_next], 0)
    cot = jnp.concatenate([cot_own, cot_next], 0)
    gain_first = blocks_of(mixer_gain.astype(f32), places)
    gain_second = blocks_of(dense_gain.astype(f32), places)
    down = blocks_of(decay_down, places)
    head = 2 * core + near
    up_own = lax.dynamic_slice_in_dim(decay_up, head * DK, DK, 1).astype(f32)
    bias_own = lax.dynamic_slice_in_dim(decay_bias, head * DK, DK, 0).astype(f32)[None]
    gain_heads = head_gain.astype(f32)[None]

    def root_of(values):
        return lax.rsqrt(jnp.mean(values * values, axis=-1, keepdims=True) + norm_eps)

    tok_f = tok.astype(f32)
    first = (tok_f * root_of(tok_f) * gain_first).astype(bf16)
    low = mm(first, down)
    qkv = mm(first, w_first[:, : 2 * DK + DV]).astype(bf16)
    swish = mm(first, w_first[:, 2 * DK + DV :])
    gated, scores, mixed = core_forward(qkv, swish, low, seg, up_own, bias_own, gain_heads)

    branch = summed_rows(
        mm_nt(gated[own_rows:], w_out).astype(bf16), mm_nt(gated[:own_rows], w_out).astype(bf16)
    )
    hidden = half(tok_own, core).astype(f32) + branch
    root_hidden = root_of(hidden)
    second_half = (hidden * root_hidden * gain_second).astype(bf16)
    second_own = whole_chip(second_half)
    second_next = from_neighbour(second_half)

    def dense(second, cot_part):
        gate = mm(second, w_g)
        upper = mm(second, w_u)
        sigma = jax.nn.sigmoid(gate)
        swished = gate * sigma
        product = (swished * upper).astype(bf16)
        d_product = mm(cot_part, w_d)
        d_gate = (d_product * upper * (sigma + gate * sigma * (1.0 - sigma))).astype(bf16)
        d_up = (d_product * swished).astype(bf16)
        return product, d_gate, d_up

    product_own, d_gate_own, d_up_own = dense(second_own, cot_own)
    product_next, d_gate_next, d_up_next = dense(second_next, cot_next)
    product = jnp.concatenate([product_own, product_next], 0)
    second = jnp.concatenate([second_own, second_next], 0)
    d_gate = jnp.concatenate([d_gate_own, d_gate_next], 0)
    d_up = jnp.concatenate([d_up_own, d_up_next], 0)
    sum_d = start(cot, product)
    sum_g = start(second, d_gate)
    sum_u = start(second, d_up)

    def d_second_of(rows_gate, rows_up):
        return (mm_nt(rows_gate, w_g) + mm_nt(rows_up, w_u)).astype(bf16)

    d_second = summed_rows(d_second_of(d_gate_next, d_up_next), d_second_of(d_gate_own, d_up_own))

    dense_out = summed_rows(mm_nt(product_next, w_d).astype(bf16), mm_nt(product_own, w_d).astype(bf16))
    output = reorder(whole_chip((hidden + dense_out).astype(bf16)), back)

    def norm_pull(values, root, gain, wanted):
        scaled = wanted * gain
        return root * scaled - values * (
            root * root * root * jnp.mean(values * scaled, axis=-1, keepdims=True)
        )

    d_hidden = half(cot_own, core).astype(f32) + norm_pull(hidden, root_hidden, gain_second, d_second)
    grad_dense_gain = jnp.sum(d_second * hidden * root_hidden, axis=0)
    d_branch_half = d_hidden.astype(bf16)
    d_branch = jnp.concatenate([whole_chip(d_branch_half), from_neighbour(d_branch_half)], 0)
    sum_o = start(d_branch, gated)
    d_gated = mm(d_branch, w_out)
    d_qkvs, d_low, grad_up, grad_bias, grad_head = core_backward(
        qkv, swish, low, seg, up_own, bias_own, gain_heads, scores, mixed, d_gated
    )
    sum_first = start(first, d_qkvs)
    down_f = down.astype(f32)

    def d_first_of(begin, end):
        return (
            mm_nt(d_qkvs[begin:end], w_first) + lax.dot_general(
                d_low[begin:end], down_f, (((1,), (1,)), ((), ())), precision=HIGH, preferred_element_type=f32
            )
        ).astype(bf16)

    d_first = summed_rows(d_first_of(own_rows, 2 * own_rows), d_first_of(0, own_rows))
    tok_mine = half(tok_own, core).astype(f32)
    root_mine = root_of(tok_mine)
    grad_half = d_hidden + norm_pull(tok_mine, root_mine, gain_first, d_first)
    grad_mixer_gain = jnp.sum(d_first * tok_mine * root_mine, axis=0)
    grad_tokens = reorder(whole_chip(grad_half), back)
    grad_down = lax.dot_general(
        first.astype(f32), d_low, (((0,), (0,)), ((), ())), precision=HIGH, preferred_element_type=f32
    )
    small = (
        blocks_of(grad_mixer_gain, back),
        blocks_of(grad_dense_gain, back),
        grad_head[0],
        blocks_of(grad_down, back),
        lax.dynamic_update_slice_in_dim(jnp.zeros(decay_up.shape, f32), grad_up, head * DK, 1),
        lax.dynamic_update_slice_in_dim(jnp.zeros(decay_bias.shape, f32), grad_bias[0], head * DK, 0),
    )
    small = lax.psum(small, ("dp", "tensor"))

    out_d, out_g, out_u = finish(sum_d), finish(sum_g), finish(sum_u)
    out_o, out_first = finish(sum_o), finish(sum_first)

    def all_of(parts):
        return columns(parts, 0, parts[0].shape[1])

    return (
        output,
        grad_tokens,
        small[0],
        columns(out_first, 0, DK),
        columns(out_first, DK, 2 * DK),
        columns(out_first, 2 * DK, 2 * DK + DV),
        columns(out_first, 2 * DK + DV, 2 * DK + 2 * DV),
        small[3],
        small[4],
        small[5],
        small[2],
        all_of(out_o).T,
        small[1],
        all_of(out_g),
        all_of(out_u),
        all_of(out_d).T,
    )


def solution(mesh):
    rows, large, turned, whole = P("dp", None), P("dp", "tensor"), P("tensor", "dp"), P()
    in_specs = (
        rows, P("dp"), rows, whole, large, large, large, large, whole, whole, whole, whole, turned,
        whole, large, large, turned,
    )
    out_specs = (
        rows, rows, whole, large, large, large, large, whole, whole, whole, whole, turned, whole,
        large, large, turned,
    )
    return jax.shard_map(on_device, mesh=mesh, in_specs=in_specs, out_specs=out_specs, check_vma=False)
```

time: 4890 us -> 1370 us (0.28)
  waiting for transfers between devices: 2710 us -> 709 us
  other arithmetic: 848 us -> 95.7 us
  local copies, waits for them, and re-layouts: 585 us -> 71.7 us
  matrix products: 641 us -> 233 us
  starting transfers between devices: 2 us -> 105 us
  Pallas kernels: 0 us -> 69.2 us
    reduce_scatter x8 -> x0, waiting for transfers between devices: 2100 us -> none  [the longest x1 483 us: on_device(): lax.psum_scatter(totals[6], 'dp', scatter_dimension=0, tiled=True)]
    ppermute x0 -> x90, waiting for transfers between devices: none -> 709 us  [the longest x74 709 us: shift(): return lax.ppermute(values, 'dp', shift_pairs(sizes, axis, step))]
    all_gather x8 -> x0, waiting for transfers between devices: 571 us -> none  [the longest x1 155 us: on_device(): lax.all_gather(shards[7], 'dp', axis=1, tiled=True)]
    reduce_sum x65 -> x4, other arithmetic: 444 us -> 11.5 us  [the longest x1 5.33 us: on_device(): grad_mixer_gain = jnp.sum(d_first * tok_mine * root_mine, axis=0)]
    dot_general x198 -> x33, matrix products: 641 us -> 233 us  [the longest x10 76.8 us: mm(): lax.dot_general(left, right, (((1,), (0,)), ((), ())), preferred_element_...]
    dynamic_update_slice x97 -> x0, other arithmetic: 291 us -> none  [the longest x96 291 us: gla_core(): lax.scan(span_step, state, (to_blocks(query, count), to_blocks(keyset, co...]
    another operation x77 -> x0, local copies, waits for them, and re-layouts: 172 us -> none
    dynamic_update_slice x84 -> x2, local copies, waits for them, and re-layouts: 159 us -> 0.26 us  [the longest x1 0.25 us: on_device(): lax.dynamic_update_slice_in_dim(jnp.zeros(decay_bias.shape, f32), grad_bi...]
  transfers between devices with their start and end apart: 20 -> 91, of which waited for: 15 -> 43; matrix products, arithmetic and copies ran while one was open for 24% -> 27% of each run, Pallas kernels for 0% -> 3%
where the time goes in v1:
time: 1370 us; the launch traced here: 1360 us
  waiting for transfers between devices  709 us (52%)
  matrix products  233 us (17%)
  starting transfers between devices  105 us (8%)
  other arithmetic  95.7 us (7%)
  local copies, waits for them, and re-layouts  71.7 us (5%)
  Pallas kernels  69.2 us (5%)
  blocking collectives  45.3 us (3%)
  between operations  27 us (2%)
    ppermute x74, waiting for transfers between devices, shift(): return lax.ppermute(values, 'dp', shift_pairs(sizes, axis, step))  709 us
    ppermute x74, starting transfers between devices, shift(): return lax.ppermute(values, 'dp', shift_pairs(sizes, axis, step))  104 us
    dot_general x10, matrix products, mm(): lax.dot_general(left, right, (((1,), (0,)), ((), ())), preferred_element_...  76.8 us
    dot_general x10, matrix products, mm_tn(): lax.dot_general(left, right, (((0,), (0,)), ((), ())), preferred_element_...  73 us
    dot_general x10, matrix products, mm_nt(): lax.dot_general(left, right, (((1,), (1,)), ((), ())), preferred_element_...  72 us
    psum x1, blocking collectives, on_device(): small = lax.psum(small, ('dp', 'tensor'))  45.3 us
    unnamed x288, local copies, waits for them, and re-layouts  40.6 us
    select_n x8, other arithmetic, in_order(): jnp.where(index == 0, jnp.concatenate([own, other], 0), jnp.concatenate([...  32.2 us
  transfers between devices with their start and end apart: 91, of which 43 were waited for; matrix products, arithmetic and copies ran while one was open for 27% of the time, Pallas kernels for 3%

profile of v1, /device:TPU:10, one launch (start us, length us, event | category | flops | bytes accessed | tf_op | source)
XLA Modules:
  0.0 1356.7 jit_solution(5539910832121766564)
XLA Ops:
  93.5 26.6 %collective-permute-done.14 = bf16[256,512]{0,1:T(8,128)(2,1)S(1)} collective-permute-done((bf16[256,512]{0,1:T(8,128)(2,1)S(1)}, bf16[256,512]{0,1:T(8,128)(2,1)S(1)}, u32[]{:S(2)}, u32[]{:S(2)}) %collective-permute-start.14) | collective-permute-done | bytes 262176 | tf_op jit(solution)/shard_map/ppermute | solution.py:36
  152.1 40.5 %collective-permute-done.26 = bf16[256,1408]{0,1:T(8,128)(2,1)S(1)} collective-permute-done((bf16[256,1408]{0,1:T(8,128)(2,1)S(1)}, bf16[256,1408]{0,1:T(8,128)(2,1)S(1)}, u32[]{:S(2)}, u32[]{:S(2)}) %collective-permute-start.26) | collective-permute-done | bytes 720928 | tf_op jit(solution)/shard_map/ppermute | solution.py:36
  196.7 21.2 %collective-permute-done.3 = bf16[256,1536]{1,0:T(8,128)(2,1)S(1)} collective-permute-done((bf16[256,1536]{1,0:T(8,128)(2,1)S(1)}, bf16[256,1536]{1,0:T(8,128)(2,1)S(1)}, u32[]{:S(2)}, u32[]{:S(2)}) %collective-permute-start.3) | collective-permute-done | bytes 786464 | tf_op jit(solution)/shard_map/ppermute | solution.py:36
  344.7 32.7 %collective-permute-done.41 = bf16[256,1408]{0,1:T(8,128)(2,1)S(1)} collective-permute-done((bf16[256,1408]{0,1:T(8,128)(2,1)}, bf16[256,1408]{0,1:T(8,128)(2,1)S(1)}, u32[]{:S(2)}, u32[]{:S(2)}) %collective-permute-start.41) | collective-permute-done | bytes 720928 | tf_op jit(solution)/shard_map/ppermute | solution.py:36
  381.6 14.9 %collective-permute-done.29 = bf16[256,1408]{0,1:T(8,128)(2,1)S(1)} collective-permute-done((bf16[256,1408]{0,1:T(8,128)(2,1)S(1)}, bf16[256,1408]{0,1:T(8,128)(2,1)S(1)}, u32[]{:S(2)}, u32[]{:S(2)}) %collective-permute-start.29) | collective-permute-done | bytes 720928 | tf_op jit(solution)/shard_map/ppermute | solution.py:36
  413.4 14.0 %collective-permute-done.36 = bf16[256,1408]{0,1:T(8,128)(2,1)S(1)} collective-permute-done((bf16[256,1408]{0,1:T(8,128)(2,1)S(1)}, bf16[256,1408]{0,1:T(8,128)(2,1)S(1)}, u32[]{:S(2)}, u32[]{:S(2)}) %collective-permute-start.36) | collective-permute-done | bytes 720928 | tf_op jit(solution)/shard_map/ppermute | solution.py:36
  443.8 14.5 %collective-permute-done.38 = bf16[256,1408]{0,1:T(8,128)(2,1)S(1)} collective-permute-done((bf16[256,1408]{0,1:T(8,128)(2,1)}, bf16[256,1408]{0,1:T(8,128)(2,1)S(1)}, u32[]{:S(2)}, u32[]{:S(2)}) %collective-permute-start.38) | collective-permute-done | bytes 720928 | tf_op jit(solution)/shard_map/ppermute | solution.py:36
  473.8 15.4 %collective-permute-done.45 = bf16[256,1408]{0,1:T(8,128)(2,1)S(1)} collective-permute-done((bf16[256,1408]{0,1:T(8,128)(2,1)S(1)}, bf16[256,1408]{0,1:T(8,128)(2,1)S(1)}, u32[]{:S(2)}, u32[]{:S(2)}) %collective-permute-start.45) | collective-permute-done | bytes 720928 | tf_op jit(solution)/shard_map/ppermute | solution.py:36
  660.2 22.7 %collective-permute-done.85 = bf16[1024,1408]{1,0:T(8,128)(2,1)} collective-permute-done((bf16[1024,1408]{1,0:T(8,128)(2,1)}, bf16[1024,1408]{1,0:T(8,128)(2,1)}, u32[]{:S(2)}, u32[]{:S(2)}) %collective-permute-start.85) | collective-permute-done | bytes 2883616 | tf_op jit(solution)/shard_map/ppermute | solution.py:36
  694.1 50.6 %collective-permute-done.80 = bf16[1024,1408]{1,0:T(8,128)(2,1)} collective-permute-done((bf16[1024,1408]{1,0:T(8,128)(2,1)}, bf16[1024,1408]{1,0:T(8,128)(2,1)}, u32[]{:S(2)}, u32[]{:S(2)}) %collective-permute-start.80) | collective-permute-done | bytes 2883616 | tf_op jit(solution)/shard_map/ppermute | solution.py:36
  755.8 50.3 %collective-permute-done.75 = bf16[1024,1408]{1,0:T(8,128)(2,1)} collective-permute-done((bf16[1024,1408]{1,0:T(8,128)(2,1)}, bf16[1024,1408]{1,0:T(8,128)(2,1)}, u32[]{:S(2)}, u32[]{:S(2)}) %collective-permute-start.75) | collective-permute-done | bytes 2883616 | tf_op jit(solution)/shard_map/ppermute | solution.py:36
  832.8 25.6 %collective-permute-done.87 = bf16[256,1408]{1,0:T(8,128)(2,1)S(1)} collective-permute-done((bf16[256,1408]{1,0:T(8,128)(2,1)}, bf16[256,1408]{1,0:T(8,128)(2,1)S(1)}, u32[]{:S(2)}, u32[]{:S(2)}) %collective-permute-start.87) | collective-permute-done | bytes 720928 | tf_op jit(solution)/shard_map/ppermute | solution.py:36
  858.4 15.8 %collective-permute-start.76 = (bf16[256,1408]{1,0:T(8,128)(2,1)S(1)}, bf16[256,1408]{1,0:T(8,128)(2,1)S(1)}, u32[]{:S(2)}, u32[]{:S(2)}) collective-permute-start(bf16[256,1408]{1,0:T(8,128)(2,1)S(1)} %get-tuple-element.105), channel_id=1, source_target_pairs={{0,24},{2,26},{4,28},{6,30},{8,0},{10,2},{12,4},{14,6},{16,8},{18,... | collective-permute-start | bytes 2162696 | tf_op jit(solution)/shard_map/ppermute | solution.py:36
  874.2 30.5 %collective-permute-done.88 = bf16[256,1408]{1,0:T(8,128)(2,1)S(1)} collective-permute-done((bf16[256,1408]{1,0:T(8,128)(2,1)}, bf16[256,1408]{1,0:T(8,128)(2,1)S(1)}, u32[]{:S(2)}, u32[]{:S(2)}) %collective-permute-start.88) | collective-permute-done | bytes 720928 | tf_op jit(solution)/shard_map/ppermute | solution.py:36
  919.0 31.0 %collective-permute-done.82 = bf16[256,1408]{1,0:T(8,128)(2,1)S(1)} collective-permute-done((bf16[256,1408]{1,0:T(8,128)(2,1)}, bf16[256,1408]{1,0:T(8,128)(2,1)S(1)}, u32[]{:S(2)}, u32[]{:S(2)}) %collective-permute-start.82) | collective-permute-done | bytes 720928 | tf_op jit(solution)/shard_map/ppermute | solution.py:36
  950.1 15.3 %collective-permute-done.83 = bf16[256,1408]{1,0:T(8,128)(2,1)S(1)} collective-permute-done((bf16[256,1408]{1,0:T(8,128)(2,1)S(1)}, bf16[256,1408]{1,0:T(8,128)(2,1)S(1)}, u32[]{:S(2)}, u32[]{:S(2)}) %collective-permute-start.83) | collective-permute-done | bytes 720928 | tf_op jit(solution)/shard_map/ppermute | solution.py:36
  982.2 14.0 %collective-permute-done.78 = bf16[256,1408]{1,0:T(8,128)(2,1)S(1)} collective-permute-done((bf16[256,1408]{1,0:T(8,128)(2,1)S(1)}, bf16[256,1408]{1,0:T(8,128)(2,1)S(1)}, u32[]{:S(2)}, u32[]{:S(2)}) %collective-permute-start.78) | collective-permute-done | bytes 720928 | tf_op jit(solution)/shard_map/ppermute | solution.py:36
  1056.8 23.5 %core_backward.1 = (bf16[1536,1536]{1,0:T(8,128)(2,1)}, f32[1536,16]{1,0:T(8,128)}, f32[16,256]{1,0:T(8,128)}, f32[1,256]{1,0:T(1,128)}, f32[1,512]{1,0:T(1,128)}) custom-call(bf16[1536,1024]{1,0:T(8,128)(2,1)} %fusion.6.qkv, f32[1536,512]{1,0:T(8,128)} %fusion.36.swish, f32[1536,16]{1,0:T(8,128)} %fusion.90.low, s32[1536,1]{1,0:T(8,128)} %broadcast_in_dim.38.seg_col, ...), custom_call_target="tpu_custom_call" | custom-call | flops 24159191040 | bytes 18874368 | tf_op jit(solution)/shard_map/core_backward/pallas_call | solution.py:271
  1129.3 15.4 %collective-permute-done.71 = bf16[256,512]{1,0:T(8,128)(2,1)S(1)} collective-permute-done((bf16[256,512]{1,0:T(8,128)(2,1)S(1)}, bf16[256,512]{1,0:T(8,128)(2,1)S(1)}, u32[]{:S(2)}, u32[]{:S(2)}) %collective-permute-start.71) | collective-permute-done | bytes 262176 | tf_op jit(solution)/shard_map/ppermute | solution.py:36
  1152.6 36.0 %collective-permute-done.74 = bf16[128,512]{1,0:T(8,128)(2,1)S(1)} collective-permute-done((bf16[128,512]{1,0:T(8,128)(2,1)S(1)}, bf16[128,512]{1,0:T(8,128)(2,1)S(1)}, u32[]{:S(2)}, u32[]{:S(2)}) %collective-permute-start.74) | collective-permute-done | bytes 131104 | tf_op jit(solution)/shard_map/ppermute | solution.py:36
  1215.1 15.9 %collective-permute-done.66 = bf16[256,1536]{1,0:T(8,128)(2,1)S(1)} collective-permute-done((bf16[256,1536]{1,0:T(8,128)(2,1)}, bf16[256,1536]{1,0:T(8,128)(2,1)S(1)}, u32[]{:S(2)}, u32[]{:S(2)}) %collective-permute-start.66) | collective-permute-done | bytes 786464 | tf_op jit(solution)/shard_map/ppermute | solution.py:36
  1231.0 32.2 %collective-permute-done.67 = bf16[256,1536]{1,0:T(8,128)(2,1)S(1)} collective-permute-done((bf16[256,1536]{1,0:T(8,128)(2,1)}, bf16[256,1536]{1,0:T(8,128)(2,1)S(1)}, u32[]{:S(2)}, u32[]{:S(2)}) %collective-permute-start.67) | collective-permute-done | bytes 786464 | tf_op jit(solution)/shard_map/ppermute | solution.py:36
  1263.1 16.8 %collective-permute-done.68 = bf16[256,1536]{1,0:T(8,128)(2,1)} collective-permute-done((bf16[256,1536]{1,0:T(8,128)(2,1)S(1)}, bf16[256,1536]{1,0:T(8,128)(2,1)}, u32[]{:S(2)}, u32[]{:S(2)}) %collective-permute-start.68) | collective-permute-done | bytes 786464 | tf_op jit(solution)/shard_map/ppermute | solution.py:36
  1283.4 45.3 %all-reduce = (f32[2048]{0:T(1024)}, f32[1024]{0:T(1024)}, f32[512]{0:T(512)}, f32[2048]{0:T(1024)}) all-reduce(f32[2048]{0:T(1024)S(1)} %constant_dynamic-update-slice_fusion.64, f32[1024]{0:T(1024)S(1)} %dynamic_update_slice.7, f32[512]{0:T(512)S(1)} %bitcast.87, ...), channel_id=1, replica_groups=mesh['dp'=16,'tensor'=2] {'dp','tensor'}, use_global_device_ids=true, to_apply=%region_6.7 | all-reduce | flops 5632 | bytes 45056 | tf_op jit(solution)/shard_map/psum | solution.py:503
  (611 shorter events, 709.1 us)
Async XLA Ops:
  7.2 1339.2 %all-reduce.4.cloned.1.call-start = ((), (), s32[]{:S(2)}) async-start(), calls=%async_computation | async-start | bytes 393216 | tf_op jit(solution)/shard_map/psum | solution.py:503
  11.5 110.7 %collective-permute-start.2 = (bf16[128,1536]{1,0:T(8,128)(2,1)}, bf16[128,1536]{1,0:T(8,128)(2,1)}, u32[]{:S(2)}, u32[]{:S(2)}) collective-permute-start(bf16[128,1536]{1,0:T(8,128)(2,1)} %pad_maximum_fusion.21), channel_id=1, source_target_pairs={{0,2},{2,0},{4,6},{6,4},{8,10},{10,8},{12,14},{14,12},{16,18},{18,... | collective-permute-start | bytes 1179656 | tf_op jit(solution)/shard_map/ppermute | solution.py:36
  129.3 90.2 %collective-permute-start = (bf16[384,2048]{1,0:T(8,128)(2,1)S(1)}, bf16[384,2048]{1,0:T(8,128)(2,1)S(1)}, u32[]{:S(2)}, u32[]{:S(2)}) collective-permute-start(bf16[384,2048]{1,0:T(8,128)(2,1)S(1)} %copy-done.28), channel_id=1, source_target_pairs={{0,2},{2,0},{4,6},{6,4},{8,10},{10,8},{12,14},{14,12},{16,18},{18,... | collective-permute-start | bytes 4718600 | tf_op jit(solution)/shard_map/ppermute | solution.py:36
  235.6 193.2 %collective-permute-start.54 = (bf16[384,2048]{1,0:T(8,128)(2,1)}, bf16[384,2048]{1,0:T(8,128)(2,1)}, u32[]{:S(2)}, u32[]{:S(2)}) collective-permute-start(bf16[384,2048]{1,0:T(8,128)(2,1)} %constant_dynamic-slice_fusion.8), channel_id=1, source_target_pairs={{0,2},{2,0},{4,6},{6,4},{8,10},{10,8},{12,14},{14,12},{16,18},{18,... | collective-permute-start | bytes 4718600 | tf_op jit(solution)/shard_map/ppermute | solution.py:36
  236.1 91.1 %collective-permute-start.33 = (bf16[256,1408]{0,1:T(8,128)(2,1)}, bf16[256,1408]{0,1:T(8,128)(2,1)}, u32[]{:S(2)}, u32[]{:S(2)}) collective-permute-start(bf16[256,1408]{0,1:T(8,128)(2,1)} %get-tuple-element.81), channel_id=1, source_target_pairs={{0,16},{2,18},{4,20},{6,22},{8,24},{10,26},{12,28},{14,30},{16,0},... | collective-permute-start | bytes 2162696 | tf_op jit(solution)/shard_map/ppermute | solution.py:36
  252.5 77.1 %collective-permute-start.34 = (bf16[256,1408]{0,1:T(8,128)(2,1)}, bf16[256,1408]{0,1:T(8,128)(2,1)}, u32[]{:S(2)}, u32[]{:S(2)}) collective-permute-start(bf16[256,1408]{0,1:T(8,128)(2,1)} %get-tuple-element.81), channel_id=1, source_target_pairs={{0,24},{2,26},{4,28},{6,30},{8,0},{10,2},{12,4},{14,6},{16,8},{18,... | collective-permute-start | bytes 2162696 | tf_op jit(solution)/shard_map/ppermute | solution.py:36
  430.9 72.4 %collective-permute-start.55 = (bf16[384,2048]{1,0:T(8,128)(2,1)}, bf16[384,2048]{1,0:T(8,128)(2,1)S(1)}, u32[]{:S(2)}, u32[]{:S(2)}) collective-permute-start(bf16[384,2048]{1,0:T(8,128)(2,1)} %collective-permute-done.54), channel_id=1, source_target_pairs={{0,1},{1,0},{2,3},{3,2},{4,5},{5,4},{6,7},{7,6},{8,9},{9,8},{10,11... | collective-permute-start | bytes 4718600 | tf_op jit(solution)/shard_map/ppermute | solution.py:40
  442.8 73.6 %collective-permute-start.22 = (bf16[384,2048]{1,0:T(8,128)(2,1)S(1)}, bf16[384,2048]{1,0:T(8,128)(2,1)S(1)}, u32[]{:S(2)}, u32[]{:S(2)}) collective-permute-start(bf16[384,2048]{1,0:T(8,128)(2,1)S(1)} %multiply_convert_fusion.6), channel_id=1, source_target_pairs={{0,1},{1,0},{2,3},{3,2},{4,5},{5,4},{6,7},{7,6},{8,9},{9,8},{10,11... | collective-permute-start | bytes 4718600 | tf_op jit(solution)/shard_map/ppermute | solution.py:40
  553.5 269.8 %collective-permute-start.47 = (bf16[384,2048]{1,0:T(8,128)(2,1)}, bf16[384,2048]{1,0:T(8,128)(2,1)S(1)}, u32[]{:S(2)}, u32[]{:S(2)}) collective-permute-start(bf16[384,2048]{1,0:T(8,128)(2,1)} %constant_dynamic-slice_fusion.11), channel_id=1, source_target_pairs={{0,1},{1,0},{2,3},{3,2},{4,5},{5,4},{6,7},{7,6},{8,9},{9,8},{10,11... | collective-permute-start | bytes 4718600 | tf_op jit(solution)/shard_map/ppermute | solution.py:40
  569.1 245.9 %collective-permute-start.53 = (bf16[384,2048]{1,0:T(8,128)(2,1)}, bf16[384,2048]{1,0:T(8,128)(2,1)S(1)}, u32[]{:S(2)}, u32[]{:S(2)}) collective-permute-start(bf16[384,2048]{1,0:T(8,128)(2,1)} %constant_dynamic-slice_fusion.9), channel_id=1, source_target_pairs={{0,1},{1,0},{2,3},{3,2},{4,5},{5,4},{6,7},{7,6},{8,9},{9,8},{10,11... | collective-permute-start | bytes 4718600 | tf_op jit(solution)/shard_map/ppermute | solution.py:40
  655.7 89.0 %collective-permute-start.80 = (bf16[1024,1408]{1,0:T(8,128)(2,1)}, bf16[1024,1408]{1,0:T(8,128)(2,1)}, u32[]{:S(2)}, u32[]{:S(2)}) collective-permute-start(bf16[1024,1408]{1,0:T(8,128)(2,1)} %convolution_convert_fusion.1), channel_id=1, source_target_pairs={{0,4},{2,6},{4,0},{6,2},{8,12},{10,14},{12,8},{14,10},{16,20},{18,... | collective-permute-start | bytes 8650760 | tf_op jit(solution)/shard_map/ppermute | solution.py:36
  657.2 148.9 %collective-permute-start.75 = (bf16[1024,1408]{1,0:T(8,128)(2,1)}, bf16[1024,1408]{1,0:T(8,128)(2,1)}, u32[]{:S(2)}, u32[]{:S(2)}) collective-permute-start(bf16[1024,1408]{1,0:T(8,128)(2,1)} %convolution_convert_fusion.2), channel_id=1, source_target_pairs={{0,4},{2,6},{4,0},{6,2},{8,12},{10,14},{12,8},{14,10},{16,20},{18,... | collective-permute-start | bytes 8650760 | tf_op jit(solution)/shard_map/ppermute | solution.py:36
  682.9 140.5 %collective-permute-start.51 = (bf16[384,2048]{1,0:T(8,128)(2,1)S(1)}, bf16[384,2048]{1,0:T(8,128)(2,1)}, u32[]{:S(2)}, u32[]{:S(2)}) collective-permute-start(bf16[384,2048]{1,0:T(8,128)(2,1)S(1)} %add_convert_fusion.11), channel_id=1, source_target_pairs={{0,2},{2,0},{4,6},{6,4},{8,10},{10,8},{12,14},{14,12},{16,18},{18,... | collective-permute-start | bytes 4718600 | tf_op jit(solution)/shard_map/ppermute | solution.py:36
  744.7 73.7 %collective-permute-start.57 = (bf16[384,2048]{1,0:T(8,128)(2,1)S(1)}, bf16[384,2048]{1,0:T(8,128)(2,1)S(1)}, u32[]{:S(2)}, u32[]{:S(2)}) collective-permute-start(bf16[384,2048]{1,0:T(8,128)(2,1)S(1)} %copy-done.27), channel_id=1, source_target_pairs={{0,2},{2,0},{4,6},{6,4},{8,10},{10,8},{12,14},{14,12},{16,18},{18,... | collective-permute-start | bytes 4718600 | tf_op jit(solution)/shard_map/ppermute | solution.py:36
  818.4 86.3 %collective-permute-start.88 = (bf16[256,1408]{1,0:T(8,128)(2,1)}, bf16[256,1408]{1,0:T(8,128)(2,1)S(1)}, u32[]{:S(2)}, u32[]{:S(2)}) collective-permute-start(bf16[256,1408]{1,0:T(8,128)(2,1)} %get-tuple-element.100), channel_id=1, source_target_pairs={{0,8},{2,10},{4,12},{6,14},{8,16},{10,18},{12,20},{14,22},{16,24},... | collective-permute-start | bytes 2162696 | tf_op jit(solution)/shard_map/ppermute | solution.py:36
  823.3 95.7 %collective-permute-start.81 = (bf16[256,1408]{1,0:T(8,128)(2,1)}, bf16[256,1408]{1,0:T(8,128)(2,1)S(1)}, u32[]{:S(2)}, u32[]{:S(2)}) collective-permute-start(bf16[256,1408]{1,0:T(8,128)(2,1)} %get-tuple-element.102), channel_id=1, source_target_pairs={{0,24},{2,26},{4,28},{6,30},{8,0},{10,2},{12,4},{14,6},{16,8},{18,... | collective-permute-start | bytes 2162696 | tf_op jit(solution)/shard_map/ppermute | solution.py:36
  824.5 125.6 %collective-permute-start.82 = (bf16[256,1408]{1,0:T(8,128)(2,1)}, bf16[256,1408]{1,0:T(8,128)(2,1)S(1)}, u32[]{:S(2)}, u32[]{:S(2)}) collective-permute-start(bf16[256,1408]{1,0:T(8,128)(2,1)} %get-tuple-element.104), channel_id=1, source_target_pairs={{0,16},{2,18},{4,20},{6,22},{8,24},{10,26},{12,28},{14,30},{16,0},... | collective-permute-start | bytes 2162696 | tf_op jit(solution)/shard_map/ppermute | solution.py:36
  830.9 134.6 %collective-permute-start.83 = (bf16[256,1408]{1,0:T(8,128)(2,1)S(1)}, bf16[256,1408]{1,0:T(8,128)(2,1)S(1)}, u32[]{:S(2)}, u32[]{:S(2)}) collective-permute-start(bf16[256,1408]{1,0:T(8,128)(2,1)S(1)} %copy-done.39), channel_id=1, source_target_pairs={{0,8},{2,10},{4,12},{6,14},{8,16},{10,18},{12,20},{14,22},{16,24},... | collective-permute-start | bytes 2162696 | tf_op jit(solution)/shard_map/ppermute | solution.py:36
  858.4 121.8 %collective-permute-start.76 = (bf16[256,1408]{1,0:T(8,128)(2,1)S(1)}, bf16[256,1408]{1,0:T(8,128)(2,1)S(1)}, u32[]{:S(2)}, u32[]{:S(2)}) collective-permute-start(bf16[256,1408]{1,0:T(8,128)(2,1)S(1)} %get-tuple-element.105), channel_id=1, source_target_pairs={{0,24},{2,26},{4,28},{6,30},{8,0},{10,2},{12,4},{14,6},{16,8},{18,... | collective-permute-start | bytes 2162696 | tf_op jit(solution)/shard_map/ppermute | solution.py:36
  904.7 76.2 %collective-permute-start.77 = (bf16[256,1408]{1,0:T(8,128)(2,1)S(1)}, bf16[256,1408]{1,0:T(8,128)(2,1)S(1)}, u32[]{:S(2)}, u32[]{:S(2)}) collective-permute-start(bf16[256,1408]{1,0:T(8,128)(2,1)S(1)} %get-tuple-element.107), channel_id=1, source_target_pairs={{0,16},{2,18},{4,20},{6,22},{8,24},{10,26},{12,28},{14,30},{16,0},... | collective-permute-start | bytes 2162696 | tf_op jit(solution)/shard_map/ppermute | solution.py:36
  919.0 77.2 %collective-permute-start.78 = (bf16[256,1408]{1,0:T(8,128)(2,1)S(1)}, bf16[256,1408]{1,0:T(8,128)(2,1)S(1)}, u32[]{:S(2)}, u32[]{:S(2)}) collective-permute-start(bf16[256,1408]{1,0:T(8,128)(2,1)S(1)} %get-tuple-element.106), channel_id=1, source_target_pairs={{0,8},{2,10},{4,12},{6,14},{8,16},{10,18},{12,20},{14,22},{16,24},... | collective-permute-start | bytes 2162696 | tf_op jit(solution)/shard_map/ppermute | solution.py:36
  950.1 90.1 %collective-permute-start.58 = (bf16[384,2048]{1,0:T(8,128)(2,1)}, bf16[384,2048]{1,0:T(8,128)(2,1)}, u32[]{:S(2)}, u32[]{:S(2)}) collective-permute-start(bf16[384,2048]{1,0:T(8,128)(2,1)} %get-tuple-element.74), channel_id=1, source_target_pairs={{0,1},{1,0},{2,3},{3,2},{4,5},{5,4},{6,7},{7,6},{8,9},{9,8},{10,11... | collective-permute-start | bytes 4718600 | tf_op jit(solution)/shard_map/ppermute | solution.py:40
  1098.6 90.1 %collective-permute-start.65 = (bf16[1024,1536]{1,0:T(8,128)(2,1)}, bf16[1024,1536]{1,0:T(8,128)(2,1)}, u32[]{:S(2)}, u32[]{:S(2)}) collective-permute-start(bf16[1024,1536]{1,0:T(8,128)(2,1)} %convolution_convert_fusion.3), channel_id=1, source_target_pairs={{0,4},{2,6},{4,0},{6,2},{8,12},{10,14},{12,8},{14,10},{16,20},{18,... | collective-permute-start | bytes 9437192 | tf_op jit(solution)/shard_map/ppermute | solution.py:36
  1208.2 123.9 %collective-permute-start.64 = (f32[384,2048]{1,0:T(8,128)}, f32[384,2048]{1,0:T(8,128)}, u32[]{:S(2)}, u32[]{:S(2)}) collective-permute-start(f32[384,2048]{1,0:T(8,128)} %fusion.14), channel_id=1, source_target_pairs={{0,1},{1,0},{2,3},{3,2},{4,5},{5,4},{6,7},{7,6},{8,9},{9,8},{10,11... | collective-permute-start | bytes 9437192 | tf_op jit(solution)/shard_map/ppermute | solution.py:40
  (171 other events, 5022.4 us)
Sparse Core Ops, SparseCore 0:
  1151.5 159.0 all-reduce.3

commit v2 on v1

v2 whole, which is shorter than its diff:
```python
from functools import partial

import jax
import jax.numpy as jnp
import numpy as np
from jax import lax
from jax.experimental import pallas as pl
from jax.experimental.pallas import tpu as pltpu
from jax.sharding import PartitionSpec as P

DK = 256
DV = 512
PIECE = 256
norm_eps = 1e-06
head_eps = 1e-05
LEVELS = (1, 2, 4, 8, 16, 32, 64, 128)
f32 = jnp.float32
bf16 = jnp.bfloat16
HIGH = lax.Precision.HIGHEST


def layout(chips):
    return {16: (4, 2, 1, 2), 64: (4, 4, 2, 2)}.get(chips, (1, 1, chips // 2, 2))


def split_place(place, sizes):
    _, deep, far, _ = sizes
    near = lax.rem(place, np.int32(2))
    far_at = lax.rem(lax.div(place, np.int32(2)), np.int32(far))
    y_at = lax.rem(lax.div(place, np.int32(2 * far)), np.int32(deep))
    return lax.div(place, np.int32(2 * far * deep)), y_at, far_at, near


def shift_pairs(sizes, axis, step):
    pairs = []
    for place in range(int(np.prod(sizes))):
        at = list(np.unravel_index(place, sizes))
        at[axis] = (at[axis] + step) % sizes[axis]
        pairs.append((place, int(np.ravel_multi_index(at, sizes))))
    return pairs


def exchange_pairs(sizes, axis, reach):
    pairs = []
    for place in range(int(np.prod(sizes))):
        at = list(np.unravel_index(place, sizes))
        at[axis] ^= reach
        pairs.append((place, int(np.ravel_multi_index(at, sizes))))
    return pairs


def shift(values, sizes, axis, step):
    return lax.ppermute(values, "dp", shift_pairs(sizes, axis, step))


def hop_pairs(sizes, axis, step, distance):
    pairs = []
    for place in range(int(np.prod(sizes))):
        at = list(np.unravel_index(place, sizes))
        behind = at[axis] if step > 0 else sizes[axis] - 1 - at[axis]
        at[axis] += step
        if behind >= distance - 1 and 0 <= at[axis] < sizes[axis]:
            pairs.append((place, int(np.ravel_multi_index(at, sizes))))
    return pairs


def reach_pairs(sizes, axis, step, reach):
    pairs = []
    for place in range(int(np.prod(sizes))):
        at = list(np.unravel_index(place, sizes))
        if 0 <= at[axis] + step * reach < sizes[axis]:
            at[axis] += step
            pairs.append((place, int(np.ravel_multi_index(at, sizes))))
    return pairs


class Link:
    def __init__(self, window):
        self.window, self.landed = window, []

    def send(self, move, values, *others):
        earlier = self.landed[-self.window :][:1] if len(self.landed) >= self.window else []
        ties = tuple(others) + tuple(earlier)
        landed = move(after(values, *ties) if ties else values)
        self.landed.append(landed)
        return landed


def after(values, *others):
    return lax.optimization_barrier((values,) + tuple(jax.tree.leaves(others)))[0]


def core_swap(values):
    return lax.ppermute(values, "tensor", [(0, 1), (1, 0)])


def in_order(index, own, other):
    return jnp.where(
        index == 0, jnp.concatenate([own, other], 0), jnp.concatenate([other, own], 0)
    )


def half(values, index, axis=0):
    size = values.shape[axis] // 2
    return lax.dynamic_slice_in_dim(values, index * size, size, axis)


def mm(left, right):
    return lax.dot_general(left, right, (((1,), (0,)), ((), ())), preferred_element_type=f32)


def mm_nt(left, right):
    return lax.dot_general(left, right, (((1,), (1,)), ((), ())), preferred_element_type=f32)


def mm_tn(left, right):
    return lax.dot_general(left, right, (((0,), (0,)), ((), ())), preferred_element_type=f32)


def reorder_kernel(places, source, target):
    count = places.shape[0]
    width = source.shape[1] // count
    for block in range(count):
        start = pl.multiple_of(places[block] * width, width)
        target[:, block * width : (block + 1) * width] = source[:, pl.ds(start, width)]


def reorder(values, places):
    rows, columns = values.shape
    count = places.shape[0]
    width = columns // count
    if width % 128 != 0:
        return jnp.concatenate(
            [lax.dynamic_slice_in_dim(values, places[i] * width, width, 1) for i in range(count)], 1
        )
    tile = 192 if rows % 192 == 0 else rows
    return pl.pallas_call(
        reorder_kernel,
        out_shape=jax.ShapeDtypeStruct(values.shape, values.dtype),
        grid_spec=pltpu.PrefetchScalarGridSpec(
            num_scalar_prefetch=1,
            grid=(rows // tile,),
            in_specs=[pl.BlockSpec((tile, columns), lambda i, p: (i, 0))],
            out_specs=pl.BlockSpec((tile, columns), lambda i, p: (i, 0)),
        ),
        cost_estimate=pl.CostEstimate(
            flops=0, bytes_accessed=2 * values.size * values.dtype.itemsize, transcendentals=0
        ),
        name="reorder",
    )(places, values)


def bit_of(shape, level):
    return (lax.broadcasted_iota(jnp.int32, shape, 0) & level) != 0


def partner(values, level, upper):
    size = values.shape[0]
    return jnp.where(
        upper, pltpu.roll(values, level, 0), pltpu.roll(values, size - level, 0)
    )


def log_decay(low, up, bias):
    pre = jnp.dot(low, up, precision=HIGH, preferred_element_type=f32) + bias
    return pre, (jnp.minimum(pre, 0.0) - jnp.log1p(jnp.exp(-jnp.abs(pre)))) * (1.0 / 16.0)


def level_exponents(decay):
    prefix, suffix, total = decay, jnp.zeros_like(decay), decay
    found = []
    for level in LEVELS:
        upper = bit_of(decay.shape, level)
        found.append(jnp.where(upper, prefix, suffix))
        if level != LEVELS[-1]:
            beside = partner(total, level, upper)
            prefix = prefix + jnp.where(upper, beside, 0.0)
            suffix = suffix + jnp.where(upper, 0.0, beside)
            total = total + beside
    return found


def pair_distance():
    rows = lax.broadcasted_iota(jnp.int32, (PIECE, PIECE), 0)
    columns = lax.broadcasted_iota(jnp.int32, (PIECE, PIECE), 1)
    return rows ^ columns, rows >= columns


def fixed(shape):
    return pl.BlockSpec(shape, lambda i: (0,) * len(shape), pipeline_mode=pl.Buffered(1))


def by_rows(tile, width):
    return pl.BlockSpec((tile, width), lambda i: (i, 0))


def shape_of(rows, width, kind):
    return jax.ShapeDtypeStruct((rows, width), kind)


vmem_limit = 60 * 1024 * 1024


def call(kernel, name, grid, in_specs, out_specs, out_shape):
    return pl.pallas_call(
        kernel,
        grid=grid,
        in_specs=in_specs,
        out_specs=out_specs,
        out_shape=out_shape,
        compiler_params=pltpu.CompilerParams(vmem_limit_bytes=vmem_limit),
        cost_estimate=pl.CostEstimate(flops=1, bytes_accessed=1, transcendentals=0),
        name=name,
    )


def piece_attention(query_low, keyset_low, decay):
    query, keyset = query_low.astype(f32), keyset_low.astype(f32)
    apart, causal = pair_distance()
    scores = mm_nt(query_low, keyset_low)
    for level, exponent in zip(LEVELS, level_exponents(decay)):
        upper = bit_of(decay.shape, level)
        scaled = (jnp.where(upper, query, keyset) * jnp.exp(exponent)).astype(bf16)
        scores = jnp.where(apart >= level, mm_nt(scaled, scaled), scores)
    return scores, causal


def mixer_forward_kernel(
    tok, w_first, down, gain_first, seg_col, seg_row, up, bias, gain,
    first_out, low_out, qkv_out, swish_out, scores_out, mixed_out, gated_out,
):
    rows = tok[...].astype(f32)
    root_rows = lax.rsqrt(jnp.mean(rows * rows, axis=-1, keepdims=True) + norm_eps)
    first = (rows * root_rows * gain_first[...]).astype(bf16)
    first_out[...] = first
    low = mm(first, down[...])
    low_out[...] = low
    qkv = mm(first, w_first[:, : 2 * DK + DV]).astype(bf16)
    qkv_out[...] = qkv
    opened = mm(first, w_first[:, 2 * DK + DV :])
    swish_out[...] = opened
    _, decay = log_decay(low, up[...], bias[...])
    scores, causal = piece_attention(qkv[:, :DK], qkv[:, DK : 2 * DK], decay)
    allowed = causal & (seg_col[...] == seg_row[0])
    scores = jnp.where(allowed, scores * (DK**-0.5), 0.0).astype(bf16)
    mixed = mm(scores, qkv[:, 2 * DK :])
    scores_out[...] = scores
    mixed_out[...] = mixed
    root = lax.rsqrt(jnp.mean(mixed * mixed, axis=-1, keepdims=True) + head_eps)
    gated_out[...] = (mixed * root * gain[...] * (opened * jax.nn.sigmoid(opened))).astype(bf16)


def mixer_forward(tok, w_first, down, gain_first, segments, up, bias, gain):
    rows, width = tok.shape
    rank = down.shape[1]
    pieces = rows // PIECE
    return call(
        mixer_forward_kernel, "mixer_forward", (pieces,),
        [
            by_rows(PIECE, width), fixed(w_first.shape), fixed(down.shape), fixed((1, width)),
            by_rows(PIECE, 1), pl.BlockSpec((1, 1, PIECE), lambda i: (i, 0, 0)),
            fixed(up.shape), fixed(bias.shape), fixed(gain.shape),
        ],
        [
            by_rows(PIECE, width), by_rows(PIECE, rank), by_rows(PIECE, 2 * DK + DV), by_rows(PIECE, DV),
            by_rows(PIECE, PIECE), by_rows(PIECE, DV), by_rows(PIECE, DV),
        ],
        [
            shape_of(rows, width, bf16), shape_of(rows, rank, f32), shape_of(rows, 2 * DK + DV, bf16),
            shape_of(rows, DV, f32), shape_of(rows, PIECE, bf16), shape_of(rows, DV, f32), shape_of(rows, DV, bf16),
        ],
    )(tok, w_first, down, gain_first, segments[:, None], segments.reshape(pieces, 1, PIECE), up, bias, gain)


def product_nt_kernel(left, right, out):
    out[...] = mm_nt(left[...], right[...]).astype(bf16)


def product_nt(left, right):
    rows, width = left.shape[0], right.shape[0]
    return call(
        product_nt_kernel, "product_nt", (rows // 256,),
        [by_rows(256, left.shape[1]), fixed(right.shape)], by_rows(256, width), shape_of(rows, width, bf16),
    )(left, right)


def mixer_backward_kernel(
    d_branch, w_out, w_first, down, qkv, swish, low, seg_col, seg_row, up, bias, gain, scores_in, mixed_in,
    d_qkvs, d_low_out, d_first, d_up, d_bias, d_gain,
):
    query = qkv[:, :DK].astype(f32)
    keyset = qkv[:, DK : 2 * DK].astype(f32)
    values = qkv[:, 2 * DK :]
    pre, decay = log_decay(low[...], up[...], bias[...])
    apart, causal = pair_distance()
    mixed = mixed_in[...]
    root = lax.rsqrt(jnp.mean(mixed * mixed, axis=-1, keepdims=True) + head_eps)
    normed = mixed * root
    opened = swish[...]
    sigma = jax.nn.sigmoid(opened)
    wanted = mm(d_branch[...], w_out[...])
    d_swish = (wanted * normed * gain[...] * (sigma + opened * sigma * (1.0 - sigma))).astype(bf16)
    d_scaled = wanted * (opened * sigma)
    gain_part = jnp.sum(d_scaled * normed, axis=0, keepdims=True)
    d_normed = d_scaled * gain[...]
    d_mixed = root * (d_normed - normed * jnp.mean(d_normed * normed, axis=-1, keepdims=True))
    d_mixed = d_mixed.astype(bf16)
    d_values = mm_tn(scores_in[...], d_mixed).astype(bf16)
    allowed = causal & (seg_col[...] == seg_row[0])
    d_scores = jnp.where(allowed, mm_nt(d_mixed, values) * (DK**-0.5), 0.0)
    on_diagonal = jnp.sum(jnp.where(apart == 0, d_scores, 0.0), axis=1, keepdims=True)
    d_query = on_diagonal * keyset
    d_keyset = on_diagonal * query
    both = d_scores + d_scores.T
    exponents = level_exponents(decay)
    d_prefix = d_suffix = d_total = jnp.zeros_like(decay)
    for level, exponent in reversed(list(zip(LEVELS, exponents))):
        upper = bit_of(decay.shape, level)
        if level != LEVELS[-1]:
            d_beside = jnp.where(upper, d_prefix, d_suffix) + d_total
            d_total = d_total + partner(d_beside, level, upper)
        base = jnp.where(upper, query, keyset)
        factor = jnp.exp(exponent)
        scaled = (base * factor).astype(bf16)
        here = jnp.where((apart >= level) & (apart < 2 * level), both, 0.0).astype(bf16)
        d_base = mm(here, scaled) * factor
        d_exponent = d_base * base
        d_query = d_query + jnp.where(upper, d_base, 0.0)
        d_keyset = d_keyset + jnp.where(upper, 0.0, d_base)
        d_prefix = d_prefix + jnp.where(upper, d_exponent, 0.0)
        d_suffix = d_suffix + jnp.where(upper, 0.0, d_exponent)
    d_pre = (d_prefix + d_total) * jax.nn.sigmoid(-pre) * (1.0 / 16.0)
    d_query, d_keyset = d_query.astype(bf16), d_keyset.astype(bf16)
    d_qkvs[:, :DK] = d_query
    d_qkvs[:, DK : 2 * DK] = d_keyset
    d_qkvs[:, 2 * DK : 2 * DK + DV] = d_values
    d_qkvs[:, 2 * DK + DV :] = d_swish
    d_low = lax.dot_general(
        d_pre, up[...], (((1,), (1,)), ((), ())), precision=HIGH, preferred_element_type=f32
    )
    d_low_out[...] = d_low
    d_first[...] = (
        mm_nt(d_query, w_first[:, :DK])
        + mm_nt(d_keyset, w_first[:, DK : 2 * DK])
        + mm_nt(d_values, w_first[:, 2 * DK : 2 * DK + DV])
        + mm_nt(d_swish, w_first[:, 2 * DK + DV :])
        + lax.dot_general(
            d_low, down[...].astype(f32), (((1,), (1,)), ((), ())), precision=HIGH, preferred_element_type=f32
        )
    ).astype(bf16)

    @pl.when(pl.program_id(0) == 0)
    def _():
        d_up[...] = jnp.zeros_like(d_up)
        d_bias[...] = jnp.zeros_like(d_bias)
        d_gain[...] = jnp.zeros_like(d_gain)

    d_up[...] += lax.dot_general(
        low[...], d_pre, (((0,), (0,)), ((), ())), precision=HIGH, preferred_element_type=f32
    )
    d_bias[...] += jnp.sum(d_pre, axis=0, keepdims=True)
    d_gain[...] += gain_part


def at_once(shape):
    return pl.BlockSpec(shape, lambda i: (0,) * len(shape))


def mixer_backward(d_branch, w_out, w_first, down, qkv, swish, low, segments, up, bias, gain, scores, mixed):
    rows, width = d_branch.shape
    rank = low.shape[1]
    pieces = rows // PIECE
    return call(
        mixer_backward_kernel, "mixer_backward", (pieces,),
        [
            by_rows(PIECE, width), fixed(w_out.shape), fixed(w_first.shape), fixed(down.shape),
            by_rows(PIECE, 2 * DK + DV), by_rows(PIECE, DV), by_rows(PIECE, rank), by_rows(PIECE, 1),
            pl.BlockSpec((1, 1, PIECE), lambda i: (i, 0, 0)), fixed(up.shape), fixed(bias.shape), fixed(gain.shape),
            by_rows(PIECE, PIECE), by_rows(PIECE, DV),
        ],
        [
            by_rows(PIECE, 2 * DK + 2 * DV), by_rows(PIECE, rank), by_rows(PIECE, width),
            at_once((rank, DK)), at_once((1, DK)), at_once((1, DV)),
        ],
        [
            shape_of(rows, 2 * DK + 2 * DV, bf16), shape_of(rows, rank, f32), shape_of(rows, width, bf16),
            shape_of(rank, DK, f32), shape_of(1, DK, f32), shape_of(1, DV, f32),
        ],
    )(
        d_branch, w_out, w_first, down, qkv, swish, low, segments[:, None], segments.reshape(pieces, 1, PIECE),
        up, bias, gain, scores, mixed,
    )


def dense_forward_kernel(second, w_g, w_u, gate_out, upper_out, product_out):
    gate = mm(second[...], w_g[...])
    gate_out[...] = gate
    upper = mm(second[...], w_u[...])
    upper_out[...] = upper
    product_out[...] = (gate * jax.nn.sigmoid(gate) * upper).astype(bf16)


def dense_forward(second, w_g, w_u):
    rows, width = second.shape
    units = w_g.shape[1]
    return call(
        dense_forward_kernel, "dense_forward", (rows // 256,),
        [by_rows(256, width), fixed(w_g.shape), fixed(w_u.shape)], [by_rows(256, units)] * 3,
        [shape_of(rows, units, f32), shape_of(rows, units, f32), shape_of(rows, units, bf16)],
    )(second, w_g, w_u)


def dense_backward_kernel(cot, w_d, w_g, w_u, gate_in, upper_in, d_gate_out, d_up_out, d_second):
    gate = gate_in[...]
    sigma = jax.nn.sigmoid(gate)
    d_product = mm(cot[...], w_d[...])
    d_gate = (d_product * upper_in[...] * (sigma + gate * sigma * (1.0 - sigma))).astype(bf16)
    d_up = (d_product * (gate * sigma)).astype(bf16)
    d_gate_out[...] = d_gate
    d_up_out[...] = d_up
    d_second[...] = (mm_nt(d_gate, w_g[...]) + mm_nt(d_up, w_u[...])).astype(bf16)


def dense_backward(cot, w_d, w_g, w_u, gate, upper):
    rows, width = cot.shape
    units = w_g.shape[1]
    return call(
        dense_backward_kernel, "dense_backward", (rows // 256,),
        [by_rows(256, width), fixed(w_d.shape), fixed(w_g.shape), fixed(w_u.shape)] + [by_rows(256, units)] * 2,
        [by_rows(256, units), by_rows(256, units), by_rows(256, width)],
        [shape_of(rows, units, bf16), shape_of(rows, units, bf16), shape_of(rows, width, bf16)],
    )(cot, w_d, w_g, w_u, gate, upper)


def slab_kernel(others, left_own, left_next, right_own, right_next, *rest):
    total = mm_tn(left_own[...], right_own[...]) + mm_tn(left_next[...], right_next[...])
    for other in rest[:others]:
        total = total + other[...].astype(f32)
    rest[others][...] = total.astype(bf16)


def slab_gradient(left, right, begin, rows, received):
    count, width = right[0].shape
    tile = 256 if rows % 256 == 0 else 128
    at = begin // tile
    column_block = pl.BlockSpec((count, tile), lambda i: (0, at + i))
    return call(
        partial(slab_kernel, len(received)), "slab_gradient", (rows // tile,),
        [column_block] * 2 + [fixed((count, width))] * 2 + [by_rows(tile, width)] * len(received),
        by_rows(tile, width), shape_of(rows, width, bf16),
    )(*left, *right, *received)


def opening_kernel(sizes, counts, *refs):
    groups, full, row_count = counts
    tall, deep, far, _ = sizes
    refs = list(refs)
    owns, others = refs[:groups], refs[groups : 2 * groups]
    rows_in = refs[2 * groups : 2 * groups + row_count]
    seg_in = refs[2 * groups + row_count]
    outs = refs[2 * groups + row_count + 1 :]
    weights, rows_out, seg_out = outs[:groups], outs[groups : groups + row_count], outs[groups + row_count]
    local_sem, x_sem, z_sem, y_sem, row_sem, core_sem, seg_sem = outs[groups + row_count + 1 :]

    place, core = lax.axis_index("dp"), lax.axis_index("tensor")
    near = place % 2
    far_at = (place // 2) % far
    y_at = (place // (2 * far)) % deep
    z_at = place // (2 * far * deep)

    def device(z, y, far_x, near_x, which):
        return (((z * deep + y) * far + far_x) * 2 + near_x, which)

    beside = device(z_at, y_at, far_at, 1 - near, core)
    other_core = device(z_at, y_at, far_at, near, 1 - core)
    above = device(z_at + 1, y_at, far_at, near, core)
    below = device(z_at - 1, y_at, far_at, near, core)
    has_above, has_below = z_at + 1 < tall, z_at >= 1
    shifts = [(fr, yr) for fr in range(far) for yr in range(deep) if fr or yr]
    peers = [device(z_at, (y_at + yr) % deep, (far_at + fr) % far, near, core) for fr, yr in shifts]

    barrier = pltpu.get_barrier_semaphore()

    def greet(who):
        pl.semaphore_signal(barrier, inc=1, device_id=who, device_id_type=pl.DeviceIdType.MESH)

    greet(beside)
    greet(other_core)
    for peer in peers:
        greet(peer)
    pl.when(has_above)(lambda: greet(above))
    pl.when(has_below)(lambda: greet(below))
    along = has_above.astype(jnp.int32) + has_below.astype(jnp.int32)
    pl.semaphore_wait(barrier, 2 + len(peers) + along)

    def remote(source, target, sems, index, who):
        return pltpu.make_async_remote_copy(
            src_ref=source, dst_ref=target, send_sem=sems.at[(0,) + index], recv_sem=sems.at[(1,) + index],
            device_id=who, device_id_type=pl.DeviceIdType.MESH,
        )

    block = owns[0].shape[0]
    size = 2 * block

    def slab(group, number, back):
        return weights[group].at[pl.ds((number * tall + back) * size, size)]

    def own_part(group):
        return weights[group].at[pl.ds(pl.multiple_of(near * block, block), block)]

    def local(group):
        return pltpu.make_async_copy(owns[group], own_part(group), local_sem.at[group])

    def crossing(group):
        return remote(others[group], own_part(group), x_sem, (group,), beside)

    def rising(group, hop):
        return remote(slab(group, 0, hop - 1), slab(group, 0, hop), z_sem, (group, 0, hop - 1), above)

    def falling(group, hop):
        return remote(
            slab(group, 0, (tall - hop + 1) % tall), slab(group, 0, tall - hop), z_sem, (group, 1, hop - 1), below
        )

    def sideways(group, number, back):
        return remote(
            slab(group, 0, back), slab(group, number + 1, back), y_sem, (group, number, back), peers[number]
        )

    half_rows = rows_in[0].shape[0]

    def mine(array):
        return rows_out[array].at[pl.ds(pl.multiple_of(core * half_rows, half_rows), half_rows)]

    def rows_crossing(array):
        return remote(rows_in[array], mine(array), row_sem, (array,), beside)

    def rows_sharing(array):
        return remote(mine(array), mine(array), core_sem, (array,), other_core)

    def seg_crossing():
        return remote(seg_in, seg_out, seg_sem, (0,), beside)

    def spread(group, back):
        for number in range(len(peers)):
            sideways(group, number, back).start()

    def step_z(group, hop):
        @pl.when(z_at >= hop)
        def _():
            rising(group, hop).wait_recv()

        if hop + 1 < tall:
            @pl.when((z_at >= hop) & has_above)
            def _():
                rising(group, hop + 1).start()

        @pl.when(z_at + hop < tall)
        def _():
            falling(group, hop).wait_recv()

        if hop + 1 < tall:
            @pl.when((z_at + hop < tall) & has_below)
            def _():
                falling(group, hop + 1).start()

        @pl.when(z_at >= hop)
        def _():
            spread(group, hop)

        @pl.when(z_at + hop < tall)
        def _():
            spread(group, tall - hop)

    def arrive(group):
        local(group).wait()
        crossing(group).wait_recv()

    def first_hop(group):
        pl.when(has_above)(lambda: rising(group, 1).start())
        pl.when(has_below)(lambda: falling(group, 1).start())

    crossing(0).start()
    for group in range(groups):
        local(group).start()
    arrive(0)
    first_hop(0)
    spread(0, 0)
    for group in range(1, groups):
        crossing(group).start()
    seg_crossing().start()
    for array in range(row_count):
        rows_crossing(array).start()
    for group in range(1, full):
        arrive(group)
        spread(group, 0)
    for hop in range(1, tall):
        step_z(0, hop)
        if hop == tall - 2 or tall == 2:
            for group in range(1, full):
                first_hop(group)
    for group in range(1, full):
        for hop in range(1, tall):
            step_z(group, hop)
    for array in range(row_count):
        rows_crossing(array).wait_recv()
        rows_sharing(array).start()
    for group in range(full, groups):
        arrive(group)
    for group in range(full):
        for number in range(len(peers)):
            for back in range(tall):
                sideways(group, number, back).wait()
        for hop in range(1, tall):
            pl.when((z_at >= hop - 1) & has_above)(lambda hop=hop: rising(group, hop).wait_send())
            pl.when((z_at + hop - 1 < tall) & has_below)(lambda hop=hop: falling(group, hop).wait_send())
    for group in range(groups):
        crossing(group).wait_send()
    for array in range(row_count):
        rows_crossing(array).wait_send()
        rows_sharing(array).wait()
    seg_crossing().wait()


def opening(sizes, full, owns, others, rows, segments):
    tall, deep, far, _ = sizes
    groups, row_count = len(owns), len(rows)
    block = owns[0].shape[0]
    blocks = tall * deep * far
    anywhere = pl.BlockSpec(memory_space=pl.ANY)
    seg = segments.reshape(-1, 128)
    outs = [
        shape_of(2 * block * (blocks if group < full else 1), own.shape[1], bf16) for group, own in enumerate(owns)
    ]
    outs += [shape_of(2 * one.shape[0], one.shape[1], bf16) for one in rows] + [shape_of(*seg.shape, jnp.int32)]
    dma = pltpu.SemaphoreType.DMA
    peers = deep * far - 1
    results = pl.pallas_call(
        partial(opening_kernel, sizes, (groups, full, row_count)),
        in_specs=[anywhere] * (2 * groups + row_count + 1),
        out_specs=[anywhere] * len(outs),
        out_shape=outs,
        scratch_shapes=[
            dma((groups,)), dma((2, groups)), dma((2, full, 2, tall - 1)), dma((2, full, peers, tall)),
            dma((2, row_count)), dma((2, row_count)), dma((2, 1)),
        ],
        compiler_params=pltpu.CompilerParams(
            collective_id=0, has_side_effects=True, vmem_limit_bytes=vmem_limit
        ),
        cost_estimate=pl.CostEstimate(flops=1, bytes_accessed=1, transcendentals=0),
        name="opening",
    )(*owns, *others, *rows, seg)
    return results[:groups], results[groups : groups + row_count], results[-1].reshape(-1)


def on_device(
    tokens, segment_ids, cotangent, mixer_gain, w_query, w_key, w_value, w_swish, decay_down, decay_up,
    decay_bias, head_gain, w_output, dense_gain, w_gate, w_up, w_down,
):
    sizes = layout(lax.axis_size("dp"))
    tall, deep, far, _ = sizes
    core = lax.axis_index("tensor")
    place = lax.axis_index("dp")
    z_at, y_at, far_at, near = split_place(place, sizes)
    own_rows = tokens.shape[0]
    half_rows = own_rows // 2
    width = tokens.shape[1]
    block = width // lax.axis_size("dp")

    count = tall * deep * far
    slot = np.arange(count, dtype=np.int32)
    slot_z, slot_y, slot_far = slot % tall, (slot // tall) % deep, slot // (tall * deep)
    from_z, from_y, from_far = slot // (deep * far), (slot // far) % deep, slot % far

    def counted(at, backwards, size):
        return lax.rem(at + (size - backwards), np.int32(size))

    places = (counted(z_at, slot_z, tall) * deep + counted(y_at, slot_y, deep)) * far + counted(far_at, slot_far, far)
    back = (counted(far_at, from_far, far) * deep + counted(y_at, from_y, deep)) * tall + counted(z_at, from_z, tall)

    def blocks_of(values, order):
        chosen = (order[:, None] == slot[None, :]).astype(f32)
        flat = values.astype(f32).reshape(count, -1)
        return jnp.dot(chosen, flat, precision=HIGH).reshape(values.shape)

    def halves(*shards):
        own = jnp.concatenate([half(shard, near, 1) for shard in shards], 1)
        other = jnp.concatenate([half(shard, 1 - near, 1) for shard in shards], 1)
        return own, other

    x_link, y_link, z_link = Link(1), Link(2), Link(4)

    def cross(values, *others):
        return x_link.send(lambda v: shift(v, sizes, 3, 1), values, *others)

    def along_z(pair):
        up = down = pair
        ups, downs = [], []
        for hop in range(1, tall):
            up = z_link.send(lambda v: lax.ppermute(v, "dp", hop_pairs(sizes, 0, 1, hop)), up)
            down = z_link.send(lambda v: lax.ppermute(v, "dp", hop_pairs(sizes, 0, -1, hop)), down)
            ups.append(up)
            downs.append(down)
        return [jnp.where(z_at >= back, ups[back - 1], downs[tall - back - 1]) for back in range(1, tall)]

    def along_y(part, *others):
        found = [part]
        for axis in (1, 2):
            found = found + [
                y_link.send(lambda v: shift(v, sizes, axis, step), one, *others)
                for step in range(1, sizes[axis]) for one in found
            ]
        return found[1:]

    def stacked(columns):
        return jnp.concatenate([column[i] for i in range(deep * far) for column in columns], 0)

    z_order = sorted(range(1, tall), key=lambda back: max(back, tall - back))

    def z_then_y(pair, along, rest, ties):
        columns = [[pair] + rest] + [None] * (tall - 1)
        for back, tie in zip(z_order, ties):
            columns[back] = [along[back - 1]] + along_y(along[back - 1], *tie)
        return stacked(columns)

    def y_then_z(pair, rest):
        slab = jnp.concatenate([pair] + rest, 0)
        size = pair.shape[0]
        slabs = [slab] + along_z(slab)
        return stacked([[one[i * size : (i + 1) * size] for i in range(deep * far)] for one in slabs])

    halved = [
        halves(w_query, w_key, w_value, w_swish), halves(w_output.T), halves(w_gate), halves(w_up), halves(w_down.T)
    ]
    (w_first, w_out, pair_g, pair_u, pair_d), (tok_next, cot_next), seg_next = opening(
        sizes, 2, [own for own, _ in halved], [other for _, other in halved],
        [half(tokens, core), half(cotangent, core)], segment_ids,
    )
    along_g = along_z(pair_g)
    rest_g = along_y(pair_g)
    rest_u, rest_d = along_y(pair_u), along_y(pair_d)
    along_u = along_z(pair_u)

    def slabs(left, right):
        slab = tall * 2 * block
        outer = deep * far
        made = [slab_gradient(left, right, number * slab, slab, ()) for number in reversed(range(1, outer))]
        return made if outer == 2 else (tuple(made),)

    def sent_y(made):
        received = []
        outer = deep * far
        for number, sent in zip(reversed(range(1, outer)), (made,) if outer == 2 else made):
            back_far, back_y = number // deep, number % deep
            if back_y:
                sent = y_link.send(lambda v: shift(v, sizes, 1, -back_y), sent)
            if back_far:
                sent = shift(sent, sizes, 2, -back_far)
            received.append(sent)
        return received

    def own_slab(left, right, received):
        return slab_gradient(left, right, 0, tall * 2 * block, received)

    def finish(total):
        rows = 2 * block
        parts = [total[step * rows : (step + 1) * rows] for step in range(tall)]
        up = down = None
        for hop in range(1, tall):
            reach = tall - hop
            rising, falling = parts[tall - reach], parts[reach]
            if up is not None:
                rising = (rising.astype(f32) + up.astype(f32)).astype(bf16)
                falling = (falling.astype(f32) + down.astype(f32)).astype(bf16)
            up = z_link.send(lambda v: lax.ppermute(v, "dp", reach_pairs(sizes, 0, 1, reach)), rising)
            down = z_link.send(lambda v: lax.ppermute(v, "dp", reach_pairs(sizes, 0, -1, reach)), falling)
        kept = parts[0].astype(f32) + up.astype(f32) + down.astype(f32)
        received = shift(half(kept, 1 - near).astype(bf16), sizes, 3, 1).astype(f32)
        return half(kept, near), received

    def columns(parts, begin, end):
        own, received = (part[:, begin:end] for part in parts)
        return jnp.where(
            near == 0, jnp.concatenate([own, received], 1), jnp.concatenate([received, own], 1)
        )

    def whole_chip(rows):
        return in_order(core, rows, core_swap(rows))

    def from_neighbour(rows):
        return whole_chip(cross(rows))

    def summed_ahead(partial_next):
        handed = core_swap(half(partial_next, 1 - core))
        ahead = (half(partial_next, core).astype(f32) + handed.astype(f32)).astype(bf16)
        return cross(ahead)

    def summed_here(partial_own, ahead):
        handed = core_swap(half(partial_own, 1 - core))
        return half(partial_own, core).astype(f32) + handed.astype(f32) + ahead.astype(f32)

    seg_own = segment_ids
    tok_own = reorder(tokens, places)
    tok_next = reorder(tok_next, places)
    gain_first = blocks_of(mixer_gain.astype(f32), places)[None]
    gain_second = blocks_of(dense_gain.astype(f32), places)
    down = blocks_of(decay_down, places).astype(bf16)
    head = 2 * core + near
    up_own = lax.dynamic_slice_in_dim(decay_up, head * DK, DK, 1).astype(f32)
    bias_own = lax.dynamic_slice_in_dim(decay_bias, head * DK, DK, 0).astype(f32)[None]
    gain_heads = head_gain.astype(f32)[None]

    def root_of(values):
        return lax.rsqrt(jnp.mean(values * values, axis=-1, keepdims=True) + norm_eps)

    def forward_of(tok, seg):
        return mixer_forward(tok, w_first, down, gain_first, seg, up_own, bias_own, gain_heads)

    first_next, low_next, qkv_next, swish_next, scores_next, mixed_next, gated_next = forward_of(tok_next, seg_next)
    first_own, low_own, qkv_own, swish_own, scores_own, mixed_own, gated_own = forward_of(
        after(tok_own, gated_next), seg_own
    )
    branch_next = product_nt(gated_next, w_out)
    branch_ahead = summed_ahead(branch_next)
    branch_own = product_nt(after(gated_own, branch_next), w_out)
    w_g = z_then_y(pair_g, along_g, rest_g, [(gated_own,), (branch_own,), (branch_own,)])
    branch = summed_here(branch_own, branch_ahead)
    hidden = half(tok_own, core).astype(f32) + branch
    root_hidden = root_of(hidden)
    second_half = (hidden * root_hidden * gain_second).astype(bf16)
    w_u = z_then_y(pair_u, along_u, rest_u, [(branch_own,), (second_half,), (second_half,)])
    w_d = y_then_z(pair_d, rest_d)
    second_next = from_neighbour(second_half)
    second_own = whole_chip(second_half)
    cot_own = reorder(after(cotangent, second_half), places)
    cot_next = reorder(after(cot_next, second_half), places)

    gate_own, upper_own, product_own = dense_forward(second_own, w_g, w_u)
    gate_next, upper_next, product_next = dense_forward(after(second_next, product_own), w_g, w_u)
    cots, products, second = (cot_own, cot_next), (product_own, product_next), (second_own, second_next)

    def tied(values, *others):
        return [after(one, *others) for one in values]

    def norm_pull(values, root, gain, wanted):
        scaled = wanted * gain
        return root * scaled - values * (
            root * root * root * jnp.mean(values * scaled, axis=-1, keepdims=True)
        )

    (slab_d,) = slabs(cots, products)
    y_d = sent_y(slab_d)
    d_gate_next, d_up_next, d_second_next = dense_backward(after(cot_next, slab_d), w_d, w_g, w_u, gate_next, upper_next)
    d_gate_own, d_up_own, d_second_own = dense_backward(
        after(cot_own, d_second_next), w_d, w_g, w_u, gate_own, upper_own
    )
    second_ahead = summed_ahead(d_second_next)
    d_gates, d_ups = (d_gate_own, d_gate_next), (d_up_own, d_up_next)
    (slab_g,) = slabs(second, d_gates)
    y_g = sent_y(slab_g)
    (slab_u,) = slabs(second, tied(d_ups, slab_g))
    y_u = sent_y(slab_u)
    d_second = summed_here(d_second_own, after(second_ahead, slab_u))
    d_hidden = half(cot_own, core).astype(f32) + norm_pull(hidden, root_hidden, gain_second, d_second)
    grad_dense_gain = jnp.sum(d_second * hidden * root_hidden, axis=0)
    d_branch_half = d_hidden.astype(bf16)
    d_branch_next = from_neighbour(d_branch_half)
    d_branch_own = whole_chip(d_branch_half)
    fixed_own = (up_own, bias_own, gain_heads)
    d_qkvs_own, d_low_own, d_first_own, *small_own = mixer_backward(
        d_branch_own, w_out, w_first, down, qkv_own, swish_own, low_own, seg_own, *fixed_own, scores_own, mixed_own
    )
    sum_d = own_slab(cots, products, tied(y_d, d_first_own))
    d_qkvs_next, d_low_next, d_first_next, *small_next = mixer_backward(
        after(d_branch_next, sum_d), w_out, w_first, down, qkv_next, swish_next, low_next, seg_next, *fixed_own,
        scores_next, mixed_next,
    )
    firsts, d_parts = (first_own, first_next), (d_qkvs_own, d_qkvs_next)
    (slab_first,) = slabs(firsts, d_parts)
    y_first = sent_y(slab_first)
    d_branches, gateds = (d_branch_own, d_branch_next), (gated_own, gated_next)
    (slab_o,) = slabs(d_branches, tied(gateds, slab_first))
    first_ahead = summed_ahead(after(d_first_next, slab_first))
    sum_g = own_slab(second, d_gates, tied(y_g, slab_o))
    out_d = finish(sum_d)
    out_g = finish(sum_g)
    dense_next = product_nt(after(product_next, sum_g), w_d)
    dense_own = product_nt(after(product_own, dense_next), w_d)
    dense_ahead = summed_ahead(dense_next)
    sum_u = own_slab(second, d_ups, tied(y_u, dense_own))
    out_u = finish(sum_u)
    y_o = sent_y(slab_o)
    d_first = summed_here(d_first_own, first_ahead)
    tok_mine = half(tok_own, core).astype(f32)
    root_mine = root_of(tok_mine)
    grad_half = d_hidden + norm_pull(tok_mine, root_mine, gain_first[0], d_first)
    grad_mixer_gain = jnp.sum(d_first * tok_mine * root_mine, axis=0)
    grad_tokens = reorder(whole_chip(grad_half), back)
    dense_out = summed_here(dense_own, dense_ahead)
    output = reorder(whole_chip((hidden + dense_out).astype(bf16)), back)
    out_first = finish(own_slab(firsts, d_parts, y_first))
    out_o = finish(own_slab(d_branches, gateds, y_o))

    def down_part(first, d_low):
        return lax.dot_general(
            first.astype(f32), d_low, (((0,), (0,)), ((), ())), precision=HIGH, preferred_element_type=f32
        )

    grad_down = down_part(first_own, d_low_own) + down_part(first_next, d_low_next)
    grad_up, grad_bias, grad_head = (one + two for one, two in zip(small_own, small_next))
    small = [
        blocks_of(grad_mixer_gain, back),
        blocks_of(grad_dense_gain, back),
        grad_head[0],
        blocks_of(grad_down, back),
        lax.dynamic_update_slice_in_dim(jnp.zeros(decay_up.shape, f32), grad_up, head * DK, 1),
        lax.dynamic_update_slice_in_dim(jnp.zeros(decay_bias.shape, f32), grad_bias[0], head * DK, 0),
    ]
    packed = jnp.concatenate([one.reshape(-1, 128) for one in small], 0)
    packed = packed + core_swap(packed)
    for axis in (3, 2, 1, 0):
        reach = 1
        while reach < sizes[axis]:
            packed = packed + lax.ppermute(packed, "dp", exchange_pairs(sizes, axis, reach))
            reach *= 2
    places_of = np.cumsum([0] + [one.size // 128 for one in small])
    small = [
        packed[begin:end].reshape(one.shape) for one, begin, end in zip(small, places_of[:-1], places_of[1:])
    ]


    def all_of(parts):
        return columns(parts, 0, parts[0].shape[1])

    return (
        output,
        grad_tokens,
        small[0],
        columns(out_first, 0, DK),
        columns(out_first, DK, 2 * DK),
        columns(out_first, 2 * DK, 2 * DK + DV),
        columns(out_first, 2 * DK + DV, 2 * DK + 2 * DV),
        small[3],
        small[4],
        small[5],
        small[2],
        all_of(out_o).T,
        small[1],
        all_of(out_g),
        all_of(out_u),
        all_of(out_d).T,
    )


def solution(mesh):
    rows, large, turned, whole = P("dp", None), P("dp", "tensor"), P("tensor", "dp"), P()
    in_specs = (
        rows, P("dp"), rows, whole, large, large, large, large, whole, whole, whole, whole, turned,
        whole, large, large, turned,
    )
    out_specs = (
        rows, rows, whole, large, large, large, large, whole, whole, whole, whole, turned, whole,
        large, large, turned,
    )
    return jax.shard_map(on_device, mesh=mesh, in_specs=in_specs, out_specs=out_specs, check_vma=False)
```

time: 1370 us -> 1090 us (0.80)
  waiting for transfers between devices: 709 us -> 257 us
  Pallas kernels: 69.2 us -> 432 us
  matrix products: 233 us -> 6.67 us
  starting transfers between devices: 105 us -> 161 us
  blocking collectives: 45.3 us -> 0 us
  other arithmetic: 95.7 us -> 127 us
  between operations: 27 us -> 2.5 us
  local copies, waits for them, and re-layouts: 71.7 us -> 89.3 us
    ppermute x74 -> x25, waiting for transfers between devices: 709 us -> 81 us  [shift(): return lax.ppermute(values, 'dp', shift_pairs(sizes, axis, step))]
    pallas_call x2 -> x23, Pallas kernels: 37.3 us -> 400 us  [the longest x1 113 us: opening(): pl.pallas_call(partial(opening_kernel, sizes, (groups, full, row_count)),...]
    dot_general x33 -> x8, matrix products: 233 us -> 6.67 us  [the longest x2 4.8 us: down_part(): lax.dot_general(first.astype(f32), d_low, (((0,), (0,)), ((), ())), preci...]
    ppermute x0 -> x52, waiting for transfers between devices: none -> 173 us  [the longest x15 56.7 us: finish(): lax.ppermute(v, 'dp', reach_pairs(sizes, 0, 1, reach))]
    ppermute x0 -> x52, starting transfers between devices: none -> 127 us  [the longest x15 41.5 us: finish(): lax.ppermute(v, 'dp', reach_pairs(sizes, 0, 1, reach))]
    ppermute x74 -> x25, starting transfers between devices: 104 us -> 32.5 us  [shift(): return lax.ppermute(values, 'dp', shift_pairs(sizes, axis, step))]
    psum x1 -> x0, blocking collectives: 45.3 us -> none  [on_device(): small = lax.psum(small, ('dp', 'tensor'))]
    convert_element_type x7 -> x15, other arithmetic: 12.8 us -> 34.3 us  [the longest x10 17.3 us: finish(): rising = (rising.astype(f32) + up.astype(f32)).astype(bf16)]
  transfers between devices with their start and end apart: 91 -> 92, of which waited for: 43 -> 36; matrix products, arithmetic and copies ran while one was open for 27% -> 17% of each run, Pallas kernels for 3% -> 27%
where the time goes in v2:
time: 1090 us; the launch traced here: 1070 us
  Pallas kernels  432 us (40%)
  waiting for transfers between devices  257 us (24%)
  starting transfers between devices  161 us (15%)
  other arithmetic  127 us (12%)
  local copies, waits for them, and re-layouts  89.3 us (8%)
    pallas_call x1, Pallas kernels, opening(): pl.pallas_call(partial(opening_kernel, sizes, (groups, full, row_count)),...  113 us
    pallas_call x10, Pallas kernels, slab_gradient(): call(partial(slab_kernel, len(received)), 'slab_gradient', (rows // tile,...  87.1 us
    ppermute x25, waiting for transfers between devices, shift(): return lax.ppermute(values, 'dp', shift_pairs(sizes, axis, step))  81 us
    ppermute x15, waiting for transfers between devices, finish(): lax.ppermute(v, 'dp', reach_pairs(sizes, 0, 1, reach))  56.7 us
    pallas_call x2, Pallas kernels, mixer_backward(): call(mixer_backward_kernel, 'mixer_backward', (pieces,), [by_rows(PIECE,...  54.7 us
    ppermute x9, waiting for transfers between devices, along_z(): lax.ppermute(v, 'dp', hop_pairs(sizes, 0, -1, hop))  51.6 us
    pallas_call x2, Pallas kernels, dense_backward(): call(dense_backward_kernel, 'dense_backward', (rows // 256,), [by_rows(25...  48.6 us
    ppermute x15, starting transfers between devices, finish(): lax.ppermute(v, 'dp', reach_pairs(sizes, 0, 1, reach))  41.5 us
  transfers between devices with their start and end apart: 92, of which 36 were waited for; matrix products, arithmetic and copies ran while one was open for 17% of the time, Pallas kernels for 27%

profile of v2, /device:TPU:10, one launch (start us, length us, event | category | flops | bytes accessed | tf_op | source)
XLA Modules:
  0.0 1074.6 jit_solution(16247664178076378827)
XLA Ops:
  15.5 113.3 %opening.1 = (bf16[2048,1536]{1,0:T(8,128)(2,1)}, bf16[2048,512]{1,0:T(8,128)(2,1)}, bf16[256,1408]{1,0:T(8,128)(2,1)}, bf16[256,1408]{1,0:T(8,128)(2,1)}, bf16[...) custom-call(bf16[128,1536]{1,0:T(8,128)(2,1)} %pad_maximum_fusion.refs_0_, ...), custom_call_target="tpu_custom_call" | custom-call | flops 1 | bytes 1 | tf_op jit(solution)/shard_map/opening/pallas_call | solution.py:638
  149.4 17.0 %mixer_forward.2 = (bf16[768,2048]{1,0:T(8,128)(2,1)}, f32[768,16]{1,0:T(8,128)}, bf16[768,1024]{1,0:T(8,128)(2,1)}, f32[768,512]{1,0:T(8,128)}, bf16[768,256]{1...) custom-call(bf16[768,2048]{1,0:T(8,128)(2,1)} %reorder.7.tok, ...), custom_call_target="tpu_custom_call" | custom-call | flops 1 | bytes 1 | tf_op jit(solution)/shard_map/mixer_forward/pallas_call | solution.py:257
  181.0 17.1 %mixer_forward.3 = (bf16[768,2048]{1,0:T(8,128)(2,1)}, f32[768,16]{1,0:T(8,128)}, bf16[768,1024]{1,0:T(8,128)(2,1)}, f32[768,512]{1,0:T(8,128)}, bf16[768,256]{1...) custom-call(bf16[768,2048]{1,0:T(8,128)(2,1)} %reorder.6.tok, ...), custom_call_target="tpu_custom_call" | custom-call | flops 1 | bytes 1 | tf_op jit(solution)/shard_map/mixer_forward/pallas_call | solution.py:257
  245.3 13.8 %collective-permute-done.17 = bf16[256,1408]{1,0:T(8,128)(2,1)S(1)} collective-permute-done((bf16[256,1408]{1,0:T(8,128)(2,1)S(1)}, bf16[256,1408]{1,0:T(8,128)(2,1)S(1)}, u32[]{:S(2)}, u32[]{:S(2)}) %collective-permute-start.17) | collective-permute-done | bytes 720928 | tf_op jit(solution)/shard_map/ppermute | solution.py:701
  291.2 10.6 collective-permute-done.12
  324.1 14.4 %collective-permute-done.28 = bf16[512,1408]{1,0:T(8,128)(2,1)} collective-permute-done((bf16[512,1408]{1,0:T(8,128)(2,1)}, bf16[512,1408]{1,0:T(8,128)(2,1)}, u32[]{:S(2)}, u32[]{:S(2)}) %collective-permute-start.28) | collective-permute-done | bytes 1441824 | tf_op jit(solution)/shard_map/ppermute | solution.py:701
  392.8 16.3 %dense_forward.2 = (f32[768,1408]{1,0:T(8,128)}, f32[768,1408]{1,0:T(8,128)}, bf16[768,1408]{1,0:T(8,128)(2,1)}) custom-call(bf16[768,2048]{1,0:T(8,128)(2,1)} %maximum_select_fusion.1.second.left_own, bf16[2048,1408]{1,0:T(8,128)(2,1)} %constant_dynamic-update-slice_fusion.w_g, bf16[2048,1408]{1,0:T(8,128)(2,1)} %constant_dynamic-update-slice_fusion.8.w_u), custom_call_target="tpu_custom_call" | custom-call | flops 1 | bytes 1 | tf_op jit(solution)/shard_map/dense_forward/pallas_call | solution.py:406
  418.9 16.3 %dense_forward.3 = (f32[768,1408]{1,0:T(8,128)}, f32[768,1408]{1,0:T(8,128)}, bf16[768,1408]{1,0:T(8,128)(2,1)}) custom-call(bf16[768,2048]{1,0:T(8,128)(2,1)} %maximum_select_fusion.2.second.left_next, bf16[2048,1408]{1,0:T(8,128)(2,1)} %constant_dynamic-update-slice_fusion.w_g, bf16[2048,1408]{1,0:T(8,128)(2,1)} %constant_dynamic-update-slice_fusion.8.w_u), custom_call_target="tpu_custom_call" | custom-call | flops 1 | bytes 1 | tf_op jit(solution)/shard_map/dense_forward/pallas_call | solution.py:406
  454.1 24.2 %dense_backward.2 = (bf16[768,1408]{1,0:T(8,128)(2,1)}, bf16[768,1408]{1,0:T(8,128)(2,1)}, bf16[768,2048]{1,0:T(8,128)(2,1)}) custom-call(bf16[768,2048]{1,0:T(8,128)(2,1)} %reorder.9.left_next.cot, bf16[2048,1408]{1,0:T(8,128)(2,1)} %slice_dynamic-update-slice_fusion.w_d.right, bf16[2048,1408]{1,0:T(8,128)(2,1)} %constant_dynamic-update-slice_fusion.w_g, ...), custom_call_target="tpu_custom_call" | custom-call | flops 1 | bytes 1 | tf_op jit(solution)/shard_map/dense_backward/pallas_call | solution.py:427
  481.1 24.4 %dense_backward.3 = (bf16[768,1408]{1,0:T(8,128)(2,1)}, bf16[768,1408]{1,0:T(8,128)(2,1)}, bf16[768,2048]{1,0:T(8,128)(2,1)}) custom-call(bf16[768,2048]{1,0:T(8,128)(2,1)} %reorder.8.left_own.cot, bf16[2048,1408]{1,0:T(8,128)(2,1)} %slice_dynamic-update-slice_fusion.w_d.right, bf16[2048,1408]{1,0:T(8,128)(2,1)} %constant_dynamic-update-slice_fusion.w_g, ...), custom_call_target="tpu_custom_call" | custom-call | flops 1 | bytes 1 | tf_op jit(solution)/shard_map/dense_backward/pallas_call | solution.py:427
  532.2 14.3 %collective-permute-done.36 = bf16[384,2048]{1,0:T(8,128)(2,1)} collective-permute-done((bf16[384,2048]{1,0:T(8,128)(2,1)}, bf16[384,2048]{1,0:T(8,128)(2,1)}, u32[]{:S(2)}, u32[]{:S(2)}) %collective-permute-start.36) | collective-permute-done | bytes 1572896 | tf_op jit(solution)/shard_map/ppermute | solution.py:53
  563.8 27.5 %mixer_backward.2 = (bf16[768,1536]{1,0:T(8,128)(2,1)}, f32[768,16]{1,0:T(8,128)}, bf16[768,2048]{1,0:T(8,128)(2,1)}, f32[16,256]{1,0:T(8,128)}, f32[1,256]{1,0:T(1,128)}, /*index=5*/f32[1,512]{1,0:T(1,128)}) custom-call(bf16[768,2048]{1,0:T(8,128)(2,1)} %maximum_select_fusion.3.d_branch.left_own, bf16[2048,512]{1,0:T(8,128)(2,1)} %get-tuple-element.148.right.w_out, ...), custom_call_target="tpu_custom_call" | custom-call | flops 1 | bytes 1 | tf_op jit(solution)/shard_map/mixer_backward/pallas_call | solution.py:373
  591.3 9.7 slab_gradient.13
  606.0 17.3 %collective-permute-done.56 = bf16[256,1408]{1,0:T(8,128)(2,1)S(1)} collective-permute-done((bf16[256,1408]{1,0:T(8,128)(2,1)S(1)}, bf16[256,1408]{1,0:T(8,128)(2,1)S(1)}, u32[]{:S(2)}, u32[]{:S(2)}) %collective-permute-start.56) | collective-permute-done | bytes 720928 | tf_op jit(solution)/shard_map/ppermute | solution.py:775
  661.2 27.2 %mixer_backward.3 = (bf16[768,1536]{1,0:T(8,128)(2,1)}, f32[768,16]{1,0:T(8,128)}, bf16[768,2048]{1,0:T(8,128)(2,1)}, f32[16,256]{1,0:T(8,128)}, f32[1,256]{1,0:T(1,128)}, /*index=5*/f32[1,512]{1,0:T(1,128)}) custom-call(bf16[768,2048]{1,0:T(8,128)(2,1)} %maximum_select_fusion.4.d_branch.left_next, bf16[2048,512]{1,0:T(8,128)(2,1)} %get-tuple-element.148.right.w_out, ...), custom_call_target="tpu_custom_call" | custom-call | flops 1 | bytes 1 | tf_op jit(solution)/shard_map/mixer_backward/pallas_call | solution.py:373
  703.2 9.7 slab_gradient.16
  713.0 9.5 product_nt.6
  746.6 9.7 slab_gradient.18
  827.9 14.5 %collective-permute-done.61 = bf16[256,1408]{1,0:T(8,128)(2,1)S(1)} collective-permute-done((bf16[256,1408]{1,0:T(8,128)(2,1)S(1)}, bf16[256,1408]{1,0:T(8,128)(2,1)S(1)}, u32[]{:S(2)}, u32[]{:S(2)}) %collective-permute-start.61) | collective-permute-done | bytes 720928 | tf_op jit(solution)/shard_map/ppermute | solution.py:775
  865.4 12.3 %collective-permute-done.54.rest_0_ = bf16[1024,1536]{1,0:T(8,128)(2,1)S(1)} collective-permute-done((bf16[1024,1536]{1,0:T(8,128)(2,1)S(1)}, bf16[1024,1536]{1,0:T(8,128)(2,1)S(1)}, u32[]{:S(2)}, u32[]{:S(2)}) %collective-permute-start.54) | collective-permute-done | bytes 3145760 | tf_op jit(solution)/shard_map/ppermute | solution.py:53
  881.6 9.9 slab_gradient.17
  938.9 19.1 %collective-permute-done.90 = bf16[128,1408]{1,0:T(8,128)(2,1)S(1)} collective-permute-done((bf16[128,1408]{1,0:T(8,128)(2,1)S(1)}, bf16[128,1408]{1,0:T(8,128)(2,1)S(1)}, u32[]{:S(2)}, u32[]{:S(2)}) %collective-permute-start.90) | collective-permute-done | bytes 360480 | tf_op jit(solution)/shard_map/ppermute | solution.py:53
  963.0 22.8 %collective-permute-done.53 = f32[428,128]{1,0:T(8,128)S(1)} collective-permute-done((f32[428,128]{1,0:T(8,128)S(1)}, f32[428,128]{1,0:T(8,128)S(1)}, u32[]{:S(2)}, u32[]{:S(2)}) %collective-permute-start.53) | collective-permute-done | bytes 219168 | tf_op jit(solution)/shard_map/ppermute | solution.py:924
  1008.5 11.1 %collective-permute-done.79 = bf16[256,1536]{1,0:T(8,128)(2,1)S(1)} collective-permute-done((bf16[256,1536]{1,0:T(8,128)(2,1)S(1)}, bf16[256,1536]{1,0:T(8,128)(2,1)S(1)}, u32[]{:S(2)}, u32[]{:S(2)}) %collective-permute-start.79) | collective-permute-done | bytes 786464 | tf_op jit(solution)/shard_map/ppermute | solution.py:776
  (479 shorter events, 590.1 us)
Async XLA Ops:
  128.8 75.9 %collective-permute-start.10 = (bf16[256,1408]{1,0:T(8,128)(2,1)}, bf16[256,1408]{1,0:T(8,128)(2,1)S(1)}, u32[]{:S(2)}, u32[]{:S(2)}) collective-permute-start(bf16[256,1408]{1,0:T(8,128)(2,1)} %get-tuple-element.150), channel_id=1, source_target_pairs={{0,4},{2,6},{4,0},{6,2},{8,12},{10,14},{12,8},{14,10},{16,20},{18,... | collective-permute-start | bytes 2162696 | tf_op jit(solution)/shard_map/ppermute | solution.py:53
  130.4 74.8 %collective-permute-start.5 = (bf16[256,1408]{1,0:T(8,128)(2,1)}, bf16[256,1408]{1,0:T(8,128)(2,1)}, u32[]{:S(2)}, u32[]{:S(2)}) collective-permute-start(bf16[256,1408]{1,0:T(8,128)(2,1)} %get-tuple-element.150), channel_id=1, source_target_pairs={{8,0},{10,2},{12,4},{14,6},{16,8},{18,10},{20,12},{22,14},{24,16},... | collective-permute-start | bytes 2162696 | tf_op jit(solution)/shard_map/ppermute | solution.py:701
  132.8 75.6 %collective-permute-start.4 = (bf16[256,1408]{1,0:T(8,128)(2,1)}, bf16[256,1408]{1,0:T(8,128)(2,1)}, u32[]{:S(2)}, u32[]{:S(2)}) collective-permute-start(bf16[256,1408]{1,0:T(8,128)(2,1)} %get-tuple-element.150), channel_id=1, source_target_pairs={{0,8},{2,10},{4,12},{6,14},{8,16},{10,18},{12,20},{14,22},{16,24},... | collective-permute-start | bytes 2162696 | tf_op jit(solution)/shard_map/ppermute | solution.py:700
  174.6 62.6 %collective-permute-start.1 = (bf16[384,2048]{1,0:T(8,128)(2,1)}, bf16[384,2048]{1,0:T(8,128)(2,1)}, u32[]{:S(2)}, u32[]{:S(2)}) collective-permute-start(bf16[384,2048]{1,0:T(8,128)(2,1)} %constant_dynamic-slice_fusion.11), channel_id=1, source_target_pairs={{0,1},{1,0},{2,3},{3,2},{4,5},{5,4},{6,7},{7,6},{8,9},{9,8},{10,11... | collective-permute-start | bytes 4718600 | tf_op jit(solution)/shard_map/ppermute | solution.py:94
  245.3 60.7 %collective-permute-start = (bf16[384,2048]{1,0:T(8,128)(2,1)S(1)}, bf16[384,2048]{1,0:T(8,128)(2,1)S(1)}, u32[]{:S(2)}, u32[]{:S(2)}) collective-permute-start(bf16[384,2048]{1,0:T(8,128)(2,1)S(1)} %constant_dynamic-slice_fusion.12), channel_id=1, source_target_pairs={{0,1},{1,0},{2,3},{3,2},{4,5},{5,4},{6,7},{7,6},{8,9},{9,8},{10,11... | collective-permute-start | bytes 4718600 | tf_op jit(solution)/shard_map/ppermute | solution.py:94
  259.2 50.6 %collective-permute-start.2 = (bf16[384,2048]{1,0:T(8,128)(2,1)S(1)}, bf16[384,2048]{1,0:T(8,128)(2,1)S(1)}, u32[]{:S(2)}, u32[]{:S(2)}) collective-permute-start(bf16[384,2048]{1,0:T(8,128)(2,1)S(1)} %add_convert_fusion.4), channel_id=1, source_target_pairs={{0,2},{2,0},{4,6},{6,4},{8,10},{10,8},{12,14},{14,12},{16,18},{18,... | collective-permute-start | bytes 4718600 | tf_op jit(solution)/shard_map/ppermute | solution.py:53
  289.7 56.2 %collective-permute-start.21 = (bf16[256,1408]{1,0:T(8,128)(2,1)}, bf16[256,1408]{1,0:T(8,128)(2,1)}, u32[]{:S(2)}, u32[]{:S(2)}) collective-permute-start(bf16[256,1408]{1,0:T(8,128)(2,1)} %collective-permute-done.20), channel_id=1, source_target_pairs={{16,24},{18,26},{20,28},{22,30},{17,25},{19,27},{21,29},{23,31}} | collective-permute-start | bytes 2162696 | tf_op jit(solution)/shard_map/ppermute | solution.py:700
  314.3 57.5 %collective-permute-start.25 = (bf16[384,2048]{1,0:T(8,128)(2,1)}, bf16[384,2048]{1,0:T(8,128)(2,1)}, u32[]{:S(2)}, u32[]{:S(2)}) collective-permute-start(bf16[384,2048]{1,0:T(8,128)(2,1)} %multiply_convert_fusion), channel_id=1, source_target_pairs={{0,2},{2,0},{4,6},{6,4},{8,10},{10,8},{12,14},{14,12},{16,18},{18,... | collective-permute-start | bytes 4718600 | tf_op jit(solution)/shard_map/ppermute | solution.py:53
  324.1 57.8 %collective-permute-start.3 = (bf16[384,2048]{1,0:T(8,128)(2,1)}, bf16[384,2048]{1,0:T(8,128)(2,1)}, u32[]{:S(2)}, u32[]{:S(2)}) collective-permute-start(bf16[384,2048]{1,0:T(8,128)(2,1)} %multiply_convert_fusion), channel_id=1, source_target_pairs={{0,1},{1,0},{2,3},{3,2},{4,5},{5,4},{6,7},{7,6},{8,9},{9,8},{10,11... | collective-permute-start | bytes 4718600 | tf_op jit(solution)/shard_map/ppermute | solution.py:94
  357.8 51.3 %collective-permute-start.31 = (bf16[512,1408]{1,0:T(8,128)(2,1)}, bf16[512,1408]{1,0:T(8,128)(2,1)}, u32[]{:S(2)}, u32[]{:S(2)}) collective-permute-start(bf16[512,1408]{1,0:T(8,128)(2,1)} %collective-permute-done.27), channel_id=1, source_target_pairs={{8,16},{10,18},{12,20},{14,22},{16,24},{18,26},{20,28},{22,30},{9,... | collective-permute-start | bytes 4325384 | tf_op jit(solution)/shard_map/ppermute | solution.py:700
  377.5 66.8 %collective-permute-start.30 = (bf16[512,1408]{1,0:T(8,128)(2,1)}, bf16[512,1408]{1,0:T(8,128)(2,1)}, u32[]{:S(2)}, u32[]{:S(2)}) collective-permute-start(bf16[512,1408]{1,0:T(8,128)(2,1)} %collective-permute-done.29), channel_id=1, source_target_pairs={{8,0},{10,2},{12,4},{14,6},{9,1},{11,3},{13,5},{15,7}} | collective-permute-start | bytes 4325384 | tf_op jit(solution)/shard_map/ppermute | solution.py:701
  512.5 78.8 %collective-permute-start.40 = (bf16[1024,1408]{1,0:T(8,128)(2,1)}, bf16[1024,1408]{1,0:T(8,128)(2,1)}, u32[]{:S(2)}, u32[]{:S(2)}) collective-permute-start(bf16[1024,1408]{1,0:T(8,128)(2,1)} %slab_gradient.10), channel_id=1, source_target_pairs={{0,4},{2,6},{4,0},{6,2},{8,12},{10,14},{12,8},{14,10},{16,20},{18,... | collective-permute-start | bytes 8650760 | tf_op jit(solution)/shard_map/ppermute | solution.py:53
  604.5 98.7 %collective-permute-start.33 = (bf16[1024,1408]{1,0:T(8,128)(2,1)}, bf16[1024,1408]{1,0:T(8,128)(2,1)}, u32[]{:S(2)}, u32[]{:S(2)}) collective-permute-start(bf16[1024,1408]{1,0:T(8,128)(2,1)} %slab_gradient.11), channel_id=1, source_target_pairs={{0,4},{2,6},{4,0},{6,2},{8,12},{10,14},{12,8},{14,10},{16,20},{18,... | collective-permute-start | bytes 8650760 | tf_op jit(solution)/shard_map/ppermute | solution.py:53
  631.7 102.7 %collective-permute-start.55 = (bf16[1024,1408]{1,0:T(8,128)(2,1)}, bf16[1024,1408]{1,0:T(8,128)(2,1)}, u32[]{:S(2)}, u32[]{:S(2)}) collective-permute-start(bf16[1024,1408]{1,0:T(8,128)(2,1)} %slab_gradient.12), channel_id=1, source_target_pairs={{0,4},{2,6},{4,0},{6,2},{8,12},{10,14},{12,8},{14,10},{16,20},{18,... | collective-permute-start | bytes 8650760 | tf_op jit(solution)/shard_map/ppermute | solution.py:53
  649.6 115.0 %collective-permute-start.71 = (bf16[256,1408]{1,0:T(8,128)(2,1)}, bf16[256,1408]{1,0:T(8,128)(2,1)}, u32[]{:S(2)}, u32[]{:S(2)}) collective-permute-start(bf16[256,1408]{1,0:T(8,128)(2,1)} %get-tuple-element.252), channel_id=1, source_target_pairs={{8,0},{10,2},{12,4},{14,6},{16,8},{18,10},{20,12},{22,14},{24,16},... | collective-permute-start | bytes 2162696 | tf_op jit(solution)/shard_map/ppermute | solution.py:776
  651.5 113.2 %collective-permute-start.59 = (bf16[256,1408]{1,0:T(8,128)(2,1)}, bf16[256,1408]{1,0:T(8,128)(2,1)}, u32[]{:S(2)}, u32[]{:S(2)}) collective-permute-start(bf16[256,1408]{1,0:T(8,128)(2,1)} %get-tuple-element.240), channel_id=1, source_target_pairs={{0,8},{2,10},{4,12},{6,14},{8,16},{10,18},{12,20},{14,22},{16,24},... | collective-permute-start | bytes 2162696 | tf_op jit(solution)/shard_map/ppermute | solution.py:775
  787.6 106.7 %collective-permute-start.47 = (bf16[384,2048]{1,0:T(8,128)(2,1)}, bf16[384,2048]{1,0:T(8,128)(2,1)}, u32[]{:S(2)}, u32[]{:S(2)}) collective-permute-start(bf16[384,2048]{1,0:T(8,128)(2,1)} %constant_dynamic-slice_fusion.5), channel_id=1, source_target_pairs={{0,1},{1,0},{2,3},{3,2},{4,5},{5,4},{6,7},{7,6},{8,9},{9,8},{10,11... | collective-permute-start | bytes 4718600 | tf_op jit(solution)/shard_map/ppermute | solution.py:94
  792.9 51.1 %collective-permute-start.42 = (bf16[384,2048]{1,0:T(8,128)(2,1)}, bf16[384,2048]{1,0:T(8,128)(2,1)}, u32[]{:S(2)}, u32[]{:S(2)}) collective-permute-start(bf16[384,2048]{1,0:T(8,128)(2,1)} %constant_dynamic-slice_fusion.7), channel_id=1, source_target_pairs={{0,1},{1,0},{2,3},{3,2},{4,5},{5,4},{6,7},{7,6},{8,9},{9,8},{10,11... | collective-permute-start | bytes 4718600 | tf_op jit(solution)/shard_map/ppermute | solution.py:94
  808.3 69.5 %collective-permute-start.54 = (bf16[1024,1536]{1,0:T(8,128)(2,1)S(1)}, bf16[1024,1536]{1,0:T(8,128)(2,1)S(1)}, u32[]{:S(2)}, u32[]{:S(2)}) collective-permute-start(bf16[1024,1536]{1,0:T(8,128)(2,1)S(1)} %copy-done.20), channel_id=1, source_target_pairs={{0,4},{2,6},{4,0},{6,2},{8,12},{10,14},{12,8},{14,10},{16,20},{18,... | collective-permute-start | bytes 9437192 | tf_op jit(solution)/shard_map/ppermute | solution.py:53
  860.7 136.8 %collective-permute-start.41 = (bf16[384,2048]{1,0:T(8,128)(2,1)}, bf16[384,2048]{1,0:T(8,128)(2,1)}, u32[]{:S(2)}, u32[]{:S(2)}) collective-permute-start(bf16[384,2048]{1,0:T(8,128)(2,1)} %constant_dynamic-slice_fusion.8), channel_id=1, source_target_pairs={{0,1},{1,0},{2,3},{3,2},{4,5},{5,4},{6,7},{7,6},{8,9},{9,8},{10,11... | collective-permute-start | bytes 4718600 | tf_op jit(solution)/shard_map/ppermute | solution.py:94
  913.8 88.5 %collective-permute-start.45 = (bf16[384,2048]{1,0:T(8,128)(2,1)}, bf16[384,2048]{1,0:T(8,128)(2,1)}, u32[]{:S(2)}, u32[]{:S(2)}) collective-permute-start(bf16[384,2048]{1,0:T(8,128)(2,1)} %add_convert_fusion.2), channel_id=1, source_target_pairs={{0,2},{2,0},{4,6},{6,4},{8,10},{10,8},{12,14},{14,12},{16,18},{18,... | collective-permute-start | bytes 4718600 | tf_op jit(solution)/shard_map/ppermute | solution.py:53
  937.6 55.7 %collective-permute-start.78 = (bf16[256,1536]{1,0:T(8,128)(2,1)}, bf16[256,1536]{1,0:T(8,128)(2,1)}, u32[]{:S(2)}, u32[]{:S(2)}) collective-permute-start(bf16[256,1536]{1,0:T(8,128)(2,1)} %get-tuple-element.259), channel_id=1, source_target_pairs={{16,8},{18,10},{20,12},{22,14},{24,16},{26,18},{28,20},{30,22},{17... | collective-permute-start | bytes 2359304 | tf_op jit(solution)/shard_map/ppermute | solution.py:776
  985.9 63.7 %collective-permute-start.48 = (f32[384,2048]{1,0:T(8,128)}, f32[384,2048]{1,0:T(8,128)}, u32[]{:S(2)}, u32[]{:S(2)}) collective-permute-start(f32[384,2048]{1,0:T(8,128)} %fusion.3), channel_id=1, source_target_pairs={{0,1},{1,0},{2,3},{3,2},{4,5},{5,4},{6,7},{7,6},{8,9},{9,8},{10,11... | collective-permute-start | bytes 9437192 | tf_op jit(solution)/shard_map/ppermute | solution.py:94
  1008.4 55.7 %collective-permute-start.46 = (bf16[384,2048]{1,0:T(8,128)(2,1)}, bf16[384,2048]{1,0:T(8,128)(2,1)}, u32[]{:S(2)}, u32[]{:S(2)}) collective-permute-start(bf16[384,2048]{1,0:T(8,128)(2,1)} %add_convert_fusion), channel_id=1, source_target_pairs={{0,1},{1,0},{2,3},{3,2},{4,5},{5,4},{6,7},{7,6},{8,9},{9,8},{10,11... | collective-permute-start | bytes 4718600 | tf_op jit(solution)/shard_map/ppermute | solution.py:94
  (128 other events, 3236.6 us)

commit v3 on v1

v3 whole, which is shorter than its diff:
```python
from functools import partial
from types import SimpleNamespace

import jax
import jax.numpy as jnp
import numpy as np
from jax import lax
from jax.experimental import pallas as pl
from jax.experimental.pallas import tpu as pltpu
from jax.sharding import PartitionSpec as P

DK = 256
DV = 512
PIECE = 256
norm_eps = 1e-06
head_eps = 1e-05
LEVELS = (1, 2, 4, 8, 16, 32, 64, 128)
f32 = jnp.float32
bf16 = jnp.bfloat16
HIGH = lax.Precision.HIGHEST


def layout(chips):
    return {16: (4, 2, 1, 2), 64: (4, 4, 2, 2)}.get(chips, (1, 1, chips // 2, 2))


def split_place(place, sizes):
    _, deep, far, _ = sizes
    near = lax.rem(place, np.int32(2))
    far_at = lax.rem(lax.div(place, np.int32(2)), np.int32(far))
    y_at = lax.rem(lax.div(place, np.int32(2 * far)), np.int32(deep))
    return lax.div(place, np.int32(2 * far * deep)), y_at, far_at, near


def mm(left, right):
    return lax.dot_general(left, right, (((1,), (0,)), ((), ())), preferred_element_type=f32)


def mm_nt(left, right):
    return lax.dot_general(left, right, (((1,), (1,)), ((), ())), preferred_element_type=f32)


def mm_tn(left, right):
    return lax.dot_general(left, right, (((0,), (0,)), ((), ())), preferred_element_type=f32)


def reorder_kernel(places, source, target):
    count = places.shape[0]
    width = source.shape[1] // count
    for block in range(count):
        start = pl.multiple_of(places[block] * width, width)
        target[:, block * width : (block + 1) * width] = source[:, pl.ds(start, width)]


def reorder(values, places):
    rows, columns = values.shape
    count = places.shape[0]
    width = columns // count
    if width % 128 != 0:
        return jnp.concatenate(
            [lax.dynamic_slice_in_dim(values, places[i] * width, width, 1) for i in range(count)], 1
        )
    tile = 192 if rows % 192 == 0 else rows
    return pl.pallas_call(
        reorder_kernel,
        out_shape=jax.ShapeDtypeStruct(values.shape, values.dtype),
        grid_spec=pltpu.PrefetchScalarGridSpec(
            num_scalar_prefetch=1,
            grid=(rows // tile,),
            in_specs=[pl.BlockSpec((tile, columns), lambda i, p: (i, 0))],
            out_specs=pl.BlockSpec((tile, columns), lambda i, p: (i, 0)),
        ),
        cost_estimate=pl.CostEstimate(
            flops=0, bytes_accessed=2 * values.size * values.dtype.itemsize, transcendentals=0
        ),
        name="reorder",
    )(places, values)


def bit_of(shape, level):
    return (lax.broadcasted_iota(jnp.int32, shape, 0) & level) != 0


def partner(values, level, upper):
    size = values.shape[0]
    return jnp.where(
        upper, pltpu.roll(values, level, 0), pltpu.roll(values, size - level, 0)
    )


def same_document(seg_row):
    across = jnp.broadcast_to(seg_row[0].astype(f32), (PIECE, PIECE))
    return across == across.T


def log_decay(low, up, bias):
    pre = jnp.dot(low, up, precision=HIGH, preferred_element_type=f32) + bias
    return pre, (jnp.minimum(pre, 0.0) - jnp.log1p(jnp.exp(-jnp.abs(pre)))) * (1.0 / 16.0)


def level_exponents(decay):
    prefix, suffix, total = decay, jnp.zeros_like(decay), decay
    found = []
    for level in LEVELS:
        upper = bit_of(decay.shape, level)
        found.append(jnp.where(upper, prefix, suffix))
        if level != LEVELS[-1]:
            beside = partner(total, level, upper)
            prefix = prefix + jnp.where(upper, beside, 0.0)
            suffix = suffix + jnp.where(upper, 0.0, beside)
            total = total + beside
    return found


def pair_distance():
    rows = lax.broadcasted_iota(jnp.int32, (PIECE, PIECE), 0)
    columns = lax.broadcasted_iota(jnp.int32, (PIECE, PIECE), 1)
    return rows ^ columns, rows >= columns


def fixed(shape):
    return pl.BlockSpec(shape, lambda i: (0,) * len(shape), pipeline_mode=pl.Buffered(1))


def by_rows(tile, width):
    return pl.BlockSpec((tile, width), lambda i: (i, 0))


def shape_of(rows, width, kind):
    return jax.ShapeDtypeStruct((rows, width), kind)


vmem_limit = 60 * 1024 * 1024


def piece_attention(query_low, keyset_low, decay):
    query, keyset = query_low.astype(f32), keyset_low.astype(f32)
    apart, causal = pair_distance()
    scores = mm_nt(query_low, keyset_low)
    for level, exponent in zip(LEVELS, level_exponents(decay)):
        upper = bit_of(decay.shape, level)
        scaled = (jnp.where(upper, query, keyset) * jnp.exp(exponent)).astype(bf16)
        scores = jnp.where(apart >= level, mm_nt(scaled, scaled), scores)
    return scores, causal


def mixer_forward_kernel(
    tok, w_first, down, gain_first, seg_row, up, bias, gain,
    first_out, low_out, qkv_out, swish_out, scores_out, mixed_out, gated_out,
):
    rows = tok[...].astype(f32)
    root_rows = lax.rsqrt(jnp.mean(rows * rows, axis=-1, keepdims=True) + norm_eps)
    first = (rows * root_rows * gain_first[...]).astype(bf16)
    first_out[...] = first
    low = mm(first, down[...])
    low_out[...] = low
    qkv = mm(first, w_first[:, : 2 * DK + DV]).astype(bf16)
    qkv_out[...] = qkv
    opened = mm(first, w_first[:, 2 * DK + DV :])
    swish_out[...] = opened
    _, decay = log_decay(low, up[...], bias[...])
    scores, causal = piece_attention(qkv[:, :DK], qkv[:, DK : 2 * DK], decay)
    allowed = causal & same_document(seg_row)
    scores = jnp.where(allowed, scores * (DK**-0.5), 0.0).astype(bf16)
    mixed = mm(scores, qkv[:, 2 * DK :])
    scores_out[...] = scores
    mixed_out[...] = mixed
    root = lax.rsqrt(jnp.mean(mixed * mixed, axis=-1, keepdims=True) + head_eps)
    gated_out[...] = (mixed * root * gain[...] * (opened * jax.nn.sigmoid(opened))).astype(bf16)


def mixer_backward_kernel(
    d_branch, w_out, w_first, down, qkv, swish, low, seg_row, up, bias, gain, scores_in, mixed_in, first,
    d_qkvs, d_first, d_up, d_bias, d_gain, d_down,
):
    query = qkv[:, :DK].astype(f32)
    keyset = qkv[:, DK : 2 * DK].astype(f32)
    values = qkv[:, 2 * DK :]
    pre, decay = log_decay(low[...], up[...], bias[...])
    apart, causal = pair_distance()
    mixed = mixed_in[...]
    root = lax.rsqrt(jnp.mean(mixed * mixed, axis=-1, keepdims=True) + head_eps)
    normed = mixed * root
    opened = swish[...]
    sigma = jax.nn.sigmoid(opened)
    wanted = mm(d_branch[...], w_out[...])
    d_swish = (wanted * normed * gain[...] * (sigma + opened * sigma * (1.0 - sigma))).astype(bf16)
    d_scaled = wanted * (opened * sigma)
    gain_part = jnp.sum(d_scaled * normed, axis=0, keepdims=True)
    d_normed = d_scaled * gain[...]
    d_mixed = root * (d_normed - normed * jnp.mean(d_normed * normed, axis=-1, keepdims=True))
    d_mixed = d_mixed.astype(bf16)
    d_values = mm_tn(scores_in[...], d_mixed).astype(bf16)
    allowed = causal & same_document(seg_row)
    d_scores = jnp.where(allowed, mm_nt(d_mixed, values) * (DK**-0.5), 0.0)
    on_diagonal = jnp.sum(jnp.where(apart == 0, d_scores, 0.0), axis=1, keepdims=True)
    d_query = on_diagonal * keyset
    d_keyset = on_diagonal * query
    both = d_scores + d_scores.T
    exponents = level_exponents(decay)
    d_prefix = d_suffix = d_total = jnp.zeros_like(decay)
    for level, exponent in reversed(list(zip(LEVELS, exponents))):
        upper = bit_of(decay.shape, level)
        if level != LEVELS[-1]:
            d_beside = jnp.where(upper, d_prefix, d_suffix) + d_total
            d_total = d_total + partner(d_beside, level, upper)
        base = jnp.where(upper, query, keyset)
        factor = jnp.exp(exponent)
        scaled = (base * factor).astype(bf16)
        here = jnp.where((apart >= level) & (apart < 2 * level), both, 0.0).astype(bf16)
        d_base = mm(here, scaled) * factor
        d_exponent = d_base * base
        d_query = d_query + jnp.where(upper, d_base, 0.0)
        d_keyset = d_keyset + jnp.where(upper, 0.0, d_base)
        d_prefix = d_prefix + jnp.where(upper, d_exponent, 0.0)
        d_suffix = d_suffix + jnp.where(upper, 0.0, d_exponent)
    d_pre = (d_prefix + d_total) * jax.nn.sigmoid(-pre) * (1.0 / 16.0)
    d_query, d_keyset = d_query.astype(bf16), d_keyset.astype(bf16)
    d_qkvs[:, :DK] = d_query
    d_qkvs[:, DK : 2 * DK] = d_keyset
    d_qkvs[:, 2 * DK : 2 * DK + DV] = d_values
    d_qkvs[:, 2 * DK + DV :] = d_swish
    d_low = lax.dot_general(
        d_pre, up[...], (((1,), (1,)), ((), ())), precision=HIGH, preferred_element_type=f32
    )
    high = d_low.astype(bf16)
    rest = (d_low - high.astype(f32)).astype(bf16)
    d_down[...] += mm_tn(high, first[...]) + mm_tn(rest, first[...])
    d_first[...] = (
        mm_nt(d_query, w_first[:, :DK])
        + mm_nt(d_keyset, w_first[:, DK : 2 * DK])
        + mm_nt(d_values, w_first[:, 2 * DK : 2 * DK + DV])
        + mm_nt(d_swish, w_first[:, 2 * DK + DV :])
        + lax.dot_general(
            d_low, down[...].astype(f32), (((1,), (1,)), ((), ())), precision=HIGH, preferred_element_type=f32
        )
    ).astype(bf16)
    d_up[...] += lax.dot_general(
        low[...], d_pre, (((0,), (0,)), ((), ())), precision=HIGH, preferred_element_type=f32
    )
    d_bias[...] += jnp.sum(d_pre, axis=0, keepdims=True)
    d_gain[...] += gain_part


def dense_forward_kernel(second, w_g, w_u, gate_out, upper_out, product_out):
    gate = mm(second[...], w_g[...])
    gate_out[...] = gate
    upper = mm(second[...], w_u[...])
    upper_out[...] = upper
    product_out[...] = (gate * jax.nn.sigmoid(gate) * upper).astype(bf16)


def dense_backward_kernel(cot, w_d, w_g, w_u, gate_in, upper_in, d_gate_out, d_up_out, d_second):
    gate = gate_in[...]
    sigma = jax.nn.sigmoid(gate)
    d_product = mm(cot[...], w_d[...])
    d_gate = (d_product * upper_in[...] * (sigma + gate * sigma * (1.0 - sigma))).astype(bf16)
    d_up = (d_product * (gate * sigma)).astype(bf16)
    d_gate_out[...] = d_gate
    d_up_out[...] = d_up
    d_second[...] = (mm_nt(d_gate, w_g[...]) + mm_nt(d_up, w_u[...])).astype(bf16)


class Place:
    def __init__(self, sizes):
        self.sizes = sizes
        tall, deep, far, _ = sizes
        place, self.core = lax.axis_index("dp"), lax.axis_index("tensor")
        self.near = place % 2
        self.far_at = (place // 2) % far
        self.y_at = (place // (2 * far)) % deep
        self.z_at = place // (2 * far * deep)
        self.has_above, self.has_below = self.z_at + 1 < tall, self.z_at >= 1
        self.beside = self.device(self.z_at, self.y_at, self.far_at, 1 - self.near, self.core)
        self.other_core = self.device(self.z_at, self.y_at, self.far_at, self.near, 1 - self.core)
        self.above = self.device(self.z_at + 1, self.y_at, self.far_at, self.near, self.core)
        self.below = self.device(self.z_at - 1, self.y_at, self.far_at, self.near, self.core)
        self.shifts = [(fr, yr) for fr in range(far) for yr in range(deep) if fr or yr]

    def device(self, z, y, far_x, near_x, which):
        _, deep, far, _ = self.sizes
        return (((z * deep + y) * far + far_x) * 2 + near_x, which)

    def peer(self, fr, yr):
        _, deep, far, _ = self.sizes
        return self.device(self.z_at, (self.y_at + yr) % deep, (self.far_at + fr) % far, self.near, self.core)

    def block_of(self, slot):
        tall, deep, far, _ = self.sizes
        back_z, back_y, back_far = slot % tall, (slot // tall) % deep, slot // (tall * deep)
        place = (self.z_at + tall - back_z) % tall * deep + (self.y_at + deep - back_y) % deep
        return place * far + (self.far_at + far - back_far) % far

    def greet(self):
        barrier = pltpu.get_barrier_semaphore()

        def signal(who):
            pl.semaphore_signal(barrier, inc=1, device_id=who, device_id_type=pl.DeviceIdType.MESH)

        signal(self.beside)
        signal(self.other_core)
        for fr, yr in self.shifts:
            signal(self.peer(fr, yr))
        tall = self.sizes[0]
        for step_z in range(1, tall):
            signal(self.device((self.z_at + step_z) % tall, self.y_at, self.far_at, self.near, self.core))
        pl.semaphore_wait(barrier, 2 + len(self.shifts) + tall - 1)

    def partners(self):
        tall, deep, far, _ = self.sizes
        found = [self.other_core, self.beside]
        at = (self.z_at, self.y_at, self.far_at)
        for axis, extent in ((2, far), (1, deep), (0, tall)):
            reach = 1
            while reach < extent:
                to = list(at)
                to[axis] = at[axis] + reach - 2 * reach * (at[axis] // reach % 2)
                found.append(self.device(*to, self.near, self.core))
                reach *= 2
        return found


class Copies:
    def __init__(self, send_sem, recv_sem):
        self.send_sem, self.recv_sem, self.used = send_sem, recv_sem, 0

    def make(self, source, target, who):
        index = self.used
        self.used += 1
        return pltpu.make_async_remote_copy(
            src_ref=source, dst_ref=target, send_sem=self.send_sem.at[index], recv_sem=self.recv_sem.at[index],
            device_id=who, device_id_type=pl.DeviceIdType.MESH,
        )


def stream(body, steps, ins, outs):
    pltpu.emit_pipeline(
        body, grid=(steps,),
        in_specs=[pl.BlockSpec(shape, index) for _, shape, index in ins],
        out_specs=[pl.BlockSpec(shape, index) for _, shape, index in outs],
    )(*[one for one, _, _ in ins], *[one for one, _, _ in outs])


def still(i):
    return (0, 0)


def step(i):
    return (i, 0)


def from_tile(first):
    return lambda i: (first + i, 0)


def pull_of(values, gain, wanted):
    root = lax.rsqrt(jnp.mean(values * values, axis=-1, keepdims=True) + norm_eps)
    scaled = wanted * gain
    pulled = root * scaled - values * (root * root * root * jnp.mean(values * scaled, axis=-1, keepdims=True))
    return pulled, jnp.sum(wanted * values * root, axis=0, keepdims=True)


def backward_part(sizes, r, here, copies):
    tall, deep, far, _ = sizes
    core, near, z_at = here.core, here.near, here.z_at
    width = r.cot.shape[1]
    rows = r.cot.shape[0]
    chip_rows = rows // 2
    half_rows = chip_rows // 2
    units = r.product.shape[1]
    tiles = half_rows // 128
    chip_tiles = chip_rows // 256
    outer = deep * far
    size = width // outer // tall
    slab = size * tall
    for total in (r.d_up_acc, r.d_bias_acc, r.d_gain_acc, r.dense_gain_acc, r.mixer_gain_acc, r.d_down_acc):
        total[...] = jnp.zeros_like(total)
    waits = []
    sides = dict(
        d=(r.cot, r.product), g=(r.second, r.d_gate), u=(r.second, r.d_up), f=(r.first, r.d_qkvs),
        o=(r.d_branch, r.gated),
    )
    slab_tile = 256 if slab % 256 == 0 else 128

    def product_slab(group, number, received, target, slabs_of=1):
        left, right = sides[group]
        columns = right.shape[1]
        at = number * slab // slab_tile

        def body(left_ref, right_ref, *rest):
            total = mm_tn(left_ref[...], right_ref[...])
            for other in rest[:-1]:
                total = total + other[...].astype(f32)
            rest[-1][...] = total.astype(bf16)

        stream(
            body, slabs_of * slab // slab_tile,
            [(left, (rows, slab_tile), lambda i: (0, at + i)), (right, (rows, columns), still)]
            + [(one, (slab_tile, columns), step) for one in received],
            [(target, (slab_tile, columns), step)],
        )

    y_copies, z_copies = {}, {}

    def part(ref, index, count):
        return ref.at[pl.ds(index * count, count)]

    def send_slabs(group):
        made = []
        for number in reversed(range(1, outer)):
            fr, yr = number // deep, number % deep
            source, target = (part(getattr(r, name + group), number - 1, slab) for name in ("y_send_", "y_recv_"))
            product_slab(group, number, (), source)
            copy = copies.make(source, target, here.peer((far - fr) % far, (deep - yr) % deep))
            copy.start()
            made.append(copy)
        y_copies[group] = made
        waits.extend(copy.wait_send for copy in made)

    z_first = ("u",)

    def numbers_of(group):
        return range(outer) if group in z_first else (0,)

    def slot_of(group, number, hop, way):
        return (number * (tall - 1) + hop - 1) * 2 + way

    def z_start(group, hop):
        reach = tall - hop
        goes_up, goes_down = z_at + reach < tall, z_at >= reach
        comes_up = here.has_below & (z_at - 1 + reach < tall)
        comes_down = here.has_above & (z_at + 1 >= reach)
        total, sent, received = (getattr(r, name + group) for name in ("sum_", "z_send_", "z_recv_"))
        made = []
        for number in numbers_of(group):
            if hop == 1:
                rising, falling = (part(total, number * tall + at, size) for at in (tall - reach, reach))
            else:
                rising, falling = (part(sent, slot_of(group, number, hop - 1, way), size) for way in (0, 1))
            up = copies.make(rising, part(received, slot_of(group, number, hop, 0), size), here.above)
            down = copies.make(falling, part(received, slot_of(group, number, hop, 1), size), here.below)
            pl.when(goes_up)(up.start)
            pl.when(goes_down)(down.start)
            waits.append(lambda up=up: pl.when(goes_up)(up.wait_send))
            waits.append(lambda down=down: pl.when(goes_down)(down.wait_send))
            made.append((up, down))
        z_copies[group, hop] = made, comes_up, comes_down

    def z_wait(group, hop):
        made, comes_up, comes_down = z_copies[group, hop]
        for up, down in made:
            pl.when(comes_up)(up.wait_recv)
            pl.when(comes_down)(down.wait_recv)

    def own_sum(group):
        for copy in y_copies[group]:
            copy.wait_recv()
        received = getattr(r, "y_recv_" + group)
        product_slab(
            group, 0, [part(received, number - 1, slab) for number in range(1, outer)], getattr(r, "sum_" + group)
        )
        z_start(group, 1)

    def all_slabs(group):
        product_slab(group, 0, (), getattr(r, "sum_" + group), outer)
        z_start(group, 1)

    def z_next(group, hop):
        z_wait(group, hop - 1)
        reach = tall - hop
        total, sent, received = (getattr(r, name + group) for name in ("sum_", "z_send_", "z_recv_"))
        columns = total.shape[1]

        def body(rising, up, falling, down, rising_out, falling_out):
            rising_out[...] = (
                rising[...].astype(f32) + jnp.where(here.has_below, up[...].astype(f32), 0.0)
            ).astype(bf16)
            falling_out[...] = (
                falling[...].astype(f32) + jnp.where(here.has_above, down[...].astype(f32), 0.0)
            ).astype(bf16)

        block = (size, columns)

        def at(index_of):
            return lambda i: (index_of(i), 0)

        stream(
            body, len(numbers_of(group)),
            [
                (total, block, at(lambda i: i * tall + tall - reach)),
                (received, block, at(lambda i: slot_of(group, i, hop - 1, 0))),
                (total, block, at(lambda i: i * tall + reach)),
                (received, block, at(lambda i: slot_of(group, i, hop - 1, 1))),
            ],
            [
                (sent, block, at(lambda i: slot_of(group, i, hop - 1, 0))),
                (sent, block, at(lambda i: slot_of(group, i, hop - 1, 1))),
            ],
        )
        z_start(group, hop)

    def y_last(group):
        z_wait(group, tall - 1)
        total, received, kept = (getattr(r, name + group) for name in ("sum_", "z_recv_", "y_send_"))
        block = (size, total.shape[1])

        def body(own, up, down, into):
            value = own[...].astype(f32) + jnp.where(here.has_below, up[...].astype(f32), 0.0)
            into[...] = (value + jnp.where(here.has_above, down[...].astype(f32), 0.0)).astype(bf16)

        stream(
            body, outer,
            [
                (total, block, lambda i: (i * tall, 0)),
                (received, block, lambda i: (slot_of(group, i, tall - 1, 0), 0)),
                (received, block, lambda i: (slot_of(group, i, tall - 1, 1), 0)),
            ],
            [(kept, block, step)],
        )
        made = []
        for number in range(1, outer):
            fr, yr = number // deep, number % deep
            target = part(getattr(r, "y_recv_" + group), number - 1, size)
            copy = copies.make(
                part(kept, number, size), target, here.peer((far - fr) % far, (deep - yr) % deep)
            )
            copy.start()
            made.append(copy)
        y_copies[group] = made
        waits.extend(copy.wait_send for copy in made)

    def z_finish(group):
        if group in z_first:
            for copy in y_copies[group]:
                copy.wait_recv()
            received = getattr(r, "y_recv_" + group)
            arrays = [part(getattr(r, "y_send_" + group), 0, size)]
            arrays += [part(received, number - 1, size) for number in range(1, outer)]
            counts = [None] * outer
        else:
            z_wait(group, tall - 1)
            received = getattr(r, "z_recv_" + group)
            arrays = [part(getattr(r, "sum_" + group), 0, size)]
            arrays += [part(received, slot_of(group, 0, tall - 1, way), size) for way in (0, 1)]
            counts = [None, here.has_below, here.has_above]
        block = (size // 2, arrays[0].shape[1])
        number_of = len(arrays)

        def body(*both):
            for inputs, into in ((both[:number_of], both[-2]), (both[number_of:-2], both[-1])):
                total = jnp.zeros(block, f32)
                for one, counted in zip(inputs, counts):
                    value = one[...].astype(f32)
                    total = total + (value if counted is None else jnp.where(counted, value, 0.0))
                into[...] = total.astype(into.dtype)

        mine, theirs = (lambda i: (near, 0)), (lambda i: (1 - near, 0))
        crossing = getattr(r, "cross_" + group)
        stream(
            body, 1,
            [(one, block, mine) for one in arrays] + [(one, block, theirs) for one in arrays],
            [(getattr(r, "kept_" + group), block, still), (crossing, block, still)],
        )
        copy = copies.make(crossing, getattr(r, "received_" + group), here.beside)
        copy.start()
        waits.append(copy.wait)

    partners = here.partners()
    exchanges = []

    def small_begin():
        count, _, each = r.by_block.shape
        r.by_block[...] = jnp.zeros_like(r.by_block)
        r.by_head[...] = jnp.zeros_like(r.by_head)
        rank = r.d_up_acc.shape[0]
        for slot in range(count):
            lanes = pl.ds(slot * each, each)
            at = here.block_of(slot)
            r.by_block[at, 0:1, :] = r.mixer_gain_acc[:, lanes]
            r.by_block[at, 1:2, :] = r.dense_gain_acc[:, lanes]
            r.by_block[at, 8 : 8 + rank, :] = r.d_down_acc[:, lanes]
        head = 2 * core + near
        r.by_head[head, 8 : 8 + rank, :] = r.d_up_acc[...]
        r.by_head[head, 0:1, :] = r.d_bias_acc[...]
        r.by_head[0, 1:2, :] = r.d_gain_acc[:, :DK]
        r.by_head[0, 2:3, :] = r.d_gain_acc[:, DK:]

    def small_send():
        index = len(exchanges)
        made = [
            copies.make(own, got.at[index], partners[index])
            for own, got in ((r.by_block, r.got_block), (r.by_head, r.got_head))
        ]
        for copy in made:
            copy.start()
        exchanges.append(made)

    def small_take():
        index = len(exchanges) - 1
        for copy in exchanges[index]:
            copy.wait()
        r.by_block[...] += r.got_block[index]
        r.by_head[...] += r.got_head[index]
        if len(exchanges) < len(partners):
            small_send()
            return True
        return False

    def rows_of(held, start):
        return held.at[pl.ds(pl.multiple_of(start, 128), half_rows)]

    hands, aheads = {}, {}

    def hand(name, following):
        first = (chip_rows if following else 0) + (1 - core) * half_rows
        suffix = "_next" if following else "_own"
        copy = copies.make(rows_of(getattr(r, name), first), getattr(r, "hand_" + name + suffix), here.other_core)
        copy.start()
        hands[name, following] = copy
        waits.append(copy.wait_send)

    def ahead(name):
        hands[name, True].wait_recv()

        def body(one, other, out):
            out[...] = (one[...].astype(f32) + other[...].astype(f32)).astype(bf16)

        block = (128, width)
        stream(
            body, tiles,
            [(getattr(r, name), block, from_tile(2 * tiles + core * tiles)), (getattr(r, "hand_" + name + "_next"), block, step)],
            [(getattr(r, "ahead_" + name), block, step)],
        )
        copy = copies.make(getattr(r, "ahead_" + name), getattr(r, "behind_" + name), here.beside)
        copy.start()
        aheads[name] = copy
        waits.append(copy.wait_send)

    def summed_inputs(name):
        hands[name, False].wait_recv()
        aheads[name].wait_recv()
        block = (128, width)
        return [
            (getattr(r, name), block, from_tile(core * tiles)), (getattr(r, "hand_" + name + "_own"), block, step),
            (getattr(r, "behind_" + name), block, step),
        ]

    def total_of(one, two, three):
        return one[...].astype(f32) + two[...].astype(f32) + three[...].astype(f32)

    def dense_back(first_tile):
        def body(cot, gate, upper, d_gate, d_up, d_second):
            dense_backward_kernel(
                cot, r.v_w_d, r.v_w_g, r.v_w_u, gate, upper, d_gate, d_up, d_second
            )

        at = from_tile(first_tile)
        stream(
            body, chip_tiles,
            [(r.cot, (256, width), at), (r.gate, (256, units), at), (r.upper, (256, units), at)],
            [(r.d_gate, (256, units), at), (r.d_up, (256, units), at), (r.d_second, (256, width), at)],
        )

    def mixer_back(first_tile):
        def body(d_branch, qkv, swish, low, seg_row, scores, mixed, first, d_qkvs, d_first):
            mixer_backward_kernel(
                d_branch, r.v_w_out, r.v_w_first, r.down, qkv, swish, low, seg_row, r.up,
                r.bias, r.gain_heads, scores, mixed, first, d_qkvs, d_first, r.d_up_acc, r.d_bias_acc,
                r.d_gain_acc, r.d_down_acc,
            )

        at = from_tile(first_tile)

        def whole(held):
            return (held, (PIECE, held.shape[1]), at)

        stream(
            body, chip_rows // PIECE,
            [
                whole(r.d_branch), whole(r.qkv), whole(r.swish), whole(r.low),
                (r.seg_row, (1, 1, PIECE), lambda i: (first_tile + i, 0, 0)), whole(r.scores), whole(r.mixed),
                whole(r.first),
            ],
            [whole(r.d_qkvs), whole(r.d_first)],
        )

    block = (128, width)
    own_half = from_tile(core * tiles)

    send_slabs("d")
    yield
    dense_back(chip_tiles)
    hand("d_second", True)
    dense_back(0)
    hand("d_second", False)
    ahead("d_second")
    send_slabs("g")
    all_slabs("u")

    def dense_out_body(product, out):
        out[...] = mm_nt(product[...], r.v_w_d[...]).astype(bf16)

    stream(
        dense_out_body, 2 * chip_tiles, [(r.product, (256, units), step)], [(r.dense, (256, width), step)]
    )

    def hidden_body(one, two, three, cot, hidden, d_hidden, d_branch):
        wanted = total_of(one, two, three)
        pulled, gain_part = pull_of(hidden[...], r.gain_second[...], wanted)
        total = cot[...].astype(f32) + pulled
        d_hidden[...] = total
        d_branch[...] = total.astype(bf16)
        r.dense_gain_acc[...] += gain_part

    stream(
        hidden_body, tiles,
        summed_inputs("d_second") + [(r.cot, block, own_half), (r.hidden, block, step)],
        [(r.d_hidden, block, step), (r.d_branch, block, own_half)],
    )
    mine = rows_of(r.d_branch, core * half_rows)
    there = rows_of(r.d_branch, chip_rows + core * half_rows)
    share_branch = copies.make(mine, mine, here.other_core)
    cross_branch = copies.make(mine, there, here.beside)
    share_branch.start()
    cross_branch.start()
    waits.extend([share_branch.wait_send, cross_branch.wait_send])
    hand("dense", True)
    hand("dense", False)
    share_branch.wait_recv()
    z_next("u", 2)
    mixer_back(0)
    hand("d_first", False)
    cross_branch.wait_recv()
    share_next = copies.make(there, there, here.other_core)
    share_next.start()
    waits.append(share_next.wait_send)
    own_sum("d")
    z_next("u", 3)
    share_next.wait_recv()
    mixer_back(chip_tiles)
    hand("d_first", True)
    send_slabs("f")
    ahead("d_first")
    y_last("u")
    send_slabs("o")
    own_sum("g")
    z_next("d", 2)
    ahead("dense")
    z_next("g", 2)
    z_next("d", 3)

    def tokens_body(one, two, three, d_hidden, tok, out):
        wanted = total_of(one, two, three)
        pulled, gain_part = pull_of(tok[...].astype(f32), r.gain_first[...], wanted)
        out[...] = d_hidden[...] + pulled
        r.mixer_gain_acc[...] += gain_part

    stream(
        tokens_body, tiles,
        summed_inputs("d_first") + [(r.d_hidden, block, step), (r.tok, block, own_half)],
        [(r.grad_tokens, block, own_half)],
    )
    mine = rows_of(r.grad_tokens, core * half_rows)
    copy = copies.make(mine, mine, here.other_core)
    copy.start()
    waits.append(copy.wait)
    small_begin()
    small_send()
    z_next("g", 3)

    def output_body(one, two, three, hidden, out):
        out[...] = (hidden[...] + total_of(one, two, three)).astype(bf16)

    stream(
        output_body, tiles, summed_inputs("dense") + [(r.hidden, block, step)], [(r.output, block, own_half)]
    )
    mine = rows_of(r.output, core * half_rows)
    copy = copies.make(mine, mine, here.other_core)
    copy.start()
    waits.append(copy.wait)
    small_take()
    z_finish("u")
    z_finish("d")
    small_take()
    z_finish("g")
    own_sum("f")
    own_sum("o")
    small_take()
    z_next("f", 2)
    z_next("o", 2)
    small_take()
    z_next("f", 3)
    z_next("o", 3)
    while small_take():
        pass
    z_finish("f")
    z_finish("o")
    yield
    for wait in waits:
        wait()


def forward_part(sizes, r, here, copies):
    tall, deep, far, _ = sizes
    core, near, z_at = here.core, here.near, here.z_at
    first, out, gate, up, down = range(5)
    weights = (r.w_first, r.w_out, r.w_g, r.w_u, r.w_d)
    shards = {
        first: (r.s_query, r.s_key, r.s_value, r.s_swish), out: (r.s_output,), gate: (r.s_gate,), up: (r.s_up,),
        down: (r.s_down,),
    }
    chip_rows, width = r.tokens.shape
    half_rows = chip_rows // 2
    tiles, chip_tiles, pieces = half_rows // 128, chip_rows // 256, chip_rows // PIECE
    outer = deep * far
    block = r.s_query.shape[0]
    size = 2 * block
    units = r.w_g.shape[1]
    waits, locals_made, loads = [], {}, {}

    def local(source, target):
        index = len(locals_made)
        locals_made[index] = copy = pltpu.make_async_copy(source, target, r.load_sem.at[index])
        copy.start()
        return copy

    def load(source, target):
        loads[source] = local(weights[source], target)

    crossings = {}

    def cross(group):
        mine = pl.ds(pl.multiple_of(near * block, 16), block)
        made, at = [], 0
        for shard in shards[group]:
            columns = shard.shape[1] // 2
            there = pl.ds(at, columns)
            keep = shard.at[:, pl.ds(pl.multiple_of(near * columns, 128), columns)]
            give = shard.at[:, pl.ds(pl.multiple_of((1 - near) * columns, 128), columns)]
            target = weights[group].at[mine, there]
            remote = copies.make(give, target, here.beside)
            remote.start()
            made.append((local(keep, target), remote))
            waits.append(remote.wait_send)
            at += columns
        crossings[group] = made

    def arrive(group):
        for kept, remote in crossings[group]:
            kept.wait()
            remote.wait_recv()

    def slab(group, number, back):
        return weights[group].at[pl.ds((number * tall + back) * size, size)]

    sideways = {}

    def spread(group, back, condition=None):
        for number, (fr, yr) in enumerate(here.shifts):
            key = (group, number, back)
            if key not in sideways:
                sideways[key] = copies.make(
                    slab(group, 0, back), slab(group, number + 1, back), here.peer(fr, yr)
                )
            if condition is None:
                sideways[key].start()
            else:
                pl.when(condition)(sideways[key].start)

    def sides_done(group, backs):
        for number in range(outer - 1):
            for back in backs:
                sideways[group, number, back].wait()

    along = {}

    def hop_start(group, hop, numbers=(0,)):
        rises, falls = here.has_above & (z_at >= hop - 1), here.has_below & (z_at + hop - 1 < tall)
        made = []
        for number in numbers:
            rising = copies.make(slab(group, number, hop - 1), slab(group, number, hop), here.above)
            falling = copies.make(
                slab(group, number, (tall - hop + 1) % tall), slab(group, number, tall - hop), here.below
            )
            pl.when(rises)(rising.start)
            pl.when(falls)(falling.start)
            waits.append(lambda rising=rising: pl.when(rises)(rising.wait_send))
            waits.append(lambda falling=falling: pl.when(falls)(falling.wait_send))
            made.append((rising, falling))
        along[group, hop] = made

    def hop_take(group, hop, sideways_too=True, numbers=(0,)):
        came_up, came_down = z_at >= hop, z_at + hop < tall
        for rising, falling in along[group, hop]:
            pl.when(came_up)(rising.wait_recv)
            pl.when(came_down)(falling.wait_recv)
        if hop + 1 < tall:
            hop_start(group, hop + 1, numbers)
        if sideways_too:
            spread(group, hop, came_up)
            spread(group, tall - hop, came_down)

    def rows_of(rows, start):
        return rows.at[pl.ds(pl.multiple_of(start, 128), half_rows)]

    def give_rows(held):
        copy = copies.make(
            rows_of(held, core * half_rows), rows_of(held, chip_rows + core * half_rows), here.beside
        )
        copy.start()
        waits.append(copy.wait_send)
        return copy

    def share_rows(held, start):
        rows = rows_of(held, start + core * half_rows)
        copy = copies.make(rows, rows, here.other_core)
        copy.start()
        waits.append(copy.wait_send)
        return copy

    def reordered(source, target):
        count = outer * tall
        each = width // count

        def body(one, into):
            for slot in range(count):
                place = here.block_of(slot)
                held = one[:, pl.ds(pl.multiple_of(place * each, each), each)] if each % 128 == 0 else None
                into[:, slot * each : (slot + 1) * each] = (
                    one[:, slot * each : (slot + 1) * each] if held is None else held
                )

        stream(
            body, chip_rows // 128, [(source, (128, width), step)], [(target, (128, width), step)]
        )

    def mixer(first_tile):
        def body(tok, seg_row, first_out, low, qkv, swish, scores, mixed, gated):
            mixer_forward_kernel(
                tok, r.v_w_first, r.down, r.gain_first, seg_row, r.up, r.bias, r.gain_heads,
                first_out, low, qkv, swish, scores, mixed, gated,
            )

        at = from_tile(first_tile)

        def whole(held):
            return (held, (PIECE, held.shape[1]), at)

        stream(
            body, pieces, [whole(r.tok), (r.seg_row, (1, 1, PIECE), lambda i: (first_tile + i, 0, 0))],
            [whole(held) for held in (r.first, r.low, r.qkv, r.swish, r.scores, r.mixed, r.gated)],
        )

    def branch_product(first_tile):
        def body(gated, into):
            into[...] = mm_nt(gated[...], r.v_w_out[...]).astype(bf16)

        at = from_tile(first_tile)
        stream(body, chip_tiles, [(r.gated, (256, DV), at)], [(r.branch, (256, width), at)])

    def hand(following):
        start = (chip_rows if following else 0) + (1 - core) * half_rows
        target = r.hand_next if following else r.hand_own
        copy = copies.make(rows_of(r.branch, start), target, here.other_core)
        copy.start()
        waits.append(copy.wait_send)
        return copy

    def dense(first_tile):
        def body(second, gate_out, upper, product):
            dense_forward_kernel(second, r.v_w_g, r.v_w_u, gate_out, upper, product)

        at = from_tile(first_tile)
        stream(
            body, chip_tiles, [(r.second, (256, width), at)],
            [(held, (256, units), at) for held in (r.gate, r.upper, r.product)],
        )

    row_block = (128, width)
    own_half = from_tile(core * tiles)
    everywhere = range(outer)

    cross(first)
    reordered(r.tokens, r.tok)
    seg_own = local(r.seg_in, r.seg_row.at[pl.ds(0, pieces)])
    arrive(first)
    hop_start(first, 1)
    spread(first, 0)
    for group in (out, gate, up, down):
        cross(group)
    seg_cross = copies.make(r.seg_in, r.seg_row.at[pl.ds(pieces, pieces)], here.beside)
    seg_cross.start()
    waits.append(seg_cross.wait_send)
    tok_cross = give_rows(r.tok)
    reordered(r.cotangent, r.cot)
    cot_cross = give_rows(r.cot)
    arrive(out)
    spread(out, 0)
    hop_take(first, 1)
    hop_take(first, 2) if tall > 2 else None
    hop_start(out, 1)
    arrive(gate)
    spread(gate, 0)
    for hop in range(3, tall):
        hop_take(first, hop)
    hop_start(gate, 1)
    tok_cross.wait_recv()
    tok_share = share_rows(r.tok, chip_rows)
    for hop in range(1, tall):
        hop_take(out, hop)
    arrive(up)
    arrive(down)
    sides_done(first, range(tall))
    load(first, r.v_w_first)
    spread(down, 0)
    spread(up, 0)
    seg_own.wait()
    seg_cross.wait_recv()
    tok_share.wait_recv()
    loads[first].wait()
    hop_take(gate, 1)
    mixer(pieces)
    hop_take(gate, 2) if tall > 2 else None
    sides_done(out, range(tall))
    load(out, r.v_w_out)
    hop_start(up, 1)
    loads[out].wait()
    branch_product(chip_tiles)
    hand_next = hand(True)
    mixer(0)
    for hop in range(3, tall):
        hop_take(gate, hop)
    hop_take(up, 1)
    branch_product(0)
    hand_own = hand(False)
    hand_next.wait_recv()

    def ahead_body(one, other, into):
        into[...] = (one[...].astype(f32) + other[...].astype(f32)).astype(bf16)

    stream(
        ahead_body, tiles,
        [(r.branch, row_block, from_tile(2 * tiles + core * tiles)), (r.hand_next, row_block, step)],
        [(r.ahead, row_block, step)],
    )
    ahead = copies.make(r.ahead, r.behind, here.beside)
    ahead.start()
    waits.append(ahead.wait_send)
    cot_cross.wait_recv()
    cot_share = share_rows(r.cot, chip_rows)
    for hop in range(2, tall):
        hop_take(up, hop)
    sides_done(down, (0,))
    hop_start(down, 1, everywhere)
    hand_own.wait_recv()
    ahead.wait_recv()

    def hidden_body(one, two, three, tok, hidden_out, second_out):
        hidden = tok[...].astype(f32) + (
            one[...].astype(f32) + two[...].astype(f32) + three[...].astype(f32)
        )
        hidden_out[...] = hidden
        root = lax.rsqrt(jnp.mean(hidden * hidden, axis=-1, keepdims=True) + norm_eps)
        second_out[...] = (hidden * root * r.gain_second[...]).astype(bf16)

    stream(
        hidden_body, tiles,
        [
            (r.branch, row_block, own_half), (r.hand_own, row_block, step), (r.behind, row_block, step),
            (r.tok, row_block, own_half),
        ],
        [(r.hidden, row_block, step), (r.second, row_block, own_half)],
    )
    second_share = share_rows(r.second, 0)
    second_cross = give_rows(r.second)
    sides_done(gate, range(tall))
    load(gate, r.v_w_g)
    second_cross.wait_recv()
    second_next = share_rows(r.second, chip_rows)
    hop_take(down, 1, False, everywhere)
    sides_done(up, range(tall))
    load(up, r.v_w_u)
    second_share.wait_recv()
    loads[gate].wait()
    loads[up].wait()
    dense(0)
    if tall > 2:
        hop_take(down, 2, False, everywhere)
    second_next.wait_recv()
    dense(chip_tiles)
    cot_share.wait_recv()
    yield
    for hop in range(3, tall):
        hop_take(down, hop, False, everywhere)
    load(down, r.v_w_d)
    loads[down].wait()
    yield
    for wait in waits:
        wait()


def layer_kernel(sizes, names, *refs):
    r = SimpleNamespace(**dict(zip(names, refs)))
    here = Place(sizes)
    here.greet()
    copies = Copies(r.send_sem, r.recv_sem)
    fore, back = forward_part(sizes, r, here, copies), backward_part(sizes, r, here, copies)
    next(fore)
    next(back)
    next(fore)
    next(back)
    for part in (fore, back):
        for _ in part:
            pass


def layer(sizes, small, large):
    tall, deep, far, _ = sizes
    chip_rows, width = large["tokens"].shape
    rows, half_rows = 2 * chip_rows, chip_rows // 2
    pieces = rows // PIECE
    units = large["s_gate"].shape[1] // 2
    rank = small["down"].shape[1]
    qkvs = 2 * DK + 2 * DV
    outer = deep * far
    count = outer * tall
    size = width // count
    slab = size * tall
    outs = dict(
        w_first=(width, qkvs), w_out=(width, DV), w_g=(width, units), w_u=(width, units), w_d=(width, units),
        tok=(rows, width), cot=(rows, width), first=(rows, width), low=(rows, rank, f32), qkv=(rows, 2 * DK + DV),
        swish=(rows, DV, f32), scores=(rows, PIECE), mixed=(rows, DV, f32), gated=(rows, DV),
        hidden=(half_rows, width, f32), second=(rows, width), gate=(rows, units, f32), upper=(rows, units, f32),
        product=(rows, units), branch=(rows, width), hand_next=(half_rows, width), hand_own=(half_rows, width),
        ahead=(half_rows, width), behind=(half_rows, width), d_gate=(rows, units), d_up=(rows, units),
        d_qkvs=(rows, qkvs), d_branch=(rows, width), d_hidden=(half_rows, width, f32), d_second=(rows, width),
        dense=(rows, width), d_first=(rows, width), grad_tokens=(chip_rows, width, f32), output=(chip_rows, width),
    )
    for name in ("d_second", "dense", "d_first"):
        for kind in ("hand_" + name + "_next", "hand_" + name + "_own", "ahead_" + name, "behind_" + name):
            outs[kind] = (half_rows, width)
    for group, columns in dict(d=units, g=units, u=units, f=qkvs, o=DV).items():
        numbers = outer if group == "u" else 1
        outs["kept_" + group] = (size // 2, columns, f32)
        outs["received_" + group] = outs["cross_" + group] = (size // 2, columns)
        outs["sum_" + group] = (numbers * slab, columns)
        outs["y_send_" + group] = (outer * size if group == "u" else (outer - 1) * slab, columns)
        outs["y_recv_" + group] = ((outer - 1) * (size if group == "u" else slab), columns)
        outs["z_send_" + group] = outs["z_recv_" + group] = (numbers * 2 * (tall - 1) * size, columns)
    shapes = {
        name: jax.ShapeDtypeStruct(one[:2], one[2] if len(one) > 2 else bf16) for name, one in outs.items()
    }
    shapes.update(seg_row=jax.ShapeDtypeStruct((pieces, 1, PIECE), jnp.int32))
    heads = large["s_query"].shape[1] * 2 // DK
    inner = dict(
        by_block=jax.ShapeDtypeStruct((count, 8 + rank, size), f32),
        by_head=jax.ShapeDtypeStruct((heads, 8 + rank, DK), f32),
    )
    steps = 2 + int(np.log2(count))
    vmem = pltpu.VMEM
    scratch = dict(
        d_up_acc=vmem((rank, DK), f32), d_bias_acc=vmem((1, DK), f32), d_gain_acc=vmem((1, DV), f32),
        dense_gain_acc=vmem((1, width), f32), mixer_gain_acc=vmem((1, width), f32),
        d_down_acc=vmem((rank, width), f32), got_block=vmem((steps, count, 8 + rank, size), f32),
        got_head=vmem((steps, heads, 8 + rank, DK), f32),
        v_w_first=vmem((width, qkvs), bf16), v_w_out=vmem((width, DV), bf16), v_w_g=vmem((width, units), bf16),
        v_w_u=vmem((width, units), bf16), v_w_d=vmem((width, units), bf16),
    )
    transfers = 8 + 5 * (outer - 1) * tall + (4 + outer) * 2 * (tall - 1) + 12
    transfers += 5 * (outer - 1 + 1) + (4 + outer) * 2 * (tall - 1) + 16 + 2 * steps
    scratch.update(
        load_sem=pltpu.SemaphoreType.DMA((15,)), send_sem=pltpu.SemaphoreType.DMA((transfers,)),
        recv_sem=pltpu.SemaphoreType.DMA((transfers,)),
    )
    anywhere, inside = pl.BlockSpec(memory_space=pl.ANY), pl.BlockSpec(memory_space=vmem)
    names = (*small, *large, *shapes, *inner, *scratch)
    results = pl.pallas_call(
        partial(layer_kernel, sizes, names),
        in_specs=[inside] * len(small) + [anywhere] * len(large),
        out_specs=[anywhere] * len(shapes) + [inside] * len(inner),
        out_shape=[*shapes.values(), *inner.values()],
        scratch_shapes=list(scratch.values()),
        compiler_params=pltpu.CompilerParams(
            collective_id=0, has_side_effects=True, vmem_limit_bytes=vmem_limit
        ),
        cost_estimate=pl.CostEstimate(flops=1, bytes_accessed=1, transcendentals=0),
        name="layer",
    )(*small.values(), *large.values())
    return SimpleNamespace(**dict(zip((*shapes, *inner), results)))


def on_device(
    tokens, segment_ids, cotangent, mixer_gain, w_query, w_key, w_value, w_swish, decay_down, decay_up,
    decay_bias, head_gain, w_output, dense_gain, w_gate, w_up, w_down,
):
    sizes = layout(lax.axis_size("dp"))
    tall, deep, far, _ = sizes
    core = lax.axis_index("tensor")
    place = lax.axis_index("dp")
    z_at, y_at, far_at, near = split_place(place, sizes)
    own_rows = tokens.shape[0]
    half_rows = own_rows // 2
    width = tokens.shape[1]
    block = width // lax.axis_size("dp")

    count = tall * deep * far
    slot = np.arange(count, dtype=np.int32)
    slot_z, slot_y, slot_far = slot % tall, (slot // tall) % deep, slot // (tall * deep)
    from_z, from_y, from_far = slot // (deep * far), (slot // far) % deep, slot % far

    def counted(at, backwards, size):
        return lax.rem(at + (size - backwards), np.int32(size))

    places = (counted(z_at, slot_z, tall) * deep + counted(y_at, slot_y, deep)) * far + counted(far_at, slot_far, far)
    back = (counted(far_at, from_far, far) * deep + counted(y_at, from_y, deep)) * tall + counted(z_at, from_z, tall)

    def blocks_of(values, order):
        chosen = (order[:, None] == slot[None, :]).astype(f32)
        flat = values.astype(f32).reshape(count, -1)
        return jnp.dot(chosen, flat, precision=HIGH).reshape(values.shape)

    def columns(parts, begin, end):
        own, received = (part[:, begin:end].astype(f32) for part in parts)
        return jnp.where(
            near == 0, jnp.concatenate([own, received], 1), jnp.concatenate([received, own], 1)
        )

    gain_first = blocks_of(mixer_gain.astype(f32), places)[None]
    gain_second = blocks_of(dense_gain.astype(f32), places)[None]
    down = blocks_of(decay_down, places).astype(bf16)
    head = 2 * core + near
    up_own = lax.dynamic_slice_in_dim(decay_up, head * DK, DK, 1).astype(f32)
    bias_own = lax.dynamic_slice_in_dim(decay_bias, head * DK, DK, 0).astype(f32)[None]
    gain_heads = head_gain.astype(f32)[None]

    aligned = (width // count) % 128 == 0
    small = dict(
        up=up_own, bias=bias_own, gain_heads=gain_heads, gain_first=gain_first, gain_second=gain_second, down=down
    )
    made = layer(sizes, small, dict(
        tokens=tokens if aligned else reorder(tokens, places),
        cotangent=cotangent if aligned else reorder(cotangent, places),
        seg_in=segment_ids.reshape(own_rows // PIECE, 1, PIECE), s_query=w_query, s_key=w_key, s_value=w_value,
        s_swish=w_swish, s_output=w_output.T, s_gate=w_gate, s_up=w_up, s_down=w_down.T,
    ))
    output = reorder(made.output, back)
    grad_tokens = reorder(made.grad_tokens, back)
    rank = decay_down.shape[1]
    grad_down = made.by_block[:, 8:].transpose(0, 2, 1).reshape(width, rank)
    small = (
        made.by_block[:, 0].reshape(width), made.by_block[:, 1].reshape(width), made.by_head[0, 1:3].reshape(DV),
        grad_down, made.by_head[:, 8:].transpose(1, 0, 2).reshape(rank, -1), made.by_head[:, 0].reshape(-1),
    )
    out_first, out_o, out_g, out_u, out_d = (
        (made.kept_f, made.received_f), (made.kept_o, made.received_o), (made.kept_g, made.received_g),
        (made.kept_u, made.received_u), (made.kept_d, made.received_d),
    )

    def all_of(parts):
        return columns(parts, 0, parts[0].shape[1])

    return (
        output,
        grad_tokens,
        small[0],
        columns(out_first, 0, DK),
        columns(out_first, DK, 2 * DK),
        columns(out_first, 2 * DK, 2 * DK + DV),
        columns(out_first, 2 * DK + DV, 2 * DK + 2 * DV),
        small[3],
        small[4],
        small[5],
        small[2],
        all_of(out_o).T,
        small[1],
        all_of(out_g),
        all_of(out_u),
        all_of(out_d).T,
    )


def solution(mesh):
    rows, large, turned, whole = P("dp", None), P("dp", "tensor"), P("tensor", "dp"), P()
    in_specs = (
        rows, P("dp"), rows, whole, large, large, large, large, whole, whole, whole, whole, turned,
        whole, large, large, turned,
    )
    out_specs = (
        rows, rows, whole, large, large, large, large, whole, whole, whole, whole, turned, whole,
        large, large, turned,
    )
    return jax.shard_map(on_device, mesh=mesh, in_specs=in_specs, out_specs=out_specs, check_vma=False)
```

time: 1370 us -> 731 us (0.53)
  waiting for transfers between devices: 709 us -> 0 us
  Pallas kernels: 69.2 us -> 689 us
  matrix products: 233 us -> 0.59 us
  starting transfers between devices: 105 us -> 0 us
  other arithmetic: 95.7 us -> 11.2 us
  local copies, waits for them, and re-layouts: 71.7 us -> 15.6 us
  blocking collectives: 45.3 us -> 0 us
  between operations: 27 us -> 1.3 us
    ppermute x90 -> x0, waiting for transfers between devices: 709 us -> none  [the longest x74 709 us: shift(): return lax.ppermute(values, 'dp', shift_pairs(sizes, axis, step))]
    pallas_call x2 -> x1, Pallas kernels: 37.3 us -> 677 us  [layer(): pl.pallas_call(partial(layer_kernel, sizes, names), in_specs=[inside] * l...]
    dot_general x33 -> x3, matrix products: 233 us -> 0.59 us  [blocks_of(): return jnp.dot(chosen, flat, precision=HIGH).reshape(values.shape)]
    ppermute x90 -> x0, starting transfers between devices: 105 us -> none  [the longest x74 104 us: shift(): return lax.ppermute(values, 'dp', shift_pairs(sizes, axis, step))]
    psum x1 -> x0, blocking collectives: 45.3 us -> none  [on_device(): small = lax.psum(small, ('dp', 'tensor'))]
    select_n x8 -> x0, other arithmetic: 32.2 us -> none  [in_order(): jnp.where(index == 0, jnp.concatenate([own, other], 0), jnp.concatenate([...]
    unnamed x288 -> x37, local copies, waits for them, and re-layouts: 40.6 us -> 8.44 us
    convert_element_type x13 -> x6, other arithmetic: 20.7 us -> 0.23 us  [columns(): own, received = (part[:, begin:end].astype(f32) for part in parts)]
  transfers between devices with their start and end apart: 91 -> 0, of which waited for: 43 -> 0; matrix products, arithmetic and copies ran while one was open for 27% -> 0% of each run, Pallas kernels for 3% -> 0%
where the time goes in v3:
time: 731 us; the launch traced here: 717 us
  Pallas kernels  689 us (94%)
  local copies, waits for them, and re-layouts  15.6 us (2%)
  other arithmetic  11.2 us (2%)
    pallas_call x1, Pallas kernels, layer(): pl.pallas_call(partial(layer_kernel, sizes, names), in_specs=[inside] * l...  677 us

profile of v3, /device:TPU:10, one launch (start us, length us, event | category | flops | bytes accessed | tf_op | source)
XLA Modules:
  0.0 717.3 jit_solution(6066993302502972777)
XLA Ops:
  0.7 1.3 fusion.7
  2.0 1.3 dynamic-slice_convert_fusion.1
  3.3 1.3 broadcast_in_dim.18
  4.5 1.3 reshape.56.refs_8_
  5.8 0.7 reshape.53
  7.3 0.7 reshape.54
  8.8 1.3 dynamic-slice_convert_fusion.refs_0_
  10.1 1.8 copy.45
  11.9 1.1 copy.44
  13.0 0.8 reshape.55
  14.0 1.2 convert_element_type.42.refs_5_
  15.2 1.1 copy.46
  16.3 676.9 %layer.1 = (bf16[2048,1536]{1,0:T(8,128)(2,1)}, bf16[2048,512]{1,0:T(8,128)(2,1)}, bf16[2048,1408]{1,0:T(8,128)(2,1)}, bf16[2048,1408]{1,0:T(8,128)(2,1)}, bf16[...) custom-call(f32[16,256]{1,0:T(8,128)} %dynamic-slice_convert_fusion., ...), custom_call_target="tpu_custom_call" | custom-call | flops 1 | bytes 1 | tf_op jit(solution)/shard_map/layer/pallas_call | solution.py:1177
  693.2 5.0 reorder.2
  698.2 6.8 reorder.3
  707.4 0.7 copy.51
  708.2 1.0 copy.49
  709.3 0.7 maximum_select_fusion.7
  710.0 0.7 maximum_select_fusion.6
  710.8 0.8 maximum_select_fusion.4
  711.6 0.8 maximum_select_fusion.3
  712.5 1.3 maximum_select_fusion
  713.9 1.3 maximum_select_fusion.1
  715.3 1.5 copy.50
  (48 shorter events, 4.8 us)
Async XLA Ops:
  0.6 14.5 %copy-start.1 = (bf16[2816,128]{1,0:T(8,128)(2,1)S(1)}, bf16[2816,128]{1,0:T(8,128)(2,1)}, u32[]{:S(2)}) copy-start(bf16[2816,128]{1,0:T(8,128)(2,1)} %param.40) | copy-start | bytes 2162692
  698.2 6.8 copy-start.12
  698.2 8.6 %copy-start.11 = (f32[8,24,256]{2,1,0:T(8,128)S(1)}, f32[8,24,256]{2,1,0:T(8,128)}, u32[]{:S(2)}) copy-start(f32[8,24,256]{2,1,0:T(8,128)} %get-tuple-element.32) | copy-start | bytes 589828
  698.2 9.9 %copy-start.10 = (bf16[128,512]{1,0:T(8,128)(2,1)S(1)}, bf16[128,512]{1,0:T(8,128)(2,1)}, u32[]{:S(2)}) copy-start(bf16[128,512]{1,0:T(8,128)(2,1)} %get-tuple-element.37) | copy-start | bytes 393220
  698.2 9.9 %copy-start.9 = (f32[128,512]{1,0:T(8,128)S(1)}, f32[128,512]{1,0:T(8,128)}, u32[]{:S(2)}) copy-start(f32[128,512]{1,0:T(8,128)} %get-tuple-element.36) | copy-start | bytes 786436
  704.9 4.2 copy-start
  704.9 4.3 copy-start.5
  709.2 3.3 copy-start.8
  709.2 3.3 copy-start.4
  710.8 3.0 copy-start.7
  711.6 2.2 copy-start.3
  712.5 2.6 copy-start.6
  713.8 1.4 copy-start.2

commit v4 on v3

--- a/solution.py
+++ b/solution.py
@@ -231,9 +231,8 @@
         + mm_nt(d_keyset, w_first[:, DK : 2 * DK])
         + mm_nt(d_values, w_first[:, 2 * DK : 2 * DK + DV])
         + mm_nt(d_swish, w_first[:, 2 * DK + DV :])
-        + lax.dot_general(
-            d_low, down[...].astype(f32), (((1,), (1,)), ((), ())), precision=HIGH, preferred_element_type=f32
-        )
+        + mm_nt(high, down[...])
+        + mm_nt(rest, down[...])
     ).astype(bf16)
     d_up[...] += lax.dot_general(
         low[...], d_pre, (((0,), (0,)), ((), ())), precision=HIGH, preferred_element_type=f32
@@ -691,9 +690,9 @@
     yield
     dense_back(chip_tiles)
     hand("d_second", True)
+    ahead("d_second")
     dense_back(0)
     hand("d_second", False)
-    ahead("d_second")
     send_slabs("g")
     all_slabs("u")
 

time: 731 us -> 730 us (level)
  no operation moved by 1% of the time
where the time goes in v4:
time: 730 us; the launch traced here: 718 us
  Pallas kernels  689 us (94%)
  local copies, waits for them, and re-layouts  15.6 us (2%)
  other arithmetic  11.2 us (2%)
    pallas_call x1, Pallas kernels, layer(): pl.pallas_call(partial(layer_kernel, sizes, names), in_specs=[inside] * l...  678 us

profile of v4, /device:TPU:10, one launch (start us, length us, event | category | flops | bytes accessed | tf_op | source)
XLA Modules:
  0.0 718.0 jit_solution(17868187450560042026)
XLA Ops:
  0.7 1.3 fusion.7
  2.0 1.3 dynamic-slice_convert_fusion.1
  3.3 1.3 broadcast_in_dim.18
  4.5 1.3 reshape.56.refs_8_
  5.8 0.7 reshape.53
  7.3 0.7 reshape.54
  8.8 1.3 dynamic-slice_convert_fusion.refs_0_
  10.1 1.8 copy.45
  11.9 1.1 copy.44
  13.0 0.8 reshape.55
  14.0 1.2 convert_element_type.42.refs_5_
  15.2 1.1 copy.46
  16.3 677.6 %layer.1 = (bf16[2048,1536]{1,0:T(8,128)(2,1)}, bf16[2048,512]{1,0:T(8,128)(2,1)}, bf16[2048,1408]{1,0:T(8,128)(2,1)}, bf16[2048,1408]{1,0:T(8,128)(2,1)}, bf16[...) custom-call(f32[16,256]{1,0:T(8,128)} %dynamic-slice_convert_fusion., ...), custom_call_target="tpu_custom_call" | custom-call | flops 1 | bytes 1 | tf_op jit(solution)/shard_map/layer/pallas_call | solution.py:1176
  693.9 5.0 reorder.2
  698.9 6.8 reorder.3
  708.1 0.7 copy.51
  708.8 1.0 copy.49
  710.0 0.7 maximum_select_fusion.7
  710.7 0.7 maximum_select_fusion.6
  711.5 0.8 maximum_select_fusion.4
  712.3 0.8 maximum_select_fusion.3
  713.2 1.3 maximum_select_fusion
  714.6 1.3 maximum_select_fusion.1
  716.0 1.5 copy.50
  (48 shorter events, 4.8 us)
Async XLA Ops:
  0.6 14.5 %copy-start.1 = (bf16[2816,128]{1,0:T(8,128)(2,1)S(1)}, bf16[2816,128]{1,0:T(8,128)(2,1)}, u32[]{:S(2)}) copy-start(bf16[2816,128]{1,0:T(8,128)(2,1)} %param.40) | copy-start | bytes 2162692
  698.9 6.8 copy-start.12
  698.9 8.6 %copy-start.11 = (f32[8,24,256]{2,1,0:T(8,128)S(1)}, f32[8,24,256]{2,1,0:T(8,128)}, u32[]{:S(2)}) copy-start(f32[8,24,256]{2,1,0:T(8,128)} %get-tuple-element.32) | copy-start | bytes 589828
  698.9 9.9 %copy-start.10 = (bf16[128,512]{1,0:T(8,128)(2,1)S(1)}, bf16[128,512]{1,0:T(8,128)(2,1)}, u32[]{:S(2)}) copy-start(bf16[128,512]{1,0:T(8,128)(2,1)} %get-tuple-element.37) | copy-start | bytes 393220
  698.9 9.9 %copy-start.9 = (f32[128,512]{1,0:T(8,128)S(1)}, f32[128,512]{1,0:T(8,128)}, u32[]{:S(2)}) copy-start(f32[128,512]{1,0:T(8,128)} %get-tuple-element.36) | copy-start | bytes 786436
  705.6 4.2 copy-start
  705.6 4.3 copy-start.5
  709.8 3.3 copy-start.8
  709.9 3.3 copy-start.4
  711.5 3.0 copy-start.7
  712.3 2.2 copy-start.3
  713.2 2.6 copy-start.6
  714.5 1.4 copy-start.2
